TPU v7x, 32 devices: a whole 2x2x4 slice. The times are simulated.
32 devices in a mesh: shard: 4 (over y, core), ctx: 2 (over x), tp: 4 (over z).
Axes of the slice: x: 2, y: 2, z: 4, core: 2. Of those that a mesh axis runs over, the one named last changes fastest.
Arguments:
- tokens: bfloat16 [16, 788, 768], P(('shard', 'tp'), 'ctx'), may hold values from -6 to 6
- cotangent: bfloat16 [16, 788, 768], P(('shard', 'tp'), 'ctx'), may hold values from -6 to 6
- routing: int32 [16, 788, 2], P(('shard', 'tp'), 'ctx'), may hold values from 0 to 7, all different within a row; in each aligned block of 394 rows (0 to 393, 394 to 787, ..., all dimensions but the last counted through in order) at most 197 rows name the same one
- gating: float32 [16, 788, 2], P(('shard', 'tp'), 'ctx'), may hold values from 0.2 to 0.8
- inward: bfloat16 [3, 768, 768], P(None, ('shard', 'ctx', 'tp')), may hold values from -0.21875 to 0.21875
- outward: bfloat16 [768, 768], P(('shard', 'ctx', 'tp')), may hold values from -1.25 to 1.25
- scales: bfloat16 [2, 768], P(None, ('shard', 'ctx', 'tp')), may hold values from 0.5 to 1.5
- shifts: bfloat16 [2, 768], P(None, ('shard', 'ctx', 'tp')), may hold values from -1.5 to 1.5
- upward: bfloat16 [8, 768, 3072], P(None, ('shard', 'ctx'), 'tp'), may hold values from -0.21875 to 0.21875
- downward: bfloat16 [8, 768, 3072], P(None, ('shard', 'ctx'), 'tp'), may hold values from -0.21875 to 0.21875
- inward_moment: float32 [3, 768, 768], P(None, ('shard', 'ctx', 'tp')), may hold values from -12 to 12
- outward_moment: float32 [768, 768], P(('shard', 'ctx', 'tp')), may hold values from -12 to 12
- scales_moment: float32 [2, 768], P(None, ('shard', 'ctx', 'tp')), may hold values from -12 to 12
- shifts_moment: float32 [2, 768], P(None, ('shard', 'ctx', 'tp')), may hold values from -12 to 12
- upward_moment: float32 [8, 768, 3072], P(None, ('shard', 'ctx'), 'tp'), may hold values from -24 to 24
- downward_moment: float32 [8, 768, 3072], P(None, ('shard', 'ctx'), 'tp'), may hold values from -24 to 24
Outputs:
- result: bfloat16 [16, 788, 768], P(('shard', 'tp'), 'ctx')
- input_grad: float32 [16, 788, 768], P(('shard', 'tp'), 'ctx')
- inward_grad: float32 [3, 768, 768], P(None, ('shard', 'ctx', 'tp'))
- outward_grad: float32 [768, 768], P(('shard', 'ctx', 'tp'))
- scales_grad: float32 [2, 768], P(None, ('shard', 'ctx', 'tp'))
- shifts_grad: float32 [2, 768], P(None, ('shard', 'ctx', 'tp'))
- upward_grad: float32 [8, 768, 3072], P(None, ('shard', 'ctx'), 'tp')
- downward_grad: float32 [8, 768, 3072], P(None, ('shard', 'ctx'), 'tp')
- inward_state: float32 [3, 768, 768], P(None, ('shard', 'ctx', 'tp'))
- outward_state: float32 [768, 768], P(('shard', 'ctx', 'tp'))
- scales_state: float32 [2, 768], P(None, ('shard', 'ctx', 'tp'))
- shifts_state: float32 [2, 768], P(None, ('shard', 'ctx', 'tp'))
- upward_state: float32 [8, 768, 3072], P(None, ('shard', 'ctx'), 'tp')
- downward_state: float32 [8, 768, 3072], P(None, ('shard', 'ctx'), 'tp')
- inward_new: float32 [3, 768, 768], P(None, ('shard', 'ctx', 'tp'))
- outward_new: float32 [768, 768], P(('shard', 'ctx', 'tp'))
- scales_new: float32 [2, 768], P(None, ('shard', 'ctx', 'tp'))
- shifts_new: float32 [2, 768], P(None, ('shard', 'ctx', 'tp'))
- upward_new: float32 [8, 768, 3072], P(None, ('shard', 'ctx'), 'tp')
- downward_new: float32 [8, 768, 3072], P(None, ('shard', 'ctx'), 'tp')
Inputs may be any that keep to these rules, and one draw needn't show every extreme that they name: `routing`: in each aligned block of 394 rows (the rows of one device) no expert is named by more than 197 of them; the 2 experts of a row differ.
All inputs are finite; a program needn't handle non-finite values.
Results may differ from a plain program's by a relative error of at most 0.022.
Values may be sent and summed in bfloat16 or wider, within the bound.
A program may use at most 320 MiB of HBM per device.

v0:
```python
import math

import jax
import jax.numpy as jnp
import numpy as np
from jax import lax
from jax.sharding import PartitionSpec as P

HEAD_DIM = 64
LEN = 197


first_coef = 3.4445
second_coef = -4.775
third_coef = 2.0315
momentum_decay = 0.9
norm_epsilon = 1e-06
orth_epsilon = 1e-07
highest = lax.Precision.HIGHEST


def normalize(values, factor, offset):
    average = jnp.mean(values, axis=-1, keepdims=True)
    centred = values - average
    inverse = lax.rsqrt(jnp.mean(centred * centred, axis=-1, keepdims=True) + norm_epsilon)
    unit_rows = centred * inverse
    return (unit_rows * factor + offset, unit_rows, inverse)


def normalize_back(gradient, unit_rows, inverse, factor):
    inner = gradient * factor
    average = jnp.mean(inner, axis=-1, keepdims=True)
    along = jnp.mean(inner * unit_rows, axis=-1, keepdims=True)
    back = inverse * (inner - average - unit_rows * along)
    return (back, jnp.sum(gradient * unit_rows, axis=0), jnp.sum(gradient, axis=0))


def slot_sources(routes, experts, capacity):
    pairs = routes.shape[0] * routes.shape[1]
    chosen = routes.reshape(pairs)
    onehot = (chosen[:, None] == jnp.arange(experts, dtype=jnp.int32)[None, :]).astype(jnp.int32)
    earlier = jnp.cumsum(onehot, axis=0) - onehot
    placed = jnp.sum(earlier * onehot, axis=1) + chosen * capacity
    matches = placed[None, :] == jnp.arange(experts * capacity, dtype=jnp.int32)[:, None]
    source = jnp.sum(jnp.where(matches, jnp.arange(pairs, dtype=jnp.int32)[None, :], 0), axis=1)
    filled = jnp.any(matches, axis=1)
    return (placed, source, filled)


def orthogonal(matrix):
    summed = jnp.sqrt(jnp.sum(matrix * matrix))
    current = matrix / (summed + orth_epsilon)
    for repeat in range(5):
        square = lax.dot_general(
            current,
            current,
            (((1,), (1,)), ((), ())),
            precision=highest,
            preferred_element_type=jnp.float32,
        )
        power = jnp.dot(square, square, precision=highest, preferred_element_type=jnp.float32)
        mixer = second_coef * square + third_coef * power
        current = first_coef * current + jnp.dot(
            mixer, current, precision=highest, preferred_element_type=jnp.float32
        )
    return current


def advance(gradient, moment):
    current = momentum_decay * moment + (1.0 - momentum_decay) * gradient
    return (current, (1.0 - momentum_decay) * gradient + momentum_decay * current)


def expert_weights(upward, downward):
    return (
        lax.all_gather(upward, ("shard", "ctx"), axis=1, tiled=True),
        lax.all_gather(downward, ("shard", "ctx"), axis=1, tiled=True),
    )


def on_device(
    tokens,
    cotangent,
    routing,
    gating,
    inward,
    outward,
    scales,
    shifts,
    upward,
    downward,
    inward_moment,
    outward_moment,
    scales_moment,
    shifts_moment,
    upward_moment,
    downward_moment,
):
    rows_here = tokens.shape[1]
    features = tokens.shape[2]
    experts = upward.shape[0]
    top_count = routing.shape[2]
    capacity = 2 * top_count * rows_here // experts
    attn_scale = HEAD_DIM ** (-0.5)
    inputs = tokens[0].astype(jnp.float32)
    routes = routing[0]
    gate_pairs = gating[0].reshape(-1)
    zero_low = jnp.zeros((), jnp.bfloat16)
    full_in, full_out, all_scales, all_shifts = (
        lax.all_gather(inward, ("shard", "ctx", "tp"), axis=1, tiled=True),
        lax.all_gather(outward, ("shard", "ctx", "tp"), axis=0, tiled=True),
        lax.all_gather(scales, ("shard", "ctx", "tp"), axis=1, tiled=True),
        lax.all_gather(shifts, ("shard", "ctx", "tp"), axis=1, tiled=True),
    )
    factor = all_scales.astype(jnp.float32)
    offset = all_shifts.astype(jnp.float32)
    normed, unit_one, inverse_one = normalize(inputs, factor[0], offset[0])
    normed_low = normed.astype(jnp.bfloat16)
    projected = jnp.einsum(
        "td,kde->kte", normed_low, full_in, preferred_element_type=jnp.float32
    ).astype(jnp.bfloat16)
    head_rows = lax.all_to_all(projected, "ctx", split_axis=2, concat_axis=1, tiled=True)
    group_rows = head_rows.shape[1]
    head_width = head_rows.shape[2]
    seqs_here = group_rows // LEN
    shaped = head_rows.reshape(3, seqs_here, LEN, head_width // HEAD_DIM, HEAD_DIM)
    query_rows, key_rows, value_rows = (shaped[0], shaped[1], shaped[2])
    scores = (
        jnp.einsum("sqhd,skhd->shqk", query_rows, key_rows, preferred_element_type=jnp.float32)
        * attn_scale
    )
    top_score = jnp.max(scores, axis=-1, keepdims=True)
    logsum = top_score + jnp.log(jnp.sum(jnp.exp(scores - top_score), axis=-1, keepdims=True))
    soft_low = jnp.exp(scores - logsum).astype(jnp.bfloat16)
    blended = jnp.einsum(
        "shqk,skhd->sqhd", soft_low, value_rows, preferred_element_type=jnp.float32
    ).astype(jnp.bfloat16)
    blended_tokens = lax.all_to_all(
        blended.reshape(group_rows, head_width), "ctx", split_axis=0, concat_axis=1, tiled=True
    )
    residual = inputs + jnp.dot(blended_tokens, full_out, preferred_element_type=jnp.float32)
    second, unit_two, inverse_two = normalize(residual, factor[1], offset[1])
    second_low = second.astype(jnp.bfloat16)
    upstream = cotangent[0].astype(jnp.float32)
    placed, source, filled = slot_sources(routes, experts, capacity)
    slot_rows = jnp.where(filled[:, None], second_low[source // top_count], zero_low)
    slot_rows = slot_rows.reshape(experts, capacity, features)
    group_slots = lax.all_gather(slot_rows, "tp", axis=1, tiled=True)
    upper_full, lower_full = expert_weights(upward, downward)
    before = jnp.einsum("ecd,edf->ecf", group_slots, upper_full, preferred_element_type=jnp.float32)
    hidden = jax.nn.gelu(before).astype(jnp.bfloat16)
    partial_out = jnp.einsum("ecf,edf->ecd", hidden, lower_full, preferred_element_type=jnp.float32)
    own_out = lax.psum_scatter(
        partial_out.astype(jnp.bfloat16), "tp", scatter_dimension=1, tiled=True
    ).astype(jnp.float32)
    picked = own_out.reshape(experts * capacity, features)[placed].reshape(
        rows_here, top_count, features
    )
    mixture = jnp.sum(picked * gating[0][:, :, None], axis=1)
    result = (residual + mixture).astype(jnp.bfloat16)
    slot_grad = jnp.where(
        filled[:, None], upstream[source // top_count] * gate_pairs[source][:, None], 0.0
    )
    slot_grad = slot_grad.astype(jnp.bfloat16).reshape(experts, capacity, features)
    group_grad = lax.all_gather(slot_grad, "tp", axis=1, tiled=True)
    upper_full, lower_full = expert_weights(upward, downward)
    d_hidden = jnp.einsum(
        "ecd,edf->ecf", group_grad, lower_full, preferred_element_type=jnp.float32
    )
    unused, gelu_back = jax.vjp(jax.nn.gelu, before)
    d_before = gelu_back(d_hidden)[0].astype(jnp.bfloat16)
    lower_part = jnp.einsum("ecd,ecf->edf", group_grad, hidden, preferred_element_type=jnp.float32)
    upper_part = jnp.einsum(
        "ecd,ecf->edf", group_slots, d_before, preferred_element_type=jnp.float32
    )
    slot_input_part = jnp.einsum(
        "ecf,edf->ecd", d_before, upper_full, preferred_element_type=jnp.float32
    )
    slot_input = lax.psum_scatter(
        slot_input_part.astype(jnp.bfloat16), "tp", scatter_dimension=1, tiled=True
    ).astype(jnp.float32)
    d_second = jnp.sum(
        slot_input.reshape(experts * capacity, features)[placed].reshape(
            rows_here, top_count, features
        ),
        axis=1,
    )
    d_norm_two, scale_two, shift_two = normalize_back(d_second, unit_two, inverse_two, factor[1])
    d_residual = upstream + d_norm_two
    d_attended = d_residual.astype(jnp.bfloat16)
    outward_part = jnp.einsum(
        "td,te->de", blended_tokens, d_attended, preferred_element_type=jnp.float32
    )
    d_blended = jnp.einsum(
        "te,de->td", d_attended, full_out, preferred_element_type=jnp.float32
    ).astype(jnp.bfloat16)
    d_heads = lax.all_to_all(d_blended, "ctx", split_axis=1, concat_axis=0, tiled=True)
    d_heads = d_heads.reshape(seqs_here, LEN, head_width // HEAD_DIM, HEAD_DIM)
    soft_full = jnp.exp(
        jnp.einsum("sqhd,skhd->shqk", query_rows, key_rows, preferred_element_type=jnp.float32)
        * attn_scale
        - logsum
    )
    d_soft = jnp.einsum("sqhd,skhd->shqk", d_heads, value_rows, preferred_element_type=jnp.float32)
    value_grad = jnp.einsum(
        "shqk,sqhd->skhd", soft_low, d_heads, preferred_element_type=jnp.float32
    ).astype(jnp.bfloat16)
    row_inner = jnp.sum(soft_full * d_soft, axis=-1, keepdims=True)
    d_scores = (soft_full * (d_soft - row_inner)).astype(jnp.bfloat16)
    query_grad = (
        jnp.einsum("shqk,skhd->sqhd", d_scores, key_rows, preferred_element_type=jnp.float32)
        * attn_scale
    ).astype(jnp.bfloat16)
    key_grad = (
        jnp.einsum("shqk,sqhd->skhd", d_scores, query_rows, preferred_element_type=jnp.float32)
        * attn_scale
    ).astype(jnp.bfloat16)
    stacked_grad = jnp.stack([query_grad, key_grad, value_grad]).reshape(3, group_rows, head_width)
    token_grad = lax.all_to_all(stacked_grad, "ctx", split_axis=1, concat_axis=2, tiled=True)
    inward_part = jnp.einsum(
        "td,kte->kde", normed_low, token_grad, preferred_element_type=jnp.float32
    )
    d_normed = jnp.einsum("kte,kde->td", token_grad, full_in, preferred_element_type=jnp.float32)
    d_norm_one, scale_one, shift_one = normalize_back(d_normed, unit_one, inverse_one, factor[0])
    input_grad = d_residual + d_norm_one
    inward_grad, outward_grad, scales_grad, shifts_grad = (
        lax.psum_scatter(inward_part, ("shard", "ctx", "tp"), scatter_dimension=1, tiled=True),
        lax.psum_scatter(outward_part, ("shard", "ctx", "tp"), scatter_dimension=0, tiled=True),
        lax.psum_scatter(
            jnp.stack([scale_one, scale_two]),
            ("shard", "ctx", "tp"),
            scatter_dimension=1,
            tiled=True,
        ),
        lax.psum_scatter(
            jnp.stack([shift_one, shift_two]),
            ("shard", "ctx", "tp"),
            scatter_dimension=1,
            tiled=True,
        ),
    )
    upward_grad, downward_grad = (
        lax.psum_scatter(
            upper_part.astype(jnp.bfloat16), ("shard", "ctx"), scatter_dimension=1, tiled=True
        ).astype(jnp.float32),
        lax.psum_scatter(
            lower_part.astype(jnp.bfloat16), ("shard", "ctx"), scatter_dimension=1, tiled=True
        ).astype(jnp.float32),
    )
    inward_state, inward_push = advance(inward_grad, inward_moment)
    outward_state, outward_push = advance(outward_grad, outward_moment)
    scales_state, scales_push = advance(scales_grad, scales_moment)
    shifts_state, shifts_push = advance(shifts_grad, shifts_moment)
    upward_state, upward_push = advance(upward_grad, upward_moment)
    downward_state, downward_push = advance(downward_grad, downward_moment)
    devices = lax.axis_size(("shard", "ctx", "tp"))
    outer_count = lax.axis_size(("shard", "ctx"))
    inner_count = lax.axis_size("tp")
    rows_local = upward.shape[1]
    cols_local = upward.shape[2]
    slot_size = rows_local * cols_local
    attention_size = inward.shape[1] * features
    full_cols = inner_count * cols_local

    def flat_pad(portion):
        flatten = portion.reshape(portion.shape[0], -1)
        return jnp.pad(flatten, ((0, 0), (0, slot_size - flatten.shape[1])))

    matrices = jnp.concatenate(
        [
            flat_pad(inward_push),
            flat_pad(outward_push[None]),
            upward_push.reshape(experts, slot_size),
            downward_push.reshape(experts, slot_size),
        ]
    )
    matrix_count = matrices.shape[0]
    owner_table = np.arange(matrix_count) * devices // matrix_count
    outgoing = jnp.zeros((devices, slot_size), jnp.float32).at[owner_table].set(matrices)
    received = lax.all_to_all(
        outgoing.astype(jnp.bfloat16),
        ("shard", "ctx", "tp"),
        split_axis=0,
        concat_axis=0,
        tiled=True,
    ).astype(outgoing.dtype)
    myself = lax.axis_index(("shard", "ctx", "tp"))
    owned = (
        jnp.sum(
            jnp.where(
                jnp.asarray(owner_table, dtype=jnp.int32) == myself,
                jnp.arange(matrix_count, dtype=jnp.int32) + 1,
                0,
            )
        )
        - 1
    )
    attention_kind = jnp.logical_and(owned >= 0, owned < 4)
    expert_form = (
        received.reshape(outer_count, inner_count, rows_local, cols_local)
        .transpose(0, 2, 1, 3)
        .reshape(features, full_cols)
    )
    attention_form = jnp.pad(
        received[:, :attention_size].reshape(features, features),
        ((0, 0), (0, full_cols - features)),
    )
    orthogonal_form = orthogonal(jnp.where(attention_kind, attention_form, expert_form))
    back_expert = (
        orthogonal_form.reshape(outer_count, rows_local, inner_count, cols_local)
        .transpose(0, 2, 1, 3)
        .reshape(devices, slot_size)
    )
    back_attention = jnp.pad(
        orthogonal_form[:, :features].reshape(devices, attention_size),
        ((0, 0), (0, slot_size - attention_size)),
    )
    returned = lax.all_to_all(
        jnp.where(attention_kind, back_attention, back_expert).astype(jnp.bfloat16),
        ("shard", "ctx", "tp"),
        split_axis=0,
        concat_axis=0,
        tiled=True,
    ).astype(jnp.float32)
    mine_parts = returned[owner_table]
    inward_new = inward.astype(jnp.float32) - mine_parts[:3, :attention_size].reshape(inward.shape)
    outward_new = outward.astype(jnp.float32) - mine_parts[3, :attention_size].reshape(
        outward.shape
    )
    upward_new = upward.astype(jnp.float32) - 2.0 * mine_parts[4 : 4 + experts].reshape(
        upward.shape
    )
    downward_new = downward.astype(jnp.float32) - mine_parts[4 + experts :].reshape(downward.shape)
    total_tokens = lax.axis_size("shard") * lax.axis_size("ctx") * lax.axis_size("tp") * rows_here
    vector_rate = 0.6 / math.sqrt(total_tokens)
    scales_new = scales.astype(jnp.float32) - vector_rate * scales_push
    shifts_new = shifts.astype(jnp.float32) - vector_rate * shifts_push
    return (
        result[None],
        input_grad[None],
        inward_grad,
        outward_grad,
        scales_grad,
        shifts_grad,
        upward_grad,
        downward_grad,
        inward_state,
        outward_state,
        scales_state,
        shifts_state,
        upward_state,
        downward_state,
        inward_new,
        outward_new,
        scales_new,
        shifts_new,
        upward_new,
        downward_new,
    )


def solution(mesh):
    in_specs = (
        P(("shard", "tp"), "ctx", None),
        P(("shard", "tp"), "ctx", None),
        P(("shard", "tp"), "ctx", None),
        P(("shard", "tp"), "ctx", None),
        P(None, ("shard", "ctx", "tp"), None),
        P(("shard", "ctx", "tp"), None),
        P(None, ("shard", "ctx", "tp")),
        P(None, ("shard", "ctx", "tp")),
        P(None, ("shard", "ctx"), "tp"),
        P(None, ("shard", "ctx"), "tp"),
        P(None, ("shard", "ctx", "tp"), None),
        P(("shard", "ctx", "tp"), None),
        P(None, ("shard", "ctx", "tp")),
        P(None, ("shard", "ctx", "tp")),
        P(None, ("shard", "ctx"), "tp"),
        P(None, ("shard", "ctx"), "tp"),
    )
    out_specs = (
        P(("shard", "tp"), "ctx", None),
        P(("shard", "tp"), "ctx", None),
        P(None, ("shard", "ctx", "tp"), None),
        P(("shard", "ctx", "tp"), None),
        P(None, ("shard", "ctx", "tp")),
        P(None, ("shard", "ctx", "tp")),
        P(None, ("shard", "ctx"), "tp"),
        P(None, ("shard", "ctx"), "tp"),
        P(None, ("shard", "ctx", "tp"), None),
        P(("shard", "ctx", "tp"), None),
        P(None, ("shard", "ctx", "tp")),
        P(None, ("shard", "ctx", "tp")),
        P(None, ("shard", "ctx"), "tp"),
        P(None, ("shard", "ctx"), "tp"),
        P(None, ("shard", "ctx", "tp"), None),
        P(("shard", "ctx", "tp"), None),
        P(None, ("shard", "ctx", "tp")),
        P(None, ("shard", "ctx", "tp")),
        P(None, ("shard", "ctx"), "tp"),
        P(None, ("shard", "ctx"), "tp"),
    )
    return jax.shard_map(
        on_device, mesh=mesh, in_specs=in_specs, out_specs=out_specs, check_vma=False
    )
```

profile of v0, /device:TPU:0, one launch (start us, length us, event | category | flops | bytes accessed | tf_op | source)
XLA Modules:
  0.0 2326.7 jit_solution(17068844136177503592)
XLA Ops:
  9.4 69.5 %all-gather = bf16[32,24,2]{1,2,0:T(2,128)(2,1)S(1)} all-gather(bf16[1,24,2]{1,2,0:T(2,128)(2,1)} %bitcast.232), channel_id=1, replica_groups=mesh['shard'=4,'ctx'=2,'tp'=4] {'shard','ctx','tp'}, dimensions={0}, use_global_device_ids=true | all-gather | bytes 3168 | tf_op jit(solution)/shard_map/all_gather | solution.py:112
  79.2 63.2 %all-gather.1 = bf16[32,24,2]{1,2,0:T(2,128)(2,1)S(1)} all-gather(bf16[1,24,2]{1,2,0:T(2,128)(2,1)} %bitcast.231), channel_id=1, replica_groups=mesh['shard'=4,'ctx'=2,'tp'=4] {'shard','ctx','tp'}, dimensions={0}, use_global_device_ids=true | all-gather | bytes 3168 | tf_op jit(solution)/shard_map/all_gather | solution.py:113
  161.3 53.1 %all-to-all-done = bf16[3,394,768]{1,0,2:T(4,128)(2,1)} async-done(((bf16[3,394,768]{1,0,2:T(4,128)(2,1)}), bf16[3,394,768]{1,0,2:T(4,128)(2,1)}, u32[]{:S(2)}, u32[]{:S(2)}) %all-to-all-start) | async-done | bytes 1815584 | tf_op jit(solution)/shard_map/all_to_all | solution.py:122
  280.2 7.7 fusion.29
  288.5 145.4 %all-gather.13.cloned.1.call-done = bf16[8,788,768]{2,0,1:T(8,128)(2,1)} async-done(((bf16[8,197,768]{2,0,1:T(8,128)(2,1)}), bf16[8,788,768]{2,0,1:T(8,128)(2,1)}) %all-gather.13.cloned.1.call-update) | async-done | bytes 9682960 | tf_op jit(solution)/shard_map/all_gather | solution.py:148
  433.9 19.0 fusion.15
  452.9 151.4 %all-gather.19.cloned.1.call-done = bf16[8,788,768]{2,0,1:T(8,128)(2,1)} async-done(((bf16[8,197,768]{2,0,1:T(8,128)(2,1)}), bf16[8,788,768]{2,0,1:T(8,128)(2,1)}) %all-gather.19.cloned.1.call-update) | async-done | bytes 9682960 | tf_op jit(solution)/shard_map/all_gather | solution.py:165
  604.3 58.8 %all-gather.17.cloned.1.call-done = bf16[8,768,768]{2,1,0:T(8,128)(2,1)} async-done(((bf16[8,96,768]{2,1,0:T(8,128)(2,1)}), bf16[8,768,768]{2,1,0:T(8,128)(2,1)}) %all-gather.17.cloned.1.call-update) | async-done | bytes 9437200 | tf_op jit(solution)/shard_map/all_gather | solution.py:77
  663.1 27.0 %fusion.6 = bf16[8,788,768]{2,1,0:T(8,128)(2,1)} fusion(f32[8,788,768]{2,1,0:T(8,128)} %fusion.15, bf16[8,768,768]{2,1,0:T(8,128)(2,1)} %all-gather.17.cloned.1.call-done, bf16[8,788,768]{2,0,1:T(8,128)(2,1)} %all-gather.19.cloned.1.call-done), kind=kOutput, calls=%fused_computation.15 | convolution fusion | flops 7533330432 | bytes 48168960 | tf_op jit(solution)/shard_map/ecd,edf->ecf/dot_general | solution.py:167
  690.1 15.6 convolution_convert_fusion
  705.8 9.5 copy.339
  715.3 17.3 convolution_convert_fusion.1
  732.6 9.5 copy.331
  742.2 18.0 fusion.20
  760.3 26.9 %fusion.23 = bf16[8,768,768]{2,1,0:T(8,128)(2,1)} fusion(bf16[8,788,768]{2,0,1:T(8,128)(2,1)} %all-gather.19.cloned.1.call-done, f32[8,788,768]{2,1,0:T(8,128)} %fusion.15), kind=kOutput, calls=%fused_computation.44 | convolution fusion | flops 7484792832 | bytes 38486016 | tf_op jit(solution)/shard_map/ecd,ecf->edf/dot_general | solution.py:172
  788.5 92.2 %reduce-scatter.10.cloned.1.call-done = bf16[8,197,768]{2,0,1:T(8,128)(2,1)} async-done(((bf16[8,788,768]{2,0,1:T(8,128)(2,1)}), bf16[8,197,768]{2,0,1:T(8,128)(2,1)}) %reduce-scatter.10.cloned.1.call-update) | async-done | bytes 2420752 | tf_op jit(solution)/shard_map/reduce_scatter | solution.py:179
  900.4 148.8 %reduce-scatter.8.cloned.1.call-done = bf16[8,197,768]{2,0,1:T(8,128)(2,1)} async-done(((bf16[8,788,768]{2,0,1:T(8,128)(2,1)}), bf16[8,197,768]{2,0,1:T(8,128)(2,1)}) %reduce-scatter.8.cloned.1.call-update) | async-done | bytes 2420752 | tf_op jit(solution)/shard_map/reduce_scatter | solution.py:153
  1090.0 14.2 all-to-all-done.2
  1132.8 31.2 %all_to_all.86 = bf16[3,788,384]{2,0,1:T(4,128)(2,1)S(1)} all-to-all(bf16[3,788,384]{2,0,1:T(4,128)(2,1)S(1)} %copy.354), channel_id=1, replica_groups=mesh['shard'=4,'ctx'=2,'tp'=4] {'ctx'}, dimensions={1} | all-to-all | bytes 3631104 | tf_op jit(solution)/shard_map/all_to_all | solution.py:219
  1176.3 11.1 copy.357
  1194.6 21.6 reduce-scatter.16.cloned.1.call-done
  1223.8 97.9 %reduce-scatter.12.cloned.1.call-done = f32[24,768]{1,0:T(8,128)} async-done(((f32[768,768]{1,0:T(8,128)}), f32[24,768]{1,0:T(8,128)}) %reduce-scatter.12.cloned.1.call-update) | async-done | bytes 73744 | tf_op jit(solution)/shard_map/reduce_scatter | solution.py:228
  1323.4 194.8 %all-reduce.11.cloned.1.call-done = f32[3,768,768]{2,0,1:T(4,128)} async-done(((f32[3,768,768]{2,0,1:T(4,128)}), f32[3,768,768]{2,0,1:T(4,128)}) %all-reduce.11.cloned.1.call-update) | async-done | bytes 7077904
  1529.1 49.6 %scatter_fusion = f32[32,73728]{1,0:T(8,128)} fusion(f32[32,73728]{1,0:T(8,128)} %broadcast_in_dim.87, s32[20]{0:T(128)S(1)} %copy-done.63, f32[20,73728]{1,0:T(8,128)} %fusion.18), kind=kCustom, calls=%fused_computation.6 | custom fusion | bytes 17694800 | tf_op jit(solution)/shard_map/scatter | solution.py:279
  1585.6 7.4 reduce.24
  1606.2 102.3 %all-to-all-done.4 = bf16[32,2,36864]{2,1,0:T(2,128)(2,1)} async-done(((bf16[32,2,36864]{2,1,0:T(2,128)(2,1)}), bf16[32,2,36864]{2,1,0:T(2,128)(2,1)}, u32[]{:S(2)}, u32[]{:S(2)}) %all-to-all-start.4) | async-done | bytes 4718624 | tf_op jit(solution)/shard_map/all_to_all | solution.py:280
  1708.5 20.2 reshape.471
  1728.6 32.5 %convert_reduce_fusion = f32[32,73728]{1,0:T(8,128)} fusion(bf16[32,1,73728]{2,1,0:T(2,128)(2,1)} %reshape.471), kind=kLoop, calls=%fused_computation.19 | loop fusion | flops 2359296 | bytes 14155776 | tf_op jit(solution)/shard_map/reshape | solution.py:302
  1761.1 11.2 copy.443
  1778.9 13.6 copy.362
  1792.4 9.5 copy.390
  1807.7 26.0 %fusion.47 = f32[768,768]{1,0:T(8,128)S(1)} fusion(f32[768,3072]{1,0:T(8,128)} %bitcast.200, bf16[768,768]{1,0:T(8,128)(2,1)S(1)} %reshape.363, f32[]{:T(128)S(6)} %add.273, pred[]{:T(512)S(6)} %and.27), kind=kOutput, calls=%fused_computation.88 | convolution fusion | flops 21750349824 | bytes 12976133 | tf_op jit(solution)/shard_map/dot_general | solution.py:54
  1839.7 24.4 %multiply_add_fusion.4 = f32[768,3072]{1,0:T(8,128)S(1)} fusion(f32[768,768]{1,0:T(8,128)S(1)} %fusion.135, f32[768,768]{1,0:T(8,128)S(1)} %fusion.47, f32[]{:T(128)S(6)} %add.273, f32[768,3072]{1,0:T(8,128)S(1)} %bitcast.203, bf16[768,768]{1,0:T(8,128)(2,1)S(1)} %reshape.363, pred[]{:T(512)S(6)} %and.27), kind=kOutput, calls=%fused_computation.25 | convolution fusion | flops 21763915776 | bytes 24772612 | tf_op jit(solution)/shard_map/dot_general | solution.py:63
  1864.1 24.1 %fusion.136 = f32[768,768]{1,0:T(8,128)S(1)} fusion(f32[768,3072]{1,0:T(8,128)S(1)} %multiply_add_fusion.4), kind=kOutput, calls=%fused_computation.241 | convolution fusion | flops 21743271936 | bytes 11796480 | tf_op jit(solution)/shard_map/dot_general | solution.py:54
  1894.2 24.2 %multiply_add_fusion.3 = f32[768,3072]{1,0:T(8,128)S(1)} fusion(f32[768,3072]{1,0:T(8,128)S(1)} %multiply_add_fusion.4, f32[768,768]{1,0:T(8,128)S(1)} %fusion.137, f32[768,768]{1,0:T(8,128)S(1)} %fusion.136), kind=kOutput, calls=%fused_computation.24 | convolution fusion | flops 21749760000 | bytes 23592960 | tf_op jit(solution)/shard_map/dot_general | solution.py:63
  1918.4 24.1 %fusion.138 = f32[768,768]{1,0:T(8,128)S(1)} fusion(f32[768,3072]{1,0:T(8,128)S(1)} %multiply_add_fusion.3), kind=kOutput, calls=%fused_computation.243 | convolution fusion | flops 21743271936 | bytes 11796480 | tf_op jit(solution)/shard_map/dot_general | solution.py:54
  1948.5 24.2 %multiply_add_fusion.2 = f32[768,3072]{1,0:T(8,128)S(1)} fusion(f32[768,3072]{1,0:T(8,128)S(1)} %multiply_add_fusion.3, f32[768,768]{1,0:T(8,128)S(1)} %fusion.139, f32[768,768]{1,0:T(8,128)S(1)} %fusion.138), kind=kOutput, calls=%fused_computation.23 | convolution fusion | flops 21749760000 | bytes 23592960 | tf_op jit(solution)/shard_map/dot_general | solution.py:63
  1972.8 24.1 %fusion.140 = f32[768,768]{1,0:T(8,128)S(1)} fusion(f32[768,3072]{1,0:T(8,128)S(1)} %multiply_add_fusion.2), kind=kOutput, calls=%fused_computation.245 | convolution fusion | flops 21743271936 | bytes 11796480 | tf_op jit(solution)/shard_map/dot_general | solution.py:54
  2002.9 24.1 %multiply_add_fusion.1 = f32[768,3072]{1,0:T(8,128)S(1)} fusion(f32[768,3072]{1,0:T(8,128)S(1)} %multiply_add_fusion.2, f32[768,768]{1,0:T(8,128)S(1)} %fusion.141, f32[768,768]{1,0:T(8,128)S(1)} %fusion.140), kind=kOutput, calls=%fused_computation.22 | convolution fusion | flops 21749760000 | bytes 23592960 | tf_op jit(solution)/shard_map/dot_general | solution.py:63
  2027.0 24.1 %fusion.142 = f32[768,768]{1,0:T(8,128)S(1)} fusion(f32[768,3072]{1,0:T(8,128)S(1)} %multiply_add_fusion.1), kind=kOutput, calls=%fused_computation.247 | convolution fusion | flops 21743271936 | bytes 11796480 | tf_op jit(solution)/shard_map/dot_general | solution.py:54
  2057.0 25.0 %multiply_add_fusion = bf16[768,3072]{1,0:T(8,128)(2,1)} fusion(f32[768,3072]{1,0:T(8,128)S(1)} %multiply_add_fusion.1, f32[768,768]{1,0:T(8,128)S(1)} %fusion.143, f32[768,768]{1,0:T(8,128)S(1)} %fusion.142), kind=kOutput, calls=%fused_computation.21 | convolution fusion | flops 21752119296 | bytes 18874368 | tf_op jit(solution)/shard_map/dot_general | solution.py:63
  2082.1 9.9 reshape.367
  2103.6 7.4 reduce.25
  2118.1 14.8 all-to-all-start.5
  2141.5 118.3 %all-reduce.8 = (f32[2,768]{1,0:T(2,128)S(1)}, f32[2,768]{1,0:T(2,128)S(1)}) all-reduce(f32[2,768]{1,0:T(2,128)S(1)} %pad_maximum_fusion.1, f32[2,768]{1,0:T(2,128)S(1)} %pad_maximum_fusion.2), channel_id=6, replica_groups=mesh['shard'=4,'ctx'=2,'tp'=4] {'shard','ctx','tp'}, use_global_device_ids=true, to_apply=%region_24.25.clone | all-reduce | flops 3072 | bytes 24576
  2262.8 20.3 reshape.473
  2283.2 12.8 bitcast_convert_fusion
  2295.9 11.2 gather_fusion.5
  (339 shorter events, 320.1 us)
Async XLA Ops:
  7.2 136.5 %copy-start.9 = (bf16[1,394,768]{2,1,0:T(8,128)(2,1)S(1)}, bf16[1,394,768]{2,1,0:T(8,128)(2,1)}, u32[]{:S(2)}) copy-start(bf16[1,394,768]{2,1,0:T(8,128)(2,1)} %param.20) | copy-start | bytes 1815556
  7.2 137.1 %all-gather.9.cloned.1.call-start = ((), (), s32[]{:S(2)}) async-start(), calls=%async_computation.11 | async-start | bytes 3649536 | tf_op jit(solution)/shard_map/all_gather | solution.py:110
  7.9 238.4 %all-gather.11.cloned.1.call-start = ((), (), s32[]{:S(2)}) async-start(), calls=%async_computation.12 | async-start | bytes 1216512 | tf_op jit(solution)/shard_map/all_gather | solution.py:111
  8.7 279.8 %all-gather.15.cloned.1.call-start = ((), (), s32[]{:S(2)}) async-start(), calls=%async_computation.14 | async-start | bytes 10616832 | tf_op jit(solution)/shard_map/all_gather | solution.py:76
  143.7 105.1 %copy-start.38 = (f32[768]{0:T(1024)}, f32[768]{0:T(1024)S(1)}, u32[]{:S(2)}) copy-start(f32[768]{0:T(1024)S(1)} %get-tuple-element.206) | copy-start | bytes 9220
  152.3 62.1 %all-to-all-start = ((bf16[3,394,768]{1,0,2:T(4,128)(2,1)}), bf16[3,394,768]{1,0,2:T(4,128)(2,1)}, u32[]{:S(2)}, u32[]{:S(2)}) async-start(bf16[3,394,768]{1,0,2:T(4,128)(2,1)} %copy.316), calls=%async_computation | async-start | bytes 6291456 | tf_op jit(solution)/shard_map/all_to_all | solution.py:122
  160.3 58.9 %copy-start.45 = (s32[788]{0:T(1024)}, s32[788]{0:T(1024)S(1)}, u32[]{:S(2)}) copy-start(s32[788]{0:T(1024)S(1)} %fusion.113) | copy-start | bytes 9460
  222.5 5.2 copy-start.20
  234.7 10.6 all-to-all-start.1
  238.2 195.7 %all-gather.13.cloned.1.call-start = ((), (), s32[]{:S(2)}) async-start(), calls=%async_computation.13 | async-start | bytes 12103680 | tf_op jit(solution)/shard_map/all_gather | solution.py:148
  248.6 7.5 copy-start.40
  248.9 7.2 copy-start.47
  261.5 342.9 %all-gather.19.cloned.1.call-start = ((), (), s32[]{:S(2)}) async-start(), calls=%async_computation.17 | async-start | bytes 12103680 | tf_op jit(solution)/shard_map/all_gather | solution.py:165
  267.8 5.7 copy-start.58
  287.9 375.3 %all-gather.17.cloned.1.call-start = ((), (), s32[]{:S(2)}) async-start(), calls=%async_computation.15 | async-start | bytes 10616832 | tf_op jit(solution)/shard_map/all_gather | solution.py:77
  288.4 592.2 %reduce-scatter.10.cloned.1.call-start = ((), (), s32[]{:S(2)}) async-start(), calls=%async_computation.18 | async-start | bytes 12103680 | tf_op jit(solution)/shard_map/reduce_scatter | solution.py:179
  715.3 333.9 %reduce-scatter.8.cloned.1.call-start = ((), (), s32[]{:S(2)}) async-start(), calls=%async_computation.16 | async-start | bytes 12103680 | tf_op jit(solution)/shard_map/reduce_scatter | solution.py:153
  742.2 445.3 %reduce-scatter.14.cloned.1.call-start = ((), (), s32[]{:S(2)}) async-start(), calls=%async_computation.20 | async-start | bytes 10616832 | tf_op jit(solution)/shard_map/reduce_scatter | solution.py:243
  760.3 456.0 %reduce-scatter.16.cloned.1.call-start = ((), (), s32[]{:S(2)}) async-start(), calls=%async_computation.21 | async-start | bytes 10616832 | tf_op jit(solution)/shard_map/reduce_scatter | solution.py:246
  897.5 156.0 %copy-start.4 = (f32[788,768]{1,0:T(8,128)}, f32[788,768]{1,0:T(8,128)S(1)}, u32[]{:S(2)}) copy-start(f32[788,768]{1,0:T(8,128)S(1)} %gather_fusion.4) | copy-start | bytes 7262212
  1081.7 6.0 copy-start.6
  1082.4 5.3 copy-start.22
  1084.1 20.2 all-to-all-start.2
  1087.6 234.1 %reduce-scatter.12.cloned.1.call-start = ((), (), s32[]{:S(2)}) async-start(), calls=%async_computation.19 | async-start | bytes 2433024 | tf_op jit(solution)/shard_map/reduce_scatter | solution.py:228
  1089.9 18.3 copy-start.17
  1090.0 18.3 copy-start.34
  1090.0 428.2 %all-reduce.11.cloned.1.call-start = ((), (), s32[]{:S(2)}) async-start(), calls=%async_computation.22 | async-start | bytes 18874368
  1106.2 6.1 slice-start
  1171.3 5.0 copy-start.8
  1221.0 100.7 %copy-start.37 = (f32[24,768]{1,0:T(8,128)S(1)}, f32[24,768]{1,0:T(8,128)}, u32[]{:S(2)}) copy-start(f32[24,768]{1,0:T(8,128)} %param.31) | copy-start | bytes 221188
  1221.0 297.1 %copy-start.31 = (f32[3,24,768]{2,1,0:T(8,128)S(1)}, f32[3,24,768]{2,1,0:T(8,128)}, u32[]{:S(2)}) copy-start(f32[3,24,768]{2,1,0:T(8,128)} %param.30) | copy-start | bytes 663556
  1600.1 108.3 %all-to-all-start.4 = ((bf16[32,2,36864]{2,1,0:T(2,128)(2,1)}), bf16[32,2,36864]{2,1,0:T(2,128)(2,1)}, u32[]{:S(2)}, u32[]{:S(2)}) async-start(bf16[32,2,36864]{2,1,0:T(2,128)(2,1)} %reshape.470), calls=%async_computation.9 | async-start | bytes 9437184 | tf_op jit(solution)/shard_map/all_to_all | solution.py:280
  1761.1 11.2 copy-start.1
  1803.9 35.8 %slice-start.2 = ((s8[9437184]{0:T(1024)(128)(4,1)}), s8[1048576]{0:T(1024)(128)(4,1)S(1)}, s32[]{:S(2)}) async-start(s8[9437184]{0:T(1024)(128)(4,1)} %bitcast.201), calls=%async_computation.25 | async-start | bytes 2097152
  1807.6 32.1 %slice-start.3 = ((s8[9437184]{0:T(1024)(128)(4,1)}), s8[4194304]{0:T(1024)(128)(4,1)S(1)}, s32[]{:S(2)}) async-start(s8[9437184]{0:T(1024)(128)(4,1)} %bitcast.201), calls=%async_computation.26 | async-start | bytes 8388608
  1807.7 32.1 %slice-start.4 = ((s8[9437184]{0:T(1024)(128)(4,1)}), s8[4194304]{0:T(1024)(128)(4,1)S(1)}, s32[]{:S(2)}) async-start(s8[9437184]{0:T(1024)(128)(4,1)} %bitcast.201), calls=%async_computation.27 | async-start | bytes 8388608
  2095.2 4.9 slice-start.5
  2118.1 14.9 copy-start.64
  2118.1 14.9 copy-start.5
  2118.1 15.1 copy-start.57
  2118.1 144.7 %all-to-all-start.5 = ((bf16[32,2,36864]{2,1,0:T(2,128)(2,1)}), bf16[32,2,36864]{2,1,0:T(2,128)(2,1)}, u32[]{:S(2)}, u32[]{:S(2)}) async-start(bf16[32,2,36864]{2,1,0:T(2,128)(2,1)} %reshape.472), calls=%async_computation.10 | async-start | bytes 9437184 | tf_op jit(solution)/shard_map/all_to_all | solution.py:318
  2138.7 121.1 %copy-start.61 = (bf16[2,24]{1,0:T(2,128)(2,1)S(1)}, bf16[2,24]{1,0:T(2,128)(2,1)}, u32[]{:S(2)}) copy-start(bf16[2,24]{1,0:T(2,128)(2,1)} %param.27) | copy-start | bytes 292
  2138.7 121.1 %copy-start.65 = (f32[2,24]{1,0:T(2,128)S(1)}, f32[2,24]{1,0:T(2,128)}, u32[]{:S(2)}) copy-start(f32[2,24]{1,0:T(2,128)} %param.33) | copy-start | bytes 580
  2138.7 121.8 %copy-start.62 = (bf16[2,24]{1,0:T(2,128)(2,1)S(1)}, bf16[2,24]{1,0:T(2,128)(2,1)}, u32[]{:S(2)}) copy-start(bf16[2,24]{1,0:T(2,128)(2,1)} %param.26) | copy-start | bytes 292
  2138.7 121.8 %copy-start.66 = (f32[2,24]{1,0:T(2,128)S(1)}, f32[2,24]{1,0:T(2,128)}, u32[]{:S(2)}) copy-start(f32[2,24]{1,0:T(2,128)} %param.32) | copy-start | bytes 580
  2138.7 122.4 %copy-start.27 = (f32[3,24,768]{2,0,1:T(4,128)S(1)}, f32[3,24,768]{2,0,1:T(4,128)}, u32[]{:S(2)}) copy-start(f32[3,24,768]{2,0,1:T(4,128)} %get-tuple-element.188) | copy-start | bytes 663556
  2139.2 122.6 %copy-start.32 = (f32[3,24,768]{2,1,0:T(8,128)S(1)}, f32[3,24,768]{2,1,0:T(8,128)}, u32[]{:S(2)}) copy-start(f32[3,24,768]{2,1,0:T(8,128)} %param.30) | copy-start | bytes 663556
  2307.1 6.7 copy-start.24
  (42 other events, 121.3 us)
Sparse Core Ops, SparseCore 0:
  11.1 63.0 all-gather.8
  76.9 52.8 all-gather.10
  131.8 80.2 all-gather.14
  261.6 172.2 all-gather.12
  435.3 168.9 all-gather.18
  606.1 57.0 all-gather.16
  715.4 165.2 reduce-scatter.9
  883.0 166.0 reduce-scatter.7
  1052.6 83.7 reduce-scatter.13
  1139.7 76.4 reduce-scatter.15
  1222.7 99.0 reduce-scatter.11
  1328.4 189.7 all-reduce.10
where the time goes:
time: 2330 us
  waiting for transfers between devices  1090 us (47%)
  matrix products  429 us (18%)
  local copies, waits for them, and re-layouts  343 us (15%)
  blocking collectives  282 us (12%)
  other arithmetic  133 us (6%)
  starting transfers between devices  32.6 us (1%)
    unnamed x13, waiting for transfers between devices  197 us
    all_gather x1, waiting for transfers between devices, on_device(): group_grad = lax.all_gather(slot_grad, 'tp', axis=1, tiled=True)  151 us
    reduce_scatter x1, waiting for transfers between devices, on_device(): lax.psum_scatter(partial_out.astype(jnp.bfloat16), 'tp', scatter_dimensio...  149 us
    all_gather x1, waiting for transfers between devices, on_device(): group_slots = lax.all_gather(slot_rows, 'tp', axis=1, tiled=True)  145 us
    dot_general x5, matrix products, orthogonal(): lax.dot_general(current, current, (((1,), (1,)), ((), ())), precision=hig...  122 us
    dot_general x5, matrix products, orthogonal(): jnp.dot(mixer, current, precision=highest, preferred_element_type=jnp.flo...  122 us
    unnamed x1, blocking collectives  118 us
    unnamed x162, local copies, waits for them, and re-layouts  103 us
  transfers between devices with their start and end apart: 17, of which 12 were waited for; matrix products, arithmetic and copies ran while one was open for 13% of the time, Pallas kernels for 0%

commit v1 on v0

--- a/solution.py
+++ b/solution.py
@@ -1,9 +1,12 @@
+import functools
 import math
 
 import jax
 import jax.numpy as jnp
 import numpy as np
 from jax import lax
+from jax.experimental import pallas as pl
+from jax.experimental.pallas import tpu as pltpu
 from jax.sharding import PartitionSpec as P
 
 HEAD_DIM = 64
@@ -359,6 +362,1245 @@
     )
 
 
+axes = ("shard", "ctx", "tp")
+TILE = 256
+SPAN = 208
+VMEM_ASK = 60 * 1024 * 1024
+
+
+def dot_nn(left, right):
+    return lax.dot_general(
+        left, right, (((1,), (0,)), ((), ())), preferred_element_type=jnp.float32
+    )
+
+
+def dot_nt(left, right):
+    return lax.dot_general(
+        left, right, (((1,), (1,)), ((), ())), preferred_element_type=jnp.float32
+    )
+
+
+def dot_tn(left, right):
+    return lax.dot_general(
+        left, right, (((0,), (0,)), ((), ())), preferred_element_type=jnp.float32
+    )
+
+
+def tile_pairs(count):
+    return [(row, col) for row in range(count) for col in range(row, count)]
+
+
+def wide_bands(size):
+    return [pl.ds(start, TILE) for start in range(0, size, TILE)]
+
+
+def wide_steps(count, gram, whole, low, whole_low, mixer):
+    bands = wide_bands(gram.shape[0])
+
+    def step(repeat, carry):
+        wide_mix(gram, whole, low, whole_low, mixer)
+        for band in bands:
+            half = first_coef * gram[band, :] + dot_nn(mixer[band, :], low[...])
+            gram[band, :] = first_coef * half + dot_nn(half.astype(jnp.bfloat16), mixer[...])
+            whole[band, :] = first_coef * whole[band, :] + dot_nn(mixer[band, :], whole_low[...])
+        return carry
+
+    lax.fori_loop(0, count, step, 0)
+
+
+def wide_mix(gram, whole, low, whole_low, mixer):
+    low[...] = gram[...].astype(jnp.bfloat16)
+    whole_low[...] = whole[...].astype(jnp.bfloat16)
+    for band in wide_bands(gram.shape[0]):
+        squared = dot_nn(low[band, :], low[...])
+        mixer[band, :] = (second_coef * gram[band, :] + third_coef * squared).astype(jnp.bfloat16)
+
+
+def wide_first_kernel(block0, block1, block3, part0, part1, part2, gram, whole, low, mixer, whole_low, block2):
+    size = gram.shape[0]
+    bands = wide_bands(size)
+    rows = lax.broadcasted_iota(jnp.int32, (TILE, size), 0)
+    cols = lax.broadcasted_iota(jnp.int32, (TILE, size), 1)
+    for part, band in zip((part0, part1, part2), bands):
+        block2[band, :] = part[...]
+    trace = 0.0
+    for place, band in enumerate(bands):
+        part = dot_nt(block0[band, :], block0[...])
+        for block in (block1, block2, block3):
+            part = part + dot_nt(block[band, :], block[...])
+        gram[band, :] = part
+        trace = trace + jnp.sum(jnp.where(rows + place * TILE == cols, part, 0.0))
+    factor = 1.0 / (jnp.sqrt(trace) + orth_epsilon)
+    for place, band in enumerate(bands):
+        gram[band, :] = gram[band, :] * (factor * factor)
+        whole[band, :] = jnp.where(rows + place * TILE == cols, factor, 0.0)
+    wide_steps(2, gram, whole, low, whole_low, mixer)
+
+
+def wide_last_kernel(gram_in, whole_in, out, gram, whole, low, mixer, whole_low):
+    bands = wide_bands(gram.shape[0])
+    gram[...] = gram_in[...]
+    whole[...] = whole_in[...]
+    wide_steps(2, gram, whole, low, whole_low, mixer)
+    wide_mix(gram, whole, low, whole_low, mixer)
+    for row, band in enumerate(bands):
+        last = first_coef * whole[band, :] + dot_nn(mixer[band, :], whole_low[...])
+        for place, pair in enumerate(tile_pairs(len(bands))):
+            if pair[0] == row:
+                out[place] = last[:, pair[1] * TILE : (pair[1] + 1) * TILE].astype(out.dtype)
+
+
+def wide_call(kernel, size, out_shape, kept, scratch, name, inputs):
+    vmem = pl.BlockSpec(memory_space=pltpu.VMEM)
+    square = (size, size)
+    return pl.pallas_call(
+        kernel,
+        out_shape=out_shape,
+        in_specs=[vmem] * len(inputs),
+        out_specs=jax.tree.map(lambda shape: vmem, out_shape),
+        scratch_shapes=[pltpu.VMEM(square, jnp.float32)] * kept
+        + [pltpu.VMEM(square, jnp.bfloat16)] * scratch,
+        compiler_params=pltpu.CompilerParams(vmem_limit_bytes=VMEM_ASK),
+        cost_estimate=pl.CostEstimate(
+            flops=20 * size**3, bytes_accessed=8 * size * size, transcendentals=0
+        ),
+        name=name,
+    )(*inputs)
+
+
+def wide_first(blocks):
+    size = blocks[0].shape[0]
+    shape = jax.ShapeDtypeStruct((size, size), jnp.float32)
+    return wide_call(wide_first_kernel, size, [shape, shape], 0, 4, "wide_first", blocks)
+
+
+def wide_last(gram, whole):
+    size = gram.shape[0]
+    pairs = len(tile_pairs(size // TILE))
+    shape = jax.ShapeDtypeStruct((pairs, TILE, TILE), jnp.bfloat16)
+    return wide_call(wide_last_kernel, size, shape, 2, 3, "wide_last", (gram, whole))
+
+
+def store_rows(chip, value, outs, which):
+    depth = outs[0].shape[2]
+    for turn, out in enumerate(outs):
+        other = jnp.bitwise_xor(chip, turn)
+        for core in range(2):
+            row = ((other // 2) * 2 + core) * 2 + other % 2
+            out[which, core] = value[pl.ds(pl.multiple_of(row * depth, 16), depth), :].astype(
+                out.dtype
+            )
+
+
+def apply_kernel(place, *refs):
+    mixers, pushes, outs, (full, moved) = refs[:4], refs[4:6], refs[6:10], refs[10:]
+    chip, core, tp = place[0], place[1], place[2]
+    count = full.shape[0] // TILE
+    for which in range(2):
+        source = lax.rem(tp - 2 * core - which + 4, 4)
+        for step in range(4):
+
+            @pl.when(source == step)
+            def _():
+                for spot, (row, col) in enumerate(tile_pairs(count)):
+                    tile = mixers[step][spot]
+                    full[pl.ds(row * TILE, TILE), pl.ds(col * TILE, TILE)] = tile
+                    if row != col:
+                        full[pl.ds(col * TILE, TILE), pl.ds(row * TILE, TILE)] = tile.T
+
+        for spot in range(2):
+
+            @pl.when(lax.rem(tp + spot, 2) == which)
+            def _():
+                moved[...] = dot_nn(full[...], pushes[spot][...])
+
+        store_rows(chip, moved, outs, which)
+
+
+def apply_mixers(place, mixers, pushes, depth):
+    size, width = pushes[0].shape
+    vmem = pl.BlockSpec(memory_space=pltpu.VMEM)
+    shape = jax.ShapeDtypeStruct((2, 2, depth, width), jnp.bfloat16)
+    return pl.pallas_call(
+        apply_kernel,
+        in_specs=[pl.BlockSpec(memory_space=pltpu.SMEM)] + [vmem] * 6,
+        out_specs=[vmem] * 4,
+        out_shape=[shape] * 4,
+        scratch_shapes=[
+            pltpu.VMEM((size, size), jnp.bfloat16),
+            pltpu.VMEM((size, width), jnp.float32),
+        ],
+        compiler_params=pltpu.CompilerParams(vmem_limit_bytes=VMEM_ASK),
+        cost_estimate=pl.CostEstimate(
+            flops=4 * size**3, bytes_accessed=10 * size * size, transcendentals=0
+        ),
+        name="apply_mixers",
+    )(place, *mixers, *pushes)
+
+
+def push_kernel(place, own, *refs):
+    gots, moments, refs = refs[:2], refs[2:6], refs[6:]
+    pushes, outs, (total,) = refs[:2], refs[2:6], refs[6:]
+    chip, core, tp = place[0], place[1], place[2]
+    keep = 1.0 - momentum_decay
+    depth = outs[0].shape[2]
+    for which in range(2):
+        total[...] = (
+            own[which].astype(jnp.float32)
+            + gots[0][which].astype(jnp.float32)
+            + gots[1][which].astype(jnp.float32)
+        )
+        store_rows(chip, total, outs, which)
+        for turn, moment in enumerate(moments):
+            other = jnp.bitwise_xor(chip, turn)
+            for side in range(2):
+                row = ((other // 2) * 2 + jnp.bitwise_xor(core, side)) * 2 + other % 2
+                rows = pl.ds(pl.multiple_of(row * depth, 16), depth)
+                pushed = (
+                    (keep + momentum_decay * keep) * total[rows, :]
+                    + momentum_decay * momentum_decay * moment[2 * which + side].astype(jnp.float32)
+                ).astype(jnp.bfloat16)
+                for spot in range(2):
+
+                    @pl.when(lax.rem(tp + spot, 2) == which)
+                    def _():
+                        pushes[spot][rows, :] = pushed
+
+
+def push_rows(place, own, gots, moments):
+    size, width = own.shape[1:]
+    depth = moments[0].shape[1]
+    vmem = pl.BlockSpec(memory_space=pltpu.VMEM)
+    rows = jax.ShapeDtypeStruct((2, 2, depth, width), jnp.bfloat16)
+    return pl.pallas_call(
+        push_kernel,
+        in_specs=[pl.BlockSpec(memory_space=pltpu.SMEM)] + [vmem] * 7,
+        out_specs=[vmem] * 6,
+        out_shape=[jax.ShapeDtypeStruct((size, width), jnp.bfloat16)] * 2 + [rows] * 4,
+        scratch_shapes=[pltpu.VMEM((size, width), jnp.float32)],
+        compiler_params=pltpu.CompilerParams(vmem_limit_bytes=VMEM_ASK),
+        cost_estimate=pl.CostEstimate(
+            flops=20 * size * width, bytes_accessed=24 * size * width, transcendentals=0
+        ),
+        name="push_rows",
+    )(place, own, *gots, *moments)
+
+
+def square_kernel(matrix, out, current, low, square, square_low, mixer):
+    size = current.shape[0]
+    bands = [pl.ds(start, TILE) for start in range(0, size, TILE)]
+    total = 0.0
+    for band in bands:
+        part = matrix[band, :].astype(jnp.float32)
+        total = total + jnp.sum(part * part)
+    factor = 1.0 / (jnp.sqrt(total) + orth_epsilon)
+    for band in bands:
+        current[band, :] = matrix[band, :].astype(jnp.float32) * factor
+
+    def step(repeat, carry):
+        low[...] = current[...].astype(jnp.bfloat16)
+        for band in bands:
+            part = dot_nt(low[band, :], low[...])
+            square[band, :] = part
+            square_low[band, :] = part.astype(jnp.bfloat16)
+        for band in bands:
+            mixed = second_coef * square[band, :] + third_coef * dot_nn(
+                square_low[band, :], square_low[...]
+            )
+            mixer[band, :] = mixed.astype(jnp.bfloat16)
+        for band in bands:
+            current[band, :] = first_coef * current[band, :] + dot_nn(mixer[band, :], low[...])
+        return carry
+
+    lax.fori_loop(0, 5, step, 0)
+    out[...] = current[...].astype(out.dtype)
+
+
+def orthogonal_square(matrix):
+    size = matrix.shape[0]
+    return pl.pallas_call(
+        square_kernel,
+        out_shape=jax.ShapeDtypeStruct((size, size), jnp.bfloat16),
+        in_specs=[pl.BlockSpec(memory_space=pltpu.VMEM)],
+        out_specs=pl.BlockSpec(memory_space=pltpu.VMEM),
+        scratch_shapes=[
+            pltpu.VMEM((size, size), jnp.float32),
+            pltpu.VMEM((size, size), jnp.bfloat16),
+            pltpu.VMEM((size, size), jnp.float32),
+            pltpu.VMEM((size, size), jnp.bfloat16),
+            pltpu.VMEM((size, size), jnp.bfloat16),
+        ],
+        compiler_params=pltpu.CompilerParams(vmem_limit_bytes=VMEM_ASK),
+        cost_estimate=pl.CostEstimate(
+            flops=30 * size**3, bytes_accessed=4 * matrix.size, transcendentals=0
+        ),
+        name="square_orthogonal",
+    )(matrix)
+
+
+root = math.sqrt(2.0 / math.pi)
+
+
+def gelu_pair(value):
+    squared = value * value
+    part = 0.5 * jnp.tanh(value * (root + (root * 0.044715) * squared)) + 0.5
+    bend = value * (2.0 * root + (6.0 * root * 0.044715) * squared)
+    return value * part, part + part * (1.0 - part) * bend
+
+
+def one_hot(rank):
+    return lax.broadcasted_iota(jnp.int32, (SPAN, rank.shape[1]), 0) == rank
+
+
+def assemble(chip, core, pieces, whole):
+    depth = pieces[0].shape[1]
+    for place, piece in enumerate(pieces):
+        other = jnp.bitwise_xor(chip, place // 2)
+        row = ((other // 2) * 2 + jnp.bitwise_xor(core, place % 2)) * 2 + other % 2
+        whole[pl.ds(pl.multiple_of(row * depth, 16), depth), :] = piece[0]
+
+
+def gate_of(hot, gate):
+    return jnp.sum(jnp.where(hot, gate, 0.0), axis=1, keepdims=True)
+
+
+def experts_kernel(
+    starts, rank, gate, *refs
+):
+    blocks = rank.shape[1]
+    ups, downs, refs = refs[:8], refs[8:16], refs[16:]
+    tokens_hbm, refs = refs[: 2 * blocks], refs[2 * blocks :]
+    hidden_out, before_out, *refs = refs
+    outs, refs = refs[:5], refs[5:]
+    rows, cots, upper, lower, slots, grads, upper_sum, lower_sum, leaving, sems, out_sems = refs
+    targets = [(outs[turn].at[0], outs[turn].at[1]) for turn in range(3)] + [(outs[3], outs[4])]
+    expert = pl.program_id(0)
+    base = expert * (blocks + 1)
+    chip = starts[pl.num_programs(0) * (blocks + 1)]
+    core = starts[pl.num_programs(0) * (blocks + 1) + 1]
+    low = jnp.bfloat16
+
+    @pl.when(expert == 0)
+    def _():
+        copies = []
+        for block in range(blocks):
+            for which, held in enumerate((rows, cots)):
+                place = which * blocks + block
+                copies.append(
+                    pltpu.make_async_copy(tokens_hbm[place], held.at[block], sems.at[place])
+                )
+        for copy in copies:
+            copy.start()
+
+    assemble(chip, core, ups, upper)
+    assemble(chip, core, downs, lower)
+
+    for block in range(blocks):
+
+        @pl.when(expert == 0)
+        def _():
+            for which, held in enumerate((rows, cots)):
+                place = which * blocks + block
+                pltpu.make_async_copy(tokens_hbm[place], held.at[block], sems.at[place]).wait()
+
+        start = pl.multiple_of(starts[base + block], 16)
+        hot = one_hot(rank[0, block : block + 1, :])
+        spread = jnp.where(hot, 1.0, 0.0).astype(low)
+        weight = gate_of(hot, gate[0, block : block + 1, :])
+        slots[pl.ds(start, SPAN), :] = dot_nn(spread, rows[block]).astype(low)
+        grads[pl.ds(start, SPAN), :] = (dot_nn(spread, cots[block]) * weight).astype(low)
+
+    end = pl.multiple_of(starts[base + blocks], 16)
+    slots[pl.ds(end, TILE), :] = jnp.zeros((TILE, slots.shape[1]), low)
+    grads[pl.ds(end, TILE), :] = jnp.zeros((TILE, slots.shape[1]), low)
+    upper_sum[...] = jnp.zeros_like(upper_sum)
+    lower_sum[...] = jnp.zeros_like(lower_sum)
+
+    def work(tile, carry):
+        band = pl.ds(pl.multiple_of(tile * TILE, TILE), TILE)
+        slot_rows, slot_grads = slots[band, :], grads[band, :]
+        hidden, slope = gelu_pair(dot_nn(slot_rows, upper[...]))
+        hidden = hidden.astype(low)
+        d_before = (dot_nn(slot_grads, lower[...]) * slope).astype(low)
+        hidden_out[0, band, :] = hidden
+        before_out[0, band, :] = d_before
+        upper_sum[...] += dot_tn(slot_rows, d_before)
+        lower_sum[...] += dot_tn(slot_grads, hidden)
+        return carry
+
+    lax.fori_loop(0, (starts[base + blocks] + TILE - 1) // TILE, work, 0)
+
+    for turn, target in enumerate(targets):
+
+        @pl.when(expert == turn)
+        def _():
+            if turn > 0:
+                for which in range(2):
+                    pltpu.make_async_copy(
+                        leaving.at[which], targets[turn - 1][which], out_sems.at[2 * turn - 2 + which]
+                    ).wait()
+            leaving[0] = upper_sum[...].astype(low)
+            leaving[1] = lower_sum[...].astype(low)
+            copies = [
+                pltpu.make_async_copy(leaving.at[which], target[which], out_sems.at[2 * turn + which])
+                for which in range(2)
+            ]
+            for copy in copies:
+                copy.start()
+            if turn == 3:
+                for copy in copies:
+                    copy.wait()
+
+
+def tokens_kernel(
+    gated, starts, rank, gate, acts, *refs
+):
+    pieces, (part_own, part_other, whole, moved, spread, found) = refs[:8], refs[8:]
+    expert = pl.program_id(0)
+    count, blocks = rank.shape[0], rank.shape[1]
+    base = expert * (blocks + 1)
+    chip, core = starts[count * (blocks + 1)], starts[count * (blocks + 1) + 1]
+    low = jnp.bfloat16
+
+    @pl.when(expert == 0)
+    def _():
+        moved[...] = jnp.zeros_like(moved)
+
+    assemble(chip, core, pieces, whole)
+
+    def work(tile, carry):
+        band = pl.ds(pl.multiple_of(tile * TILE, TILE), TILE)
+        moved[expert, band, :] = dot_nt(acts[0, band, :], whole[...]).astype(low)
+        return carry
+
+    lax.fori_loop(0, (starts[base + blocks] + TILE - 1) // TILE, work, 0)
+
+    @pl.when(expert == count - 1)
+    def _():
+        for side, part in enumerate((part_own, part_other)):
+
+            def collect(place, carry):
+                block = side * (blocks // 2) + place
+                for each in range(count):
+                    start = pl.multiple_of(starts[each * (blocks + 1) + block], 16)
+                    hot = one_hot(rank[each, pl.ds(block, 1), :])
+                    rows = moved[each, pl.ds(start, SPAN), :]
+                    if gated:
+                        weight = gate_of(hot, gate[each, pl.ds(block, 1), :])
+                        rows = (rows.astype(jnp.float32) * weight).astype(low)
+                    band = pl.ds(each * SPAN, SPAN)
+                    spread[band, :] = jnp.where(hot, 1.0, 0.0).astype(low)
+                    found[band, :] = rows
+                part[place] = dot_tn(spread[...], found[...]).astype(low)
+                return carry
+
+            lax.fori_loop(0, blocks // 2, collect, 0)
+
+
+def pass_shapes(rank, pieces):
+    count = pieces[0].shape[0]
+    blocks, padded = rank.shape[1], rank.shape[2]
+    tiles = -(-blocks * SPAN // TILE)
+
+    def of_expert(expert, starts):
+        return (expert, 0, 0)
+
+    piece_specs = [
+        pl.BlockSpec(
+            (1,) + pieces[0].shape[1:],
+            lambda expert, starts, turn=place // 2: (jnp.bitwise_xor(expert, turn), 0, 0),
+        )
+        for place in range(8)
+    ]
+    return count, blocks, padded, tiles, of_expert, piece_specs
+
+
+def experts_pass(starts, rank, gate, rows, cots, ups, downs):
+    count, blocks, padded, tiles, of_expert, piece_specs = pass_shapes(rank, ups)
+    features = rows[0].shape[1]
+    width = ups[0].shape[2]
+    most = blocks * SPAN
+    low = jnp.bfloat16
+    vectors = pl.BlockSpec((1, blocks, padded), of_expert)
+    acts = pl.BlockSpec((1, tiles * TILE, width), of_expert)
+    acts_shape = jax.ShapeDtypeStruct((count, tiles * TILE, width), low)
+    grad_shape = jax.ShapeDtypeStruct((features, width), low)
+    pair_shape = jax.ShapeDtypeStruct((2, features, width), low)
+    return pl.pallas_call(
+        experts_kernel,
+        grid_spec=pltpu.PrefetchScalarGridSpec(
+            num_scalar_prefetch=1,
+            grid=(count,),
+            in_specs=[vectors, vectors]
+            + piece_specs * 2
+            + [pl.BlockSpec(memory_space=pl.ANY)] * (2 * blocks),
+            out_specs=[acts, acts] + [pl.BlockSpec(memory_space=pl.ANY)] * 5,
+            scratch_shapes=[
+                pltpu.VMEM((blocks, padded, features), low),
+                pltpu.VMEM((blocks, padded, features), low),
+                pltpu.VMEM((features, width), low),
+                pltpu.VMEM((features, width), low),
+                pltpu.VMEM((most + TILE, features), low),
+                pltpu.VMEM((most + TILE, features), low),
+                pltpu.VMEM((features, width), jnp.float32),
+                pltpu.VMEM((features, width), jnp.float32),
+                pltpu.VMEM((2, features, width), low),
+                pltpu.SemaphoreType.DMA((2 * blocks,)),
+                pltpu.SemaphoreType.DMA((8,)),
+            ],
+        ),
+        out_shape=[acts_shape, acts_shape] + [pair_shape] * 3 + [grad_shape] * 2,
+        compiler_params=pltpu.CompilerParams(vmem_limit_bytes=VMEM_ASK),
+        cost_estimate=pl.CostEstimate(
+            flops=4 * count * most * features * width,
+            bytes_accessed=60 * 1024 * 1024,
+            transcendentals=count * most * width,
+        ),
+        name="experts_pass",
+    )(starts, rank, gate, *ups, *downs, *rows, *cots)
+
+
+def tokens_pass(starts, rank, gate, acts, pieces, gated):
+    count, blocks, padded, tiles, of_expert, piece_specs = pass_shapes(rank, pieces)
+    width = pieces[0].shape[2]
+    features = 8 * pieces[0].shape[1]
+    most = blocks * SPAN
+    low = jnp.bfloat16
+    vectors = pl.BlockSpec(rank.shape, lambda expert, starts: (0, 0, 0))
+    parts = pl.BlockSpec((blocks // 2, padded, features), lambda expert, starts: (0, 0, 0))
+    part_shape = jax.ShapeDtypeStruct((blocks // 2, padded, features), low)
+    return pl.pallas_call(
+        functools.partial(tokens_kernel, gated),
+        grid_spec=pltpu.PrefetchScalarGridSpec(
+            num_scalar_prefetch=1,
+            grid=(count,),
+            in_specs=[vectors, vectors, pl.BlockSpec((1, tiles * TILE, width), of_expert)]
+            + piece_specs,
+            out_specs=[parts, parts],
+            scratch_shapes=[
+                pltpu.VMEM((features, width), low),
+                pltpu.VMEM((count, most + TILE, features), low),
+                pltpu.VMEM((count * SPAN, padded), low),
+                pltpu.VMEM((count * SPAN, features), low),
+            ],
+        ),
+        out_shape=[part_shape, part_shape],
+        compiler_params=pltpu.CompilerParams(vmem_limit_bytes=VMEM_ASK),
+        cost_estimate=pl.CostEstimate(
+            flops=2 * count * most * features * width,
+            bytes_accessed=30 * 1024 * 1024,
+            transcendentals=0,
+        ),
+        name="tokens_gated" if gated else "tokens_plain",
+    )(starts, rank, gate, acts, *pieces)
+
+
+IMAGE = 208
+
+
+def row_norm(values, factor, offset):
+    width = values.shape[1]
+    average = jnp.sum(values, axis=1, keepdims=True) / width
+    centred = values - average
+    spread = jnp.sum(centred * centred, axis=1, keepdims=True) / width
+    inverse = lax.rsqrt(spread + norm_epsilon)
+    unit = centred * inverse
+    return unit * factor + offset, unit, inverse
+
+
+def row_norm_back(gradient, unit, inverse, factor):
+    width = gradient.shape[1]
+    inner = gradient * factor
+    average = jnp.sum(inner, axis=1, keepdims=True) / width
+    along = jnp.sum(inner * unit, axis=1, keepdims=True) / width
+    return inverse * (inner - average - unit * along)
+
+
+def head_soft(query, key, here, keys_used):
+    own = jnp.where(here, query, jnp.zeros_like(query))
+    scores = dot_nt(own, key) * (HEAD_DIM ** (-0.5))
+    scores = jnp.where(keys_used, scores, -1e30)
+    powers = jnp.exp(scores - jnp.max(scores, axis=1, keepdims=True))
+    return powers / jnp.sum(powers, axis=1, keepdims=True)
+
+
+def forward_kernel(
+    place, tokens, norms, w0, w1, w2, w3, others_near, others_far,
+    normed_out, qkv_out, blended_out, residual_out, second_out, weights,
+):
+    features = tokens.shape[2]
+    low = jnp.bfloat16
+
+    @pl.when(pl.program_id(0) == 0)
+    def _():
+        chip, core = place[0], place[1]
+        depth = features // 8
+        others = (others_near.at[0], others_near.at[1], others_far.at[0], others_far.at[1])
+        for side, pieces in enumerate(((w0, w1, w2, w3), others)):
+            for turn, piece in enumerate(pieces):
+                other = jnp.bitwise_xor(chip, turn)
+                row = ((other // 2) * 2 + jnp.bitwise_xor(core, side)) * 2 + other % 2
+                rows = pl.ds(pl.multiple_of(row * depth, 16), depth)
+                for which in range(4):
+                    weights[which, rows, :] = piece[which]
+
+    normed, unused, unused = row_norm(
+        tokens[0].astype(jnp.float32), norms[0:1, :], norms[2:3, :]
+    )
+    normed_out[0] = normed.astype(low)
+    for which in range(3):
+        qkv_out[0, which] = dot_nn(normed_out[0], weights[which]).astype(low)
+    keys_used = lax.broadcasted_iota(jnp.int32, (IMAGE, IMAGE), 1) < LEN
+    first = lax.broadcasted_iota(jnp.int32, (IMAGE, 2 * HEAD_DIM), 1) < HEAD_DIM
+    for start in range(0, features, 2 * HEAD_DIM):
+        cols = pl.ds(start, 2 * HEAD_DIM)
+        query, key, value = (qkv_out[0, which, :, cols] for which in range(3))
+        mixed = []
+        for here in (first, jnp.logical_not(first)):
+            soft = head_soft(query, key, here, keys_used).astype(low)
+            mixed.append(dot_nn(soft, value))
+        blended_out[0, :, cols] = jnp.where(first, mixed[0], mixed[1]).astype(low)
+    residual = tokens[0].astype(jnp.float32) + dot_nn(blended_out[0], weights[3])
+    residual_out[0] = residual
+    second, unused, unused = row_norm(residual, norms[1:2, :], norms[3:4, :])
+    second_out[0] = second.astype(low)
+
+
+def attention_forward(place, tokens, norms, pieces, others):
+    images, rows, features = tokens.shape
+    low = jnp.bfloat16
+    image = pl.BlockSpec((1, rows, features), lambda i, place: (i, 0, 0))
+    shape = jax.ShapeDtypeStruct((images, rows, features), low)
+    return pl.pallas_call(
+        forward_kernel,
+        grid_spec=pltpu.PrefetchScalarGridSpec(
+            num_scalar_prefetch=1,
+            grid=(images,),
+            in_specs=[image, pl.BlockSpec(norms.shape, lambda i, place: (0, 0))]
+            + [pl.BlockSpec(pieces[0].shape, lambda i, place: (0, 0, 0))] * 4
+            + [pl.BlockSpec(others[0].shape, lambda i, place: (0, 0, 0, 0))] * 2,
+            out_specs=[
+                image,
+                pl.BlockSpec((1, 3, rows, features), lambda i, place: (i, 0, 0, 0)),
+                image,
+                image,
+                image,
+                pl.BlockSpec((4, features, features), lambda i, place: (0, 0, 0)),
+            ],
+        ),
+        out_shape=[
+            shape,
+            jax.ShapeDtypeStruct((images, 3, rows, features), low),
+            shape,
+            jax.ShapeDtypeStruct((images, rows, features), jnp.float32),
+            shape,
+            jax.ShapeDtypeStruct((4, features, features), low),
+        ],
+        compiler_params=pltpu.CompilerParams(vmem_limit_bytes=VMEM_ASK),
+        cost_estimate=pl.CostEstimate(
+            flops=10 * images * rows * features * features,
+            bytes_accessed=16 * 1024 * 1024,
+            transcendentals=0,
+        ),
+        name="attention_forward",
+    )(place, tokens, norms, *pieces, *others)
+
+
+def backward_kernel(
+    place, tokens, cots, residual, blended, normed, qkv, weights, norms,
+    second0, second1, second2, second3,
+    input_grad, mine, theirs, vectors,
+    parts, d_heads, d_qkv, d_sum,
+):
+    image = pl.program_id(0)
+    features = tokens.shape[2]
+    low = jnp.bfloat16
+    core = place[1]
+    seconds = (second0, second1, second2, second3)
+    last = image == pl.num_programs(0) - 1
+
+    @pl.when(image == 0)
+    def _():
+        vectors[...] = jnp.zeros_like(vectors)
+
+    d_second = seconds[0][0].astype(jnp.float32)
+    for piece in seconds[1:]:
+        d_second = d_second + piece[0].astype(jnp.float32)
+    unused, unit, inverse = row_norm(residual[0], norms[1:2, :], norms[3:4, :])
+    vectors[1:2, :] += jnp.sum(d_second * unit, axis=0, keepdims=True)
+    vectors[3:4, :] += jnp.sum(d_second, axis=0, keepdims=True)
+    d_sum[...] = cots[0].astype(jnp.float32) + row_norm_back(
+        d_second, unit, inverse, norms[1:2, :]
+    )
+    d_attended = d_sum[...].astype(low)
+    d_heads[...] = dot_nt(d_attended, weights[3]).astype(low)
+    out_part = dot_tn(blended[0], d_attended)
+
+    @pl.when(image == 0)
+    def _():
+        parts[3] = out_part
+
+    @pl.when(image > 0)
+    def _():
+        parts[3] = parts[3] + out_part
+
+    keys_used = lax.broadcasted_iota(jnp.int32, (IMAGE, IMAGE), 1) < LEN
+    first = lax.broadcasted_iota(jnp.int32, (IMAGE, 2 * HEAD_DIM), 1) < HEAD_DIM
+    scale = HEAD_DIM ** (-0.5)
+    for start in range(0, features, 2 * HEAD_DIM):
+        cols = pl.ds(start, 2 * HEAD_DIM)
+        query, key, value = (qkv[0, which, :, cols] for which in range(3))
+        upper = d_heads[:, cols]
+        found = []
+        for here in (first, jnp.logical_not(first)):
+            soft = head_soft(query, key, here, keys_used)
+            d_soft = dot_nt(jnp.where(here, upper, jnp.zeros_like(upper)), value)
+            inner = jnp.sum(soft * d_soft, axis=1, keepdims=True)
+            d_scores = (soft * (d_soft - inner)).astype(low)
+            found.append(
+                (
+                    dot_nn(d_scores, key) * scale,
+                    dot_tn(d_scores, query) * scale,
+                    dot_tn(soft.astype(low), upper),
+                )
+            )
+        for which in range(3):
+            d_qkv[which, :, cols] = jnp.where(first, found[0][which], found[1][which]).astype(low)
+    d_normed = dot_nt(d_qkv[0], weights[0])
+    for which in range(1, 3):
+        d_normed = d_normed + dot_nt(d_qkv[which], weights[which])
+    for which in range(3):
+        in_part = dot_tn(normed[0], d_qkv[which])
+
+        @pl.when(image == 0)
+        def _():
+            parts[which] = in_part
+
+        @pl.when(image > 0)
+        def _():
+            parts[which] = parts[which] + in_part
+
+    unused, unit, inverse = row_norm(
+        tokens[0].astype(jnp.float32), norms[0:1, :], norms[2:3, :]
+    )
+    vectors[0:1, :] += jnp.sum(d_normed * unit, axis=0, keepdims=True)
+    vectors[2:3, :] += jnp.sum(d_normed, axis=0, keepdims=True)
+    input_grad[0] = d_sum[...] + row_norm_back(d_normed, unit, inverse, norms[0:1, :])
+
+    @pl.when(last)
+    def _():
+        slab = mine.shape[2]
+        for which in range(4):
+            for side in range(2):
+                own = pl.ds(pl.multiple_of((2 * side + core) * slab, slab), slab)
+                other = pl.ds(pl.multiple_of((2 * side + 1 - core) * slab, slab), slab)
+                mine[which, side] = parts[which, own, :].astype(low)
+                theirs[which, side] = parts[which, other, :].astype(low)
+
+
+def attention_backward(place, tokens, cots, residual, blended, normed, qkv, seconds, weights, norms):
+    images, rows, features = tokens.shape
+    low = jnp.bfloat16
+    image = pl.BlockSpec((1, rows, features), lambda i, place: (i, 0, 0))
+    half_shape = jax.ShapeDtypeStruct((4, 2, features // 4, features), low)
+    half = pl.BlockSpec(half_shape.shape, lambda i, place: (0, 0, 0, 0))
+    return pl.pallas_call(
+        backward_kernel,
+        grid_spec=pltpu.PrefetchScalarGridSpec(
+            num_scalar_prefetch=1,
+            grid=(images,),
+            in_specs=[
+                image,
+                image,
+                image,
+                image,
+                image,
+                pl.BlockSpec((1, 3, rows, features), lambda i, place: (i, 0, 0, 0)),
+                pl.BlockSpec(weights.shape, lambda i, place: (0, 0, 0)),
+                pl.BlockSpec(norms.shape, lambda i, place: (0, 0)),
+            ]
+            + [image] * 4,
+            out_specs=[
+                image,
+                half,
+                half,
+                pl.BlockSpec((8, features), lambda i, place: (0, 0)),
+            ],
+            scratch_shapes=[
+                pltpu.VMEM((4, features, features), jnp.float32),
+                pltpu.VMEM((rows, features), low),
+                pltpu.VMEM((3, rows, features), low),
+                pltpu.VMEM((rows, features), jnp.float32),
+            ],
+        ),
+        out_shape=[
+            jax.ShapeDtypeStruct((images, rows, features), jnp.float32),
+            half_shape,
+            half_shape,
+            jax.ShapeDtypeStruct((8, features), jnp.float32),
+        ],
+        compiler_params=pltpu.CompilerParams(vmem_limit_bytes=VMEM_ASK),
+        cost_estimate=pl.CostEstimate(
+            flops=40 * images * rows * features * features,
+            bytes_accessed=24 * 1024 * 1024,
+            transcendentals=0,
+        ),
+        name="attention_backward",
+    )(place, tokens, cots, residual, blended, normed, qkv, weights, norms, *seconds)
+
+
+def route_to(place):
+    shards, ctxs, tps = (lax.axis_size(name) for name in axes)
+    pairs = []
+    for shard in range(shards):
+        for ctx in range(ctxs):
+            for tp in range(tps):
+                other_shard, other_ctx, other_tp = place(shard, ctx, tp)
+                pairs.append(
+                    (
+                        (shard * ctxs + ctx) * tps + tp,
+                        (other_shard * ctxs + other_ctx) * tps + other_tp % tps,
+                    )
+                )
+    return pairs
+
+
+def swap_core(value):
+    return lax.ppermute(value, axes, route_to(lambda s, c, t: (s ^ 1, c, t)))
+
+
+def swap_chip(value, turn):
+    return lax.ppermute(
+        value, axes, route_to(lambda s, c, t: (s ^ (turn & 2), c ^ (turn & 1), t))
+    )
+
+
+def swap_tp(value, turn):
+    return lax.ppermute(value, axes, route_to(lambda s, c, t: (s, c, t ^ turn)))
+
+
+def pass_on(value):
+    return lax.ppermute(value, axes, route_to(lambda s, c, t: (s, c, t + 1)))
+
+
+def worker_route(source, target):
+    shards, ctxs, tps = (lax.axis_size(name) for name in axes)
+    pairs = []
+    for shard in range(shards):
+        for ctx in range(ctxs):
+            for worker in range(tps):
+                if worker // 2 == shard % 2:
+                    base = (shard * ctxs + ctx) * tps
+                    pairs.append((base + source(worker) % tps, base + target(worker) % tps))
+    return pairs
+
+
+def to_worker(value, turn):
+    return lax.ppermute(value, axes, worker_route(lambda w: w + turn, lambda w: w))
+
+
+def from_worker(value, turn):
+    step = 1 if turn > 0 else -1
+    return lax.ppermute(
+        value, axes, worker_route(lambda w: w + turn - step, lambda w: w + turn)
+    )
+
+
+def pick(value, index, axis=0):
+    return lax.dynamic_index_in_dim(value, index, axis, keepdims=False)
+
+
+def relative(value, chip):
+    return [pick(value, jnp.bitwise_xor(chip, turn)) for turn in range(4)]
+
+
+def pass_by(value, steps):
+    return lax.ppermute(value, axes, route_to(lambda s, c, t: (s, c, t + steps)))
+
+
+def direct_gather(value):
+    return [value] + [pass_by(value, steps) for steps in range(1, lax.axis_size("tp"))]
+
+
+class Live:
+    def __init__(self, values=None):
+        vars(self).update(values or {})
+
+    @property
+    def drop(self):
+        return Drop(vars(self))
+
+
+class Drop:
+    def __init__(self, values):
+        self._values = values
+
+    def __getattr__(self, name):
+        return self._values.pop(name)
+
+
+def hold(live):
+    return Live(lax.optimization_barrier(vars(live)))
+
+
+def by_tp(held, tp):
+    count = len(held)
+    stacked = jnp.stack(held)
+    return jnp.stack([pick(stacked, (tp - place) % count) for place in range(count)])
+
+
+def place_chips(pieces, chip):
+    stacked = jnp.stack(pieces)
+    return jnp.stack([pick(stacked, jnp.bitwise_xor(chip, place)) for place in range(4)])
+
+
+def place_cores(own, other, core):
+    return jnp.where(core == 0, jnp.stack([own, other]), jnp.stack([other, own]))
+
+
+def low_dot(spec, left, right):
+    return jnp.einsum(
+        spec,
+        left.astype(jnp.bfloat16),
+        right.astype(jnp.bfloat16),
+        preferred_element_type=jnp.float32,
+    )
+
+
+def plane_device(
+    tokens,
+    cotangent,
+    routing,
+    gating,
+    inward,
+    outward,
+    scales,
+    shifts,
+    upward,
+    downward,
+    inward_moment,
+    outward_moment,
+    scales_moment,
+    shifts_moment,
+    upward_moment,
+    downward_moment,
+):
+    rows_here = tokens.shape[1]
+    features = tokens.shape[2]
+    seqs = rows_here // LEN
+    experts = upward.shape[0]
+    half_experts = experts // 2
+    shard = lax.axis_index("shard")
+    core = shard % 2
+    ctx = lax.axis_index("ctx")
+    tp = lax.axis_index("tp")
+    tps = lax.axis_size("tp")
+    devices = lax.axis_size(axes)
+    chip = (shard // 2) * 2 + ctx
+    low = jnp.bfloat16
+    rows_attn = inward.shape[1]
+    rows_local = upward.shape[1]
+    cols_local = upward.shape[2]
+
+    v = Live()
+    place = jnp.stack([chip, core, tp]).astype(jnp.int32)
+    y_here, x_here = shard // 2, ctx
+    padded = seqs * IMAGE
+    half = tps // 2
+    own_tokens, own_cot = (
+        jnp.pad(value[0].reshape(seqs, LEN, features), ((0, 0), (0, IMAGE - LEN), (0, 0)))
+        for value in (tokens, cotangent)
+    )
+
+    def halves(value):
+        value = value.astype(low).reshape(2, half_experts, rows_local, cols_local)
+        return pick(value, core), pick(value, 1 - core)
+
+    def own_order(value):
+        return jnp.stack([pick(value, jnp.bitwise_xor(chip, r)) for r in range(4)])
+
+    up_kept, up_sent = halves(upward)
+    down_kept, down_sent = halves(downward)
+    v.up, v.down = [own_order(up_kept)], [own_order(down_kept)]
+    v.up_x, v.down_y = [swap_chip(v.up[0], 1)], [swap_chip(v.down[0], 2)]
+    v.column = direct_gather(jnp.concatenate([inward, outward[None]]))
+    v.sent = jnp.stack([up_sent, down_sent])
+    v.cots = [own_cot.reshape(padded, features)]
+
+    packed = jnp.concatenate([routing[0].astype(jnp.float32).T, gating[0].T])
+    packed = jnp.pad(
+        packed.reshape(4, seqs, LEN), ((0, 0), (0, 0), (0, IMAGE - LEN)), constant_values=-1.0
+    )
+    norm_rows = jnp.concatenate([scales, shifts]).astype(jnp.float32)
+    packed = jnp.concatenate(
+        [packed.reshape(4, padded), jnp.pad(norm_rows, ((0, 0), (0, padded - rows_attn)))]
+    )
+    v.packs = direct_gather(packed)
+    v = hold(v)
+
+    column = by_tp(v.drop.column, tp).transpose(1, 0, 2, 3)
+    column = column.reshape(4, tps * rows_attn, features)
+    v.pieces = [column, swap_chip(column, 1), swap_chip(column, 2)]
+    v.cots.append(pass_on(v.cots[-1]))
+    v.got = swap_core(v.drop.sent)
+    packs = jnp.stack(v.packs)
+    v.packs = [packs, swap_core(packs)]
+    v = hold(v)
+
+    column, from_x, from_y = v.pieces
+    v.far = [swap_chip(from_x[:2], 2), swap_chip(from_y[2:], 1)]
+    v.others = [swap_core(jnp.stack(v.pieces[:2]))]
+    got = v.drop.got
+    v.up.append(own_order(got[0]))
+    v.down.append(own_order(got[1]))
+    own_packs, other_packs = v.drop.packs
+    norms = [by_tp(list(each[:, 4:, :rows_attn]), tp) for each in (own_packs, other_packs)]
+    norms = place_cores(*norms, core)
+    v.norms = [norms, swap_chip(norms, 1)]
+    packs = jnp.concatenate([own_packs, other_packs])
+    mine = core * half_experts + jnp.bitwise_xor(chip, jnp.arange(4, dtype=jnp.int32))
+    hits = packs[None, :, :2] == mine.astype(jnp.float32)[:, None, None, None]
+    chosen = jnp.any(hits, axis=2)
+    gate_tok = jnp.sum(jnp.where(hits, packs[None, :, 2:4], 0.0), axis=2)
+    places = jnp.arange(padded)
+    earlier = (places[:, None] < places[None, :]).astype(low)
+    rank = jnp.einsum(
+        "rbt,tu->rbu", chosen.astype(low), earlier, preferred_element_type=jnp.float32
+    )
+    rank = jnp.where(chosen, rank, -1.0).astype(jnp.int32)
+    counts = jnp.sum(chosen.astype(jnp.int32), axis=2)
+    counts = (counts + 15) // 16 * 16
+    starts = jnp.cumsum(jnp.pad(counts, ((0, 0), (1, 0))), axis=1).astype(jnp.int32).reshape(-1)
+    v.routes = (jnp.concatenate([starts, place[:2]]), rank, gate_tok)
+    v = hold(v)
+    far = jnp.concatenate(v.drop.far)
+    v.pieces = v.pieces + [far]
+    v.others.append(swap_core(jnp.stack(v.pieces[2:])))
+    v.cots.append(pass_on(v.cots[-1]))
+    v.up_x.append(swap_chip(v.up[1], 1))
+    v.down_y.append(swap_chip(v.down[1], 2))
+    norms = place_cores(*v.norms, ctx)
+    v.norms = [norms, swap_chip(norms, 2)]
+    v = hold(v)
+    norms = place_cores(*v.drop.norms, y_here)
+    norms = norms.transpose(4, 0, 2, 1, 3, 5).reshape(4, features)
+
+    normed, qkv, blended, residual, second, full_weights = attention_forward(
+        place, own_tokens, norms, v.drop.pieces, v.drop.others
+    )
+    v.seconds = [second.reshape(padded, features)]
+    v.up_xy, v.down_xy = [swap_chip(v.up_x[0], 2)], [swap_chip(v.down_y[0], 1)]
+    v.cots.append(pass_on(v.cots[-1]))
+    v.cots_other = [swap_core(each) for each in v.cots[:2]]
+    v = hold(v)
+
+    v.seconds.append(pass_on(v.seconds[-1]))
+    v.up_xy.append(swap_chip(v.up_x[1], 2))
+    v.down_xy.append(swap_chip(v.down_y[1], 1))
+    v.cots_other += [swap_core(each) for each in v.cots[2:]]
+    v = hold(v)
+    v.seconds.append(pass_on(v.seconds[-1]))
+    v.down_x, v.up_y = [swap_chip(v.down[0], 1)], [swap_chip(v.up[0], 2)]
+    v.seconds_other = [swap_core(v.seconds[0])]
+    moments = halves(upward_moment) + halves(downward_moment)
+    v.moments = moments[0], moments[2], swap_core(jnp.stack([moments[1], moments[3]]))
+    v = hold(v)
+    v.seconds.append(pass_on(v.seconds[-1]))
+    v.down_x.append(swap_chip(v.down[1], 1))
+    v.up_y.append(swap_chip(v.up[1], 2))
+    v.seconds_other += [swap_core(each) for each in v.seconds[1:3]]
+    moments = v.drop.moments
+    moments = jnp.stack([moments[0], moments[2][0], moments[1], moments[2][1]])
+    v.moments = [pick(moments, jnp.bitwise_xor(chip, turn), 1) for turn in range(4)]
+    v = hold(v)
+    v.seconds_other.append(swap_core(v.seconds[3]))
+    v = hold(v)
+
+    ups = v.drop.up + v.drop.up_x + v.drop.up_y + v.drop.up_xy
+    downs = v.drop.down + v.drop.down_x + v.drop.down_y + v.drop.down_xy
+    v.moments = [v.moments[0]] + [swap_chip(v.moments[turn], turn) for turn in range(1, 4)]
+    hidden, before, v.own, v.near_x, v.near_y, v.far_x, v.far_y = experts_pass(
+        *v.routes,
+        v.drop.seconds + v.drop.seconds_other,
+        v.drop.cots + v.drop.cots_other,
+        ups, downs,
+    )
+    v.hidden, v.before = hidden, before
+    v.ups, v.downs = ups, downs
+    v = hold(v)
+
+    v.part = tokens_pass(*v.routes, v.drop.before, v.drop.ups, False)
+    v.far_x, v.far_y = swap_chip(v.far_x, 1), swap_chip(v.far_y, 2)
+    v = hold(v)
+
+    def join(own, other):
+        return (own.astype(jnp.float32) + other.astype(jnp.float32)).astype(low)
+
+    v.along_x = v.near_x.at[1].set(join(v.near_x[1], v.drop.far_y))
+    v.along_y = v.near_y.at[0].set(join(v.near_y[0], v.drop.far_x))
+    v.near_x = v.near_y = None
+    v.part = [v.part[0], swap_core(v.part[1])]
+    v = hold(v)
+    kept = join(*v.drop.part)
+    v.along_x, v.along_y = swap_chip(v.along_x, 1), swap_chip(v.along_y, 2)
+    v.seconds = [kept[0]] + [pass_by(kept[turn], -turn) for turn in range(1, tps)]
+    v.mixed = tokens_pass(*v.drop.routes, v.drop.hidden, v.drop.downs, True)
+    v = hold(v)
+
+    *pushes, rows0, rows1, rows2, rows3 = push_rows(
+        place, v.drop.own, (v.drop.along_x, v.drop.along_y), v.drop.moments
+    )
+    v.push, v.rows = pushes, [rows0, rows1, rows2, rows3]
+    v = hold(v)
+
+    def rows_out(rows):
+        return [rows[0]] + [swap_chip(rows[turn], turn) for turn in range(1, 4)]
+
+    def rows_between(got):
+        got = place_chips(got, chip)
+        return pick(got, core, 2), swap_core(pick(got, 1 - core, 2))
+
+    def rows_in(kept, got):
+        joined = place_cores(kept, got, core).transpose(2, 0, 1, 3, 4)
+        joined = joined.reshape(2, experts, rows_local, cols_local)
+        return joined.astype(jnp.float32)
+
+    v.joined = [v.push[0]] + [to_worker(v.push[1], turn) for turn in (1, 3)]
+    v.block = v.push[0]
+    v.rows = rows_out(v.rows)
+    v.input_grad, v.own, v.gone, v.vectors = attention_backward(
+        place, own_tokens, own_cot, residual, blended, normed, qkv,
+        [each.reshape(seqs, IMAGE, features) for each in v.drop.seconds],
+        full_weights, norms,
+    )
+    v = hold(v)
+
+    def added(value, got):
+        return value.astype(jnp.float32) + got.astype(jnp.float32)
+
+    third = features // 3
+    v.gone = swap_core(v.gone)
+    v.blocks = [to_worker(v.block[:third], 2)]
+    v.rows = rows_between(v.rows)
+    v = hold(v)
+    sums = added(v.drop.own, v.drop.gone).reshape(4, 2, 2, tps, rows_attn, features)
+    first, last = sums[:, :, :, :half], sums[:, :, :, half:]
+    v.first = [pick(first, x_here, 2), swap_chip(pick(first, 1 - x_here, 2).astype(low), 1)]
+    v.last = [pick(last, y_here, 1), swap_chip(pick(last, 1 - y_here, 1).astype(low), 2)]
+    v.blocks.append(to_worker(v.block[third : 2 * third], 2))
+    v = hold(v)
+    first, last = added(*v.first), added(*v.last)
+    v.first = [pick(first, y_here, 1), swap_chip(pick(first, 1 - y_here, 1).astype(low), 2)]
+    v.last = [pick(last, x_here, 1), swap_chip(pick(last, 1 - x_here, 1).astype(low), 1)]
+    v.blocks.append(to_worker(v.drop.block[2 * third :], 2))
+    v.mixed = [v.mixed[0], swap_core(v.mixed[1])]
+    v = hold(v)
+
+    sums = jnp.concatenate([added(*v.drop.first), added(*v.drop.last)], axis=1)
+    parts = [pick(sums, (tp - turn) % tps, 1) for turn in range(tps)]
+    v.sums = [parts[0]] + [
+        pass_by(parts[turn].astype(low), -turn) for turn in range(1, tps)
+    ]
+    mixed = added(*v.mixed)
+    v.mixed = [mixed, pass_on(mixed[1].astype(low))]
+    v.mixers = wide_first(v.drop.joined + v.drop.blocks)
+    vectors = v.vectors[:4]
+    v.vectors = [vectors, swap_core(vectors)]
+    v = hold(v)
+    sums = sum(part.astype(jnp.float32) for part in v.drop.sums)
+    inward_grad, outward_grad = sums[:3], sums[3]
+    inward_state, inward_push = advance(inward_grad, inward_moment)
+    outward_state, outward_push = advance(outward_grad, outward_moment)
+    v.column = direct_gather(jnp.concatenate([inward_push, outward_push[None]]).astype(low))
+    v.mixers = [wide_last(*v.mixers)]
+    mixed, got = v.mixed
+    v.mixed = [mixed, pass_on(added(mixed[2], got).astype(low))]
+    vectors = sum(v.vectors)
+    v.vectors = [vectors, swap_chip(vectors, 1)]
+    v = hold(v)
+    column = by_tp(v.drop.column, tp).transpose(1, 0, 2, 3)
+    gone = relative(column, chip)
+    v.pushes = [gone[0]] + [swap_chip(gone[turn], turn) for turn in range(1, 4)]
+    v.mixers.append(from_worker(v.mixers[0], 1))
+    v.mixers.append(from_worker(v.mixers[0], -1))
+    v = hold(v)
+    pushes = place_chips(v.pushes, chip)
+    v.pushes = [pushes, swap_core(pushes)]
+    v.mixers.insert(2, from_worker(v.mixers[1], 2))
+    vectors = sum(v.vectors)
+    v.vectors = [vectors, swap_chip(vectors, 2)]
+    v.input_grad = v.input_grad[:, :LEN].reshape(rows_here, features)
+    upward_grad, downward_grad = rows_in(*v.drop.rows)
+    v.states = [
+        (upward_grad, advance(upward_grad, upward_moment)[0]),
+        (downward_grad, advance(downward_grad, downward_moment)[0]),
+    ]
+    v = hold(v)
+    pushes = place_cores(*v.drop.pushes, core)
+    pushes = pushes.reshape(2, 2, 2, tps, rows_attn, features).transpose(1, 0, 2, 3, 4, 5)
+    v.pushes = pushes.reshape(features, features)
+    vectors = sum(v.vectors)
+    v.vectors = [vectors, swap_tp(vectors, 1)]
+    v.new = apply_mixers(place, v.drop.mixers, v.drop.push, rows_local)
+    v = hold(v)
+
+    v.new = rows_out(v.new)
+    mixed, got = v.mixed
+    v.mixed = [mixed, pass_on(added(mixed[3], got).astype(low))]
+    vectors = sum(v.vectors)
+    v.vectors = [vectors, swap_tp(vectors, 2)]
+    v.moved = orthogonal_square(v.drop.pushes)
+    v = hold(v)
+    moved = v.drop.moved.reshape(2, 2, 2, tps, rows_attn, features)
+    moved = pick(pick(moved, core, 1), tp, 2).reshape(4, rows_attn, features)
+    gone = relative(moved, chip)
+    v.moved = [gone[0]] + [swap_chip(gone[turn], turn) for turn in range(1, 4)]
+    v.new = rows_between(v.new)
+    mixed, got = v.drop.mixed
+    result = (residual.reshape(padded, features) + added(mixed[0], got)).astype(low)
+    v.result = result.reshape(seqs, IMAGE, features)[:, :LEN].reshape(rows_here, features)
+    vectors = lax.dynamic_slice(
+        sum(v.drop.vectors), (0, lax.axis_index(axes) * rows_attn), (4, rows_attn)
+    )
+    v = hold(v)
+    result, input_grad = v.result, v.input_grad
+    scales_grad, shifts_grad = vectors[:2], vectors[2:]
+    scales_state, scales_push = advance(scales_grad, scales_moment)
+    shifts_state, shifts_push = advance(shifts_grad, shifts_moment)
+    up_new, down_new = rows_in(*v.new)
+    upward_new = upward.astype(jnp.float32) - 2.0 * up_new
+    downward_new = downward.astype(jnp.float32) - down_new
+    (upward_grad, upward_state), (downward_grad, downward_state) = v.states
+    got = place_chips(v.moved, chip).astype(jnp.float32)
+    inward_new = inward.astype(jnp.float32) - got[:3]
+    outward_new = outward.astype(jnp.float32) - got[3]
+    vector_rate = 0.6 / math.sqrt(devices * rows_here)
+    scales_new = scales.astype(jnp.float32) - vector_rate * scales_push
+    shifts_new = shifts.astype(jnp.float32) - vector_rate * shifts_push
+    return (
+        result[None],
+        input_grad[None],
+        inward_grad,
+        outward_grad,
+        scales_grad,
+        shifts_grad,
+        upward_grad,
+        downward_grad,
+        inward_state,
+        outward_state,
+        scales_state,
+        shifts_state,
+        upward_state,
+        downward_state,
+        inward_new,
+        outward_new,
+        scales_new,
+        shifts_new,
+        upward_new,
+        downward_new,
+    )
+
+
 def solution(mesh):
     in_specs = (
         P(("shard", "tp"), "ctx", None),
@@ -400,6 +1642,7 @@
         P(None, ("shard", "ctx"), "tp"),
         P(None, ("shard", "ctx"), "tp"),
     )
+    body = plane_device if mesh.shape["shard"] == 4 and mesh.shape["ctx"] == 2 and mesh.shape["tp"] == 4 else on_device
     return jax.shard_map(
-        on_device, mesh=mesh, in_specs=in_specs, out_specs=out_specs, check_vma=False
-    )
+        body, mesh=mesh, in_specs=in_specs, out_specs=out_specs, check_vma=False
+    )

time: 2330 us -> 590 us (0.25)
  waiting for transfers between devices: 1090 us -> 169 us
  matrix products: 429 us -> 0.81 us
  local copies, waits for them, and re-layouts: 343 us -> 35.1 us
  blocking collectives: 282 us -> 0 us
  Pallas kernels: 0 us -> 213 us
  other arithmetic: 133 us -> 49.9 us
  starting transfers between devices: 32.6 us -> 110 us
    dot_general x33 -> x1, matrix products: 429 us -> 0.81 us  [plane_device(): jnp.einsum('rbt,tu->rbu', chosen.astype(low), earlier, preferred_element_...]
    reduce_scatter x5 -> x0, waiting for transfers between devices: 361 us -> none  [the longest x1 149 us: on_device(): lax.psum_scatter(partial_out.astype(jnp.bfloat16), 'tp', scatter_dimensio...]
    all_gather x6 -> x0, waiting for transfers between devices: 356 us -> none  [the longest x1 151 us: on_device(): group_grad = lax.all_gather(slot_grad, 'tp', axis=1, tiled=True)]
    pallas_call x0 -> x10, Pallas kernels: none -> 213 us  [the longest x1 55.1 us: experts_pass(): pl.pallas_call(experts_kernel, grid_spec=pltpu.PrefetchScalarGridSpec(num...]
    unnamed x13 -> x0, waiting for transfers between devices: 197 us -> none
    all_to_all x5 -> x0, waiting for transfers between devices: 176 us -> none  [the longest x1 102 us: on_device(): lax.all_to_all(outgoing.astype(jnp.bfloat16), ('shard', 'ctx', 'tp'), spl...]
    ppermute x0 -> x97, waiting for transfers between devices: none -> 169 us  [the longest x43 91 us: swap_chip(): lax.ppermute(value, axes, route_to(lambda s, c, t: (s ^ turn & 2, c ^ tur...]
    all_gather x2 -> x0, blocking collectives: 133 us -> none  [the longest x1 69.5 us: on_device(): lax.all_gather(scales, ('shard', 'ctx', 'tp'), axis=1, tiled=True)]
  transfers between devices with their start and end apart: 17 -> 97, of which waited for: 12 -> 33; matrix products, arithmetic and copies ran while one was open for 13% -> 9% of each run, Pallas kernels for 0% -> 35%
where the time goes in v1:
time: 590 us; the launch traced here: 581 us
  Pallas kernels  213 us (36%)
  waiting for transfers between devices  169 us (29%)
  starting transfers between devices  110 us (19%)
  other arithmetic  49.9 us (8%)
  local copies, waits for them, and re-layouts  35.1 us (6%)
    ppermute x43, waiting for transfers between devices, swap_chip(): lax.ppermute(value, axes, route_to(lambda s, c, t: (s ^ turn & 2, c ^ tur...  91 us
    pallas_call x1, Pallas kernels, experts_pass(): pl.pallas_call(experts_kernel, grid_spec=pltpu.PrefetchScalarGridSpec(num...  55.1 us
    pallas_call x2, Pallas kernels, tokens_pass(): pl.pallas_call(functools.partial(tokens_kernel, gated), grid_spec=pltpu.P...  49.9 us
    ppermute x43, starting transfers between devices, swap_chip(): lax.ppermute(value, axes, route_to(lambda s, c, t: (s ^ turn & 2, c ^ tur...  46.7 us
    ppermute x15, waiting for transfers between devices, pass_by(): lax.ppermute(value, axes, route_to(lambda s, c, t: (s, c, t + steps)))  38.8 us
    pallas_call x1, Pallas kernels, attention_backward(): pl.pallas_call(backward_kernel, grid_spec=pltpu.PrefetchScalarGridSpec(nu...  31.6 us
    pallas_call x2, Pallas kernels, wide_call(): pl.pallas_call(kernel, out_shape=out_shape, in_specs=[vmem] * len(inputs)...  30 us
    ppermute x5, waiting for transfers between devices, to_worker(): lax.ppermute(value, axes, worker_route(lambda w: w + turn, lambda w: w))  22.6 us
  transfers between devices with their start and end apart: 97, of which 33 were waited for; matrix products, arithmetic and copies ran while one was open for 9% of the time, Pallas kernels for 35%

profile of v1, /device:TPU:0, one launch (start us, length us, event | category | flops | bytes accessed | tf_op | source)
XLA Modules:
  0.0 580.6 jit_solution(16196274015051141963)
XLA Ops:
  3.3 2.9 collective-permute-start.7
  10.5 2.6 collective-permute-start.5
  18.5 2.3 collective-permute-start.2
  24.1 3.8 collective-permute-done.1
  28.1 3.1 collective-permute-start.8
  35.1 12.9 %collective-permute-done.11.w1 = bf16[4,96,768]{2,1,0:T(8,128)(2,1)S(1)} collective-permute-done((bf16[4,96,768]{2,1,0:T(8,128)(2,1)S(1)}, bf16[4,96,768]{2,1,0:T(8,128)(2,1)S(1)}, u32[]{:S(2)}, u32[]{:S(2)}) %collective-permute-start.11) | collective-permute-done | bytes 589856 | tf_op jit(solution)/shard_map/ppermute | solution.py:1173
  55.7 4.2 collective-permute-done.13
  64.6 13.4 %collective-permute-done.19 = f32[2,2,4,4,24]{4,3,2,1,0:T(4,128)S(1)} collective-permute-done((f32[2,2,4,4,24]{4,3,2,1,0:T(4,128)S(1)}, f32[2,2,4,4,24]{4,3,2,1,0:T(4,128)S(1)}, u32[]{:S(2)}, u32[]{:S(2)}) %collective-permute-start.19) | collective-permute-done | bytes 6176 | tf_op jit(solution)/shard_map/ppermute | solution.py:1173
  85.4 12.9 %attention_forward.1 = (bf16[2,208,768]{2,1,0:T(8,128)(2,1)}, bf16[2,3,208,768]{3,2,1,0:T(8,128)(2,1)}, bf16[2,208,768]{2,1,0:T(8,128)(2,1)}, f32[2,208,768]{2,1...) custom-call(s32[3]{0:T(128)} %pad_add_fusion.1.place, bf16[2,208,768]{2,1,0:T(8,128)(2,1)} %pad.28.tokens, ...), custom_call_target="tpu_custom_call" | custom-call | flops 2453667840 | bytes 16777216 | tf_op jit(solution)/shard_map/attention_forward/pallas_call | solution.py:974
  103.8 9.6 %collective-permute-done.29.refs_15_.refs_7_ = bf16[4,96,768]{2,1,0:T(8,128)(2,1)S(1)} collective-permute-done((bf16[4,96,768]{2,1,0:T(8,128)(2,1)}, bf16[4,96,768]{2,1,0:T(8,128)(2,1)S(1)}, u32[]{:S(2)}, u32[]{:S(2)}) %collective-permute-start.29) | collective-permute-done | bytes 589856 | tf_op jit(solution)/shard_map/ppermute | solution.py:1173
  113.4 4.8 collective-permute-done.31.refs_7_
  118.2 2.9 collective-permute-done.30.refs_17_
  123.2 13.9 %collective-permute-done.32.refs_10_.refs_2_ = bf16[4,96,768]{2,1,0:T(8,128)(2,1)S(1)} collective-permute-done((bf16[4,96,768]{2,1,0:T(8,128)(2,1)}, bf16[4,96,768]{2,1,0:T(8,128)(2,1)S(1)}, u32[]{:S(2)}, u32[]{:S(2)}) %collective-permute-start.32) | collective-permute-done | bytes 589856 | tf_op jit(solution)/shard_map/ppermute | solution.py:1173
  144.3 11.4 %collective-permute-done.37.refs_11_.refs_3_ = bf16[4,96,768]{2,1,0:T(8,128)(2,1)S(1)} collective-permute-done((bf16[4,96,768]{2,1,0:T(8,128)(2,1)S(1)}, bf16[4,96,768]{2,1,0:T(8,128)(2,1)S(1)}, u32[]{:S(2)}, u32[]{:S(2)}) %collective-permute-start.37) | collective-permute-done | bytes 589856 | tf_op jit(solution)/shard_map/ppermute | solution.py:1173
  157.0 2.1 collective-permute-done.42.refs_23_
  160.3 2.4 collective-permute-start.45
  162.6 55.1 %experts_pass.1 = (bf16[4,1792,768]{2,1,0:T(8,128)(2,1)}, bf16[4,1792,768]{2,1,0:T(8,128)(2,1)}, bf16[2,768,768]{2,1,0:T(8,128)(2,1)}, bf16[2,768,768]{2,1,0:T(8...) custom-call(s32[38]{0:T(128)} %pad_add_fusion.starts, ...), custom_call_target="tpu_custom_call" | custom-call | flops 15703474176 | bytes 62914560 | tf_op jit(solution)/shard_map/experts_pass/pallas_call | solution.py:829
  219.3 23.6 %tokens_plain.1 = (bf16[4,416,768]{2,1,0:T(8,128)(2,1)}, bf16[4,416,768]{2,1,0:T(8,128)(2,1)}) custom-call(s32[38]{0:T(128)} %pad_add_fusion.starts, s32[4,8,416]{2,1,0:T(8,128)} %fusion.10.rank, f32[4,8,416]{2,1,0:T(8,128)} %fusion.29.gate, bf16[4,1792,768]{2,1,0:T(8,128)(2,1)} %get-tuple-element.816.acts, bf16[4,96,768]{2,1,0:T(8,128)(2,1)} %pad_maximum_fusion.10.refs_0_, ...), custom_call_target="tpu_custom_call" | custom-call | flops 7851737088 | bytes 31457280 | tf_op jit(solution)/shard_map/tokens_plain/pallas_call | solution.py:872
  247.1 2.8 fusion.7
  258.7 26.3 %tokens_gated.1 = (bf16[4,416,768]{2,1,0:T(8,128)(2,1)}, bf16[4,416,768]{2,1,0:T(8,128)(2,1)}) custom-call(s32[38]{0:T(128)} %pad_add_fusion.starts, s32[4,8,416]{2,1,0:T(8,128)} %fusion.10.rank, f32[4,8,416]{2,1,0:T(8,128)} %fusion.29.gate, bf16[4,1792,768]{2,1,0:T(8,128)(2,1)} %get-tuple-element.855.acts, ...), custom_call_target="tpu_custom_call" | custom-call | flops 7851737088 | bytes 31457280 | tf_op jit(solution)/shard_map/tokens_gated/pallas_call | solution.py:872
  284.9 27.6 %collective-permute-done.52 = bf16[416,768]{1,0:T(8,128)(2,1)} collective-permute-done((bf16[416,768]{1,0:T(8,128)(2,1)}, bf16[416,768]{1,0:T(8,128)(2,1)}, u32[]{:S(2)}, u32[]{:S(2)}) %collective-permute-start.52) | collective-permute-done | bytes 639008 | tf_op jit(solution)/shard_map/ppermute | solution.py:1218
  312.5 8.7 %push_rows.1 = (bf16[768,768]{1,0:T(8,128)(2,1)}, bf16[768,768]{1,0:T(8,128)(2,1)}, bf16[2,2,96,768]{3,2,1,0:T(8,128)(2,1)}, bf16[2,2,96,768]{3,2,1,0:T(8,128)(2...) custom-call(s32[3]{0:T(128)} %pad_add_fusion.1.place, ...), custom_call_target="tpu_custom_call" | custom-call | flops 11796480 | bytes 14155776 | tf_op jit(solution)/shard_map/push_rows/pallas_call | solution.py:575
  322.5 4.6 collective-permute-start.55
  328.5 2.1 collective-permute-start.58
  330.6 31.6 %attention_backward.1 = (f32[2,208,768]{2,1,0:T(8,128)}, bf16[4,2,192,768]{3,2,1,0:T(8,128)(2,1)}, bf16[4,2,192,768]{3,2,1,0:T(8,128)(2,1)}, f32[8,768]{1,0:T(8,128)}) custom-call(s32[3]{0:T(128)} %pad_add_fusion.1.place, bf16[2,208,768]{2,1,0:T(8,128)(2,1)} %pad.28.tokens, bf16[2,208,768]{2,1,0:T(8,128)(2,1)} %pad.24.cots, ...), custom_call_target="tpu_custom_call" | custom-call | flops 9814671360 | bytes 25165824 | tf_op jit(solution)/shard_map/attention_backward/pallas_call | solution.py:1107
  369.7 12.8 %collective-permute-done.59.part0 = bf16[256,768]{1,0:T(8,128)(2,1)} collective-permute-done((bf16[256,768]{1,0:T(8,128)(2,1)}, bf16[256,768]{1,0:T(8,128)(2,1)}, u32[]{:S(2)}, u32[]{:S(2)}) %collective-permute-start.59) | collective-permute-done | bytes 393248 | tf_op jit(solution)/shard_map/ppermute | solution.py:1199
  382.5 3.3 convert_add_fusion.1
  394.4 7.5 %collective-permute-done.62.part1 = bf16[256,768]{1,0:T(8,128)(2,1)} collective-permute-done((bf16[256,768]{1,0:T(8,128)(2,1)}, bf16[256,768]{1,0:T(8,128)(2,1)}, u32[]{:S(2)}, u32[]{:S(2)}) %collective-permute-start.62) | collective-permute-done | bytes 393248 | tf_op jit(solution)/shard_map/ppermute | solution.py:1199
  408.0 4.7 collective-permute-done.67
  412.7 3.6 collective-permute-done.66
  416.3 2.3 collective-permute-done.65.part2
  422.2 2.3 copy-done
  426.8 16.6 %wide_first.1 = (f32[768,768]{1,0:T(8,128)}, f32[768,768]{1,0:T(8,128)}) custom-call(bf16[768,768]{1,0:T(8,128)(2,1)} %get-tuple-element.1034.block0.refs_4_, bf16[768,768]{1,0:T(8,128)(2,1)} %collective-permute-done.54.block1, bf16[768,768]{1,0:T(8,128)(2,1)} %collective-permute-done.55.block3, bf16[256,768]{1,0:T(8,128)(2,1)} %collective-permute-done.59.part0, ...), custom_call_target="tpu_custom_call" | custom-call | flops 9059696640 | bytes 4718592 | tf_op jit(solution)/shard_map/wide_first/pallas_call | solution.py:456
  443.5 2.6 collective-permute-done.71
  450.7 2.8 collective-permute-start.76
  454.7 2.5 fusion.5
  457.3 13.4 %wide_last.1.refs_0_ = bf16[6,256,256]{2,1,0:T(8,128)(2,1)} custom-call(f32[768,768]{1,0:T(8,128)} %get-tuple-element.989.gram_in, f32[768,768]{1,0:T(8,128)} %get-tuple-element.990.whole_in), custom_call_target="tpu_custom_call" | custom-call | flops 9059696640 | bytes 4718592 | tf_op jit(solution)/shard_map/wide_last/pallas_call | solution.py:456
  470.8 4.7 collective-permute-done.75
  475.5 6.1 %collective-permute-start.79 = (bf16[6,256,256]{2,1,0:T(8,128)(2,1)}, bf16[6,256,256]{2,1,0:T(8,128)(2,1)}, u32[]{:S(2)}, u32[]{:S(2)}) collective-permute-start(bf16[6,256,256]{2,1,0:T(8,128)(2,1)} %wide_last.1.refs_0_), channel_id=1, source_target_pairs={{0,1},{1,2},{4,5},{5,6},{10,11},{11,8},{14,15},{15,12},{16,17},{17... | collective-permute-start | bytes 2359304 | tf_op jit(solution)/shard_map/ppermute | solution.py:1204
  492.0 6.9 %collective-permute-done.80.refs_3_ = bf16[6,256,256]{2,1,0:T(8,128)(2,1)S(1)} collective-permute-done((bf16[6,256,256]{2,1,0:T(8,128)(2,1)}, bf16[6,256,256]{2,1,0:T(8,128)(2,1)S(1)}, u32[]{:S(2)}, u32[]{:S(2)}) %collective-permute-start.80) | collective-permute-done | bytes 786464 | tf_op jit(solution)/shard_map/ppermute | solution.py:1204
  501.1 2.1 collective-permute-start.84
  507.7 4.2 collective-permute-start.87
  511.8 7.0 %apply_mixers.1 = (bf16[2,2,96,768]{3,2,1,0:T(8,128)(2,1)}, bf16[2,2,96,768]{3,2,1,0:T(8,128)(2,1)}, bf16[2,2,96,768]{3,2,1,0:T(8,128)(2,1)}, bf16[2,2,96,768]{3,2,1,0:T(8,128)(2,1)}) custom-call(s32[3]{0:T(128)} %pad_add_fusion.1.place, bf16[6,256,256]{2,1,0:T(8,128)(2,1)} %wide_last.1.refs_0_, bf16[6,256,256]{2,1,0:T(8,128)(2,1)} %collective-permute-done.79.refs_1_, ...), custom_call_target="tpu_custom_call" | custom-call | flops 1811939328 | bytes 5898240 | tf_op jit(solution)/shard_map/apply_mixers/pallas_call | solution.py:524
  518.9 2.5 maximum_select_fusion.2
  521.4 8.5 %collective-permute-start.92 = (f32[4,768]{1,0:T(4,128)S(1)}, f32[4,768]{1,0:T(4,128)S(1)}, u32[]{:S(2)}, u32[]{:S(2)}) collective-permute-start(f32[4,768]{1,0:T(4,128)S(1)} %add.388), channel_id=1, source_target_pairs={{0,2},{1,3},{2,0},{3,1},{4,6},{5,7},{6,4},{7,5},{8,10},{9,11},{10,... | collective-permute-start | bytes 36872 | tf_op jit(solution)/shard_map/ppermute | solution.py:1179
  534.9 18.0 %square_orthogonal.1 = bf16[768,768]{1,0:T(8,128)(2,1)} custom-call(bf16[768,768]{1,0:T(8,128)(2,1)} %bitcast.268), custom_call_target="tpu_custom_call" | custom-call | flops 13589544960 | bytes 2359296 | tf_op jit(solution)/shard_map/square_orthogonal/pallas_call | solution.py:621
  552.9 5.2 collective-permute-done.90
  577.8 2.3 copy.62
  (447 shorter events, 148.3 us)
Async XLA Ops:
  3.3 24.7 %collective-permute-start.7 = (bf16[4,96,768]{2,1,0:T(8,128)(2,1)}, bf16[4,96,768]{2,1,0:T(8,128)(2,1)}, u32[]{:S(2)}, u32[]{:S(2)}) collective-permute-start(bf16[4,96,768]{2,1,0:T(8,128)(2,1)} %pad_maximum_fusion.10.refs_0_), channel_id=1, source_target_pairs={{0,4},{1,5},{2,6},{3,7},{4,0},{5,1},{6,2},{7,3},{8,12},{9,13},{10,... | collective-permute-start | bytes 1769480 | tf_op jit(solution)/shard_map/ppermute | solution.py:1173
  7.1 20.8 %collective-permute-start.3 = (bf16[4,96,768]{2,1,0:T(8,128)(2,1)}, bf16[4,96,768]{2,1,0:T(8,128)(2,1)}, u32[]{:S(2)}, u32[]{:S(2)}) collective-permute-start(bf16[4,96,768]{2,1,0:T(8,128)(2,1)} %pad_maximum_fusion.9.refs_8_.refs_0_), channel_id=1, source_target_pairs={{0,16},{1,17},{2,18},{3,19},{4,20},{5,21},{6,22},{7,23},{8,24},{9,... | collective-permute-start | bytes 1769480 | tf_op jit(solution)/shard_map/ppermute | solution.py:1173
  28.0 20.3 %collective-permute-start.9 = (bf16[2,4,96,768]{3,2,1,0:T(8,128)(2,1)}, bf16[2,4,96,768]{3,2,1,0:T(8,128)(2,1)}, u32[]{:S(2)}, u32[]{:S(2)}) collective-permute-start(bf16[2,4,96,768]{3,2,1,0:T(8,128)(2,1)} %pad_maximum_fusion.5), channel_id=1, source_target_pairs={{0,8},{1,9},{2,10},{3,11},{4,12},{5,13},{6,14},{7,15},{8,0},{9,1},... | collective-permute-start | bytes 3538952 | tf_op jit(solution)/shard_map/ppermute | solution.py:1169
  28.1 20.1 %collective-permute-start.8 = (bf16[416,768]{1,0:T(8,128)(2,1)}, bf16[416,768]{1,0:T(8,128)(2,1)}, u32[]{:S(2)}, u32[]{:S(2)}) collective-permute-start(bf16[416,768]{1,0:T(8,128)(2,1)} %bitcast.1.refs_24_), channel_id=1, source_target_pairs={{0,1},{1,2},{2,3},{3,0},{4,5},{5,6},{6,7},{7,4},{8,9},{9,10},{10,1... | collective-permute-start | bytes 1916936 | tf_op jit(solution)/shard_map/ppermute | solution.py:1183
  61.5 18.9 %collective-permute-start.20 = (bf16[2,4,96,768]{3,2,1,0:T(8,128)(2,1)}, bf16[2,4,96,768]{3,2,1,0:T(8,128)(2,1)}, u32[]{:S(2)}, u32[]{:S(2)}) collective-permute-start(bf16[2,4,96,768]{3,2,1,0:T(8,128)(2,1)} %pad_maximum_fusion.7), channel_id=1, source_target_pairs={{0,8},{1,9},{2,10},{3,11},{4,12},{5,13},{6,14},{7,15},{8,0},{9,1},... | collective-permute-start | bytes 3538952 | tf_op jit(solution)/shard_map/ppermute | solution.py:1169
  61.5 18.9 %collective-permute-start.17 = (bf16[416,768]{1,0:T(8,128)(2,1)}, bf16[416,768]{1,0:T(8,128)(2,1)}, u32[]{:S(2)}, u32[]{:S(2)}) collective-permute-start(bf16[416,768]{1,0:T(8,128)(2,1)} %collective-permute-done.8.refs_25_), channel_id=1, source_target_pairs={{0,1},{1,2},{2,3},{3,0},{4,5},{5,6},{6,7},{7,4},{8,9},{9,10},{10,1... | collective-permute-start | bytes 1916936 | tf_op jit(solution)/shard_map/ppermute | solution.py:1183
  80.5 18.1 %collective-permute-start.22 = (bf16[416,768]{1,0:T(8,128)(2,1)}, bf16[416,768]{1,0:T(8,128)(2,1)}, u32[]{:S(2)}, u32[]{:S(2)}) collective-permute-start(bf16[416,768]{1,0:T(8,128)(2,1)} %collective-permute-done.17.refs_26_), channel_id=1, source_target_pairs={{0,1},{1,2},{2,3},{3,0},{4,5},{5,6},{6,7},{7,4},{8,9},{9,10},{10,1... | collective-permute-start | bytes 1916936 | tf_op jit(solution)/shard_map/ppermute | solution.py:1183
  80.5 18.1 %collective-permute-start.23 = (bf16[416,768]{1,0:T(8,128)(2,1)}, bf16[416,768]{1,0:T(8,128)(2,1)}, u32[]{:S(2)}, u32[]{:S(2)}) collective-permute-start(bf16[416,768]{1,0:T(8,128)(2,1)} %bitcast.1.refs_24_), channel_id=1, source_target_pairs={{0,8},{1,9},{2,10},{3,11},{4,12},{5,13},{6,14},{7,15},{8,0},{9,1},... | collective-permute-start | bytes 1916936 | tf_op jit(solution)/shard_map/ppermute | solution.py:1169
  80.5 18.1 %collective-permute-start.24 = (bf16[416,768]{1,0:T(8,128)(2,1)}, bf16[416,768]{1,0:T(8,128)(2,1)}, u32[]{:S(2)}, u32[]{:S(2)}) collective-permute-start(bf16[416,768]{1,0:T(8,128)(2,1)} %collective-permute-done.8.refs_25_), channel_id=1, source_target_pairs={{0,8},{1,9},{2,10},{3,11},{4,12},{5,13},{6,14},{7,15},{8,0},{9,1},... | collective-permute-start | bytes 1916936 | tf_op jit(solution)/shard_map/ppermute | solution.py:1169
  81.0 17.3 %collective-permute-start.25 = (bf16[4,96,768]{2,1,0:T(8,128)(2,1)}, bf16[4,96,768]{2,1,0:T(8,128)(2,1)}, u32[]{:S(2)}, u32[]{:S(2)}) collective-permute-start(bf16[4,96,768]{2,1,0:T(8,128)(2,1)} %collective-permute-done.3.refs_12_.refs_4_), channel_id=1, source_target_pairs={{0,4},{1,5},{2,6},{3,7},{4,0},{5,1},{6,2},{7,3},{8,12},{9,13},{10,... | collective-permute-start | bytes 1769480 | tf_op jit(solution)/shard_map/ppermute | solution.py:1173
  81.6 16.7 %collective-permute-start.26 = (bf16[4,96,768]{2,1,0:T(8,128)(2,1)}, bf16[4,96,768]{2,1,0:T(8,128)(2,1)}, u32[]{:S(2)}, u32[]{:S(2)}) collective-permute-start(bf16[4,96,768]{2,1,0:T(8,128)(2,1)} %collective-permute-done.7.refs_2_), channel_id=1, source_target_pairs={{0,16},{1,17},{2,18},{3,19},{4,20},{5,21},{6,22},{7,23},{8,24},{9,... | collective-permute-start | bytes 1769480 | tf_op jit(solution)/shard_map/ppermute | solution.py:1173
  102.9 18.1 %collective-permute-start.30 = (bf16[416,768]{1,0:T(8,128)(2,1)S(1)}, bf16[416,768]{1,0:T(8,128)(2,1)S(1)}, u32[]{:S(2)}, u32[]{:S(2)}) collective-permute-start(bf16[416,768]{1,0:T(8,128)(2,1)S(1)} %bitcast.299), channel_id=1, source_target_pairs={{0,1},{1,2},{2,3},{3,0},{4,5},{5,6},{6,7},{7,4},{8,9},{9,10},{10,1... | collective-permute-start | bytes 1916936 | tf_op jit(solution)/shard_map/ppermute | solution.py:1183
  121.1 17.3 %collective-permute-start.34 = (bf16[416,768]{1,0:T(8,128)(2,1)S(1)}, bf16[416,768]{1,0:T(8,128)(2,1)S(1)}, u32[]{:S(2)}, u32[]{:S(2)}) collective-permute-start(bf16[416,768]{1,0:T(8,128)(2,1)S(1)} %collective-permute-done.30.refs_17_), channel_id=1, source_target_pairs={{0,1},{1,2},{2,3},{3,0},{4,5},{5,6},{6,7},{7,4},{8,9},{9,10},{10,1... | collective-permute-start | bytes 1916936 | tf_op jit(solution)/shard_map/ppermute | solution.py:1183
  121.1 17.3 %collective-permute-start.35 = (bf16[416,768]{1,0:T(8,128)(2,1)S(1)}, bf16[416,768]{1,0:T(8,128)(2,1)S(1)}, u32[]{:S(2)}, u32[]{:S(2)}) collective-permute-start(bf16[416,768]{1,0:T(8,128)(2,1)S(1)} %bitcast.300), channel_id=1, source_target_pairs={{0,8},{1,9},{2,10},{3,11},{4,12},{5,13},{6,14},{7,15},{8,0},{9,1},... | collective-permute-start | bytes 1916936 | tf_op jit(solution)/shard_map/ppermute | solution.py:1169
  138.4 18.5 %collective-permute-start.38 = (bf16[416,768]{1,0:T(8,128)(2,1)S(1)}, bf16[416,768]{1,0:T(8,128)(2,1)S(1)}, u32[]{:S(2)}, u32[]{:S(2)}) collective-permute-start(bf16[416,768]{1,0:T(8,128)(2,1)S(1)} %collective-permute-done.34.refs_18_), channel_id=1, source_target_pairs={{0,1},{1,2},{2,3},{3,0},{4,5},{5,6},{6,7},{7,4},{8,9},{9,10},{10,1... | collective-permute-start | bytes 1916936 | tf_op jit(solution)/shard_map/ppermute | solution.py:1183
  140.0 16.9 %collective-permute-start.40 = (bf16[416,768]{1,0:T(8,128)(2,1)S(1)}, bf16[416,768]{1,0:T(8,128)(2,1)S(1)}, u32[]{:S(2)}, u32[]{:S(2)}) collective-permute-start(bf16[416,768]{1,0:T(8,128)(2,1)S(1)} %collective-permute-done.34.refs_18_), channel_id=1, source_target_pairs={{0,8},{1,9},{2,10},{3,11},{4,12},{5,13},{6,14},{7,15},{8,0},{9,1},... | collective-permute-start | bytes 1916936 | tf_op jit(solution)/shard_map/ppermute | solution.py:1169
  140.0 16.9 %collective-permute-start.39 = (bf16[416,768]{1,0:T(8,128)(2,1)S(1)}, bf16[416,768]{1,0:T(8,128)(2,1)S(1)}, u32[]{:S(2)}, u32[]{:S(2)}) collective-permute-start(bf16[416,768]{1,0:T(8,128)(2,1)S(1)} %collective-permute-done.30.refs_17_), channel_id=1, source_target_pairs={{0,8},{1,9},{2,10},{3,11},{4,12},{5,13},{6,14},{7,15},{8,0},{9,1},... | collective-permute-start | bytes 1916936 | tf_op jit(solution)/shard_map/ppermute | solution.py:1169
  159.1 58.7 %collective-permute-start.43 = (bf16[4,96,768]{2,1,0:T(8,128)(2,1)}, bf16[4,96,768]{2,1,0:T(8,128)(2,1)S(1)}, u32[]{:S(2)}, u32[]{:S(2)}) collective-permute-start(bf16[4,96,768]{2,1,0:T(8,128)(2,1)} %get-tuple-element.789), channel_id=1, source_target_pairs={{0,4},{1,5},{2,6},{3,7},{4,0},{5,1},{6,2},{7,3},{8,12},{9,13},{10,... | collective-permute-start | bytes 1769480 | tf_op jit(solution)/shard_map/ppermute | solution.py:1173
  159.7 58.1 %collective-permute-start.44 = (bf16[4,96,768]{2,1,0:T(8,128)(2,1)}, bf16[4,96,768]{2,1,0:T(8,128)(2,1)S(1)}, u32[]{:S(2)}, u32[]{:S(2)}) collective-permute-start(bf16[4,96,768]{2,1,0:T(8,128)(2,1)} %get-tuple-element.790), channel_id=1, source_target_pairs={{0,16},{1,17},{2,18},{3,19},{4,20},{5,21},{6,22},{7,23},{8,24},{9,... | collective-permute-start | bytes 1769480 | tf_op jit(solution)/shard_map/ppermute | solution.py:1173
  160.3 57.5 %collective-permute-start.45 = (bf16[4,96,768]{2,1,0:T(8,128)(2,1)}, bf16[4,96,768]{2,1,0:T(8,128)(2,1)}, u32[]{:S(2)}, u32[]{:S(2)}) collective-permute-start(bf16[4,96,768]{2,1,0:T(8,128)(2,1)} %get-tuple-element.791), channel_id=1, source_target_pairs={{0,20},{1,21},{2,22},{3,23},{4,16},{5,17},{6,18},{7,19},{8,28},{9,... | collective-permute-start | bytes 1769480 | tf_op jit(solution)/shard_map/ppermute | solution.py:1173
  218.8 24.2 %collective-permute-start.46 = (bf16[768,768]{1,0:T(8,128)(2,1)}, bf16[768,768]{1,0:T(8,128)(2,1)S(1)}, u32[]{:S(2)}, u32[]{:S(2)}) collective-permute-start(bf16[768,768]{1,0:T(8,128)(2,1)} %get-tuple-element.803), channel_id=1, source_target_pairs={{0,4},{1,5},{2,6},{3,7},{4,0},{5,1},{6,2},{7,3},{8,12},{9,13},{10,... | collective-permute-start | bytes 3538952 | tf_op jit(solution)/shard_map/ppermute | solution.py:1173
  219.3 23.6 %collective-permute-start.47 = (bf16[768,768]{1,0:T(8,128)(2,1)}, bf16[768,768]{1,0:T(8,128)(2,1)}, u32[]{:S(2)}, u32[]{:S(2)}) collective-permute-start(bf16[768,768]{1,0:T(8,128)(2,1)} %get-tuple-element.804), channel_id=1, source_target_pairs={{0,16},{1,17},{2,18},{3,19},{4,20},{5,21},{6,22},{7,23},{8,24},{9,... | collective-permute-start | bytes 3538952 | tf_op jit(solution)/shard_map/ppermute | solution.py:1173
  249.9 62.7 %collective-permute-start.49 = (bf16[2,768,768]{2,1,0:T(8,128)(2,1)}, bf16[2,768,768]{2,1,0:T(8,128)(2,1)}, u32[]{:S(2)}, u32[]{:S(2)}) collective-permute-start(bf16[2,768,768]{2,1,0:T(8,128)(2,1)} %fusion.7), channel_id=1, source_target_pairs={{0,4},{1,5},{2,6},{3,7},{4,0},{5,1},{6,2},{7,3},{8,12},{9,13},{10,... | collective-permute-start | bytes 7077896 | tf_op jit(solution)/shard_map/ppermute | solution.py:1173
  251.8 60.7 %collective-permute-start.50 = (bf16[2,768,768]{2,1,0:T(8,128)(2,1)}, bf16[2,768,768]{2,1,0:T(8,128)(2,1)}, u32[]{:S(2)}, u32[]{:S(2)}) collective-permute-start(bf16[2,768,768]{2,1,0:T(8,128)(2,1)} %fusion.9), channel_id=1, source_target_pairs={{0,16},{1,17},{2,18},{3,19},{4,20},{5,21},{6,22},{7,23},{8,24},{9,... | collective-permute-start | bytes 7077896 | tf_op jit(solution)/shard_map/ppermute | solution.py:1173
  254.8 30.2 %collective-permute-start.51 = (bf16[416,768]{1,0:T(8,128)(2,1)}, bf16[416,768]{1,0:T(8,128)(2,1)}, u32[]{:S(2)}, u32[]{:S(2)}) collective-permute-start(bf16[416,768]{1,0:T(8,128)(2,1)} %get-tuple-element.1148), channel_id=1, source_target_pairs={{0,3},{1,0},{2,1},{3,2},{4,7},{5,4},{6,5},{7,6},{8,11},{9,8},{10,9... | collective-permute-start | bytes 1916936 | tf_op jit(solution)/shard_map/ppermute | solution.py:1218
  256.2 56.3 %collective-permute-start.52 = (bf16[416,768]{1,0:T(8,128)(2,1)}, bf16[416,768]{1,0:T(8,128)(2,1)}, u32[]{:S(2)}, u32[]{:S(2)}) collective-permute-start(bf16[416,768]{1,0:T(8,128)(2,1)} %get-tuple-element.1147), channel_id=1, source_target_pairs={{0,2},{1,3},{2,0},{3,1},{4,6},{5,7},{6,4},{7,5},{8,10},{9,11},{10,... | collective-permute-start | bytes 1916936 | tf_op jit(solution)/shard_map/ppermute | solution.py:1218
  256.6 55.9 %collective-permute-start.53 = (bf16[416,768]{1,0:T(8,128)(2,1)S(1)}, bf16[416,768]{1,0:T(8,128)(2,1)}, u32[]{:S(2)}, u32[]{:S(2)}) collective-permute-start(bf16[416,768]{1,0:T(8,128)(2,1)S(1)} %get-tuple-element.1146), channel_id=1, source_target_pairs={{0,1},{1,2},{2,3},{3,0},{4,5},{5,6},{6,7},{7,4},{8,9},{9,10},{10,1... | collective-permute-start | bytes 1916936 | tf_op jit(solution)/shard_map/ppermute | solution.py:1218
  321.2 41.0 %collective-permute-start.54 = (bf16[768,768]{1,0:T(8,128)(2,1)}, bf16[768,768]{1,0:T(8,128)(2,1)}, u32[]{:S(2)}, u32[]{:S(2)}) collective-permute-start(bf16[768,768]{1,0:T(8,128)(2,1)} %get-tuple-element.1035.refs_5_), channel_id=1, source_target_pairs={{1,0},{2,1},{5,4},{6,5},{11,10},{8,11},{15,14},{12,15},{17,16},{18... | collective-permute-start | bytes 3538952 | tf_op jit(solution)/shard_map/ppermute | solution.py:1199
  322.5 39.8 %collective-permute-start.55 = (bf16[768,768]{1,0:T(8,128)(2,1)}, bf16[768,768]{1,0:T(8,128)(2,1)}, u32[]{:S(2)}, u32[]{:S(2)}) collective-permute-start(bf16[768,768]{1,0:T(8,128)(2,1)} %get-tuple-element.1035.refs_5_), channel_id=1, source_target_pairs={{3,0},{0,1},{7,4},{4,5},{9,10},{10,11},{13,14},{14,15},{19,16},{16... | collective-permute-start | bytes 3538952 | tf_op jit(solution)/shard_map/ppermute | solution.py:1199
  327.1 35.2 %collective-permute-start.56 = (bf16[2,2,96,768]{3,2,1,0:T(8,128)(2,1)}, bf16[2,2,96,768]{3,2,1,0:T(8,128)(2,1)S(1)}, u32[]{:S(2)}, u32[]{:S(2)}) collective-permute-start(bf16[2,2,96,768]{3,2,1,0:T(8,128)(2,1)} %get-tuple-element.909), channel_id=1, source_target_pairs={{0,4},{1,5},{2,6},{3,7},{4,0},{5,1},{6,2},{7,3},{8,12},{9,13},{10,... | collective-permute-start | bytes 1769480 | tf_op jit(solution)/shard_map/ppermute | solution.py:1173
  328.2 34.0 %collective-permute-start.57 = (bf16[2,2,96,768]{3,2,1,0:T(8,128)(2,1)}, bf16[2,2,96,768]{3,2,1,0:T(8,128)(2,1)}, u32[]{:S(2)}, u32[]{:S(2)}) collective-permute-start(bf16[2,2,96,768]{3,2,1,0:T(8,128)(2,1)} %get-tuple-element.910), channel_id=1, source_target_pairs={{0,16},{1,17},{2,18},{3,19},{4,20},{5,21},{6,22},{7,23},{8,24},{9,... | collective-permute-start | bytes 1769480 | tf_op jit(solution)/shard_map/ppermute | solution.py:1173
  328.5 33.8 %collective-permute-start.58 = (bf16[2,2,96,768]{3,2,1,0:T(8,128)(2,1)}, bf16[2,2,96,768]{3,2,1,0:T(8,128)(2,1)}, u32[]{:S(2)}, u32[]{:S(2)}) collective-permute-start(bf16[2,2,96,768]{3,2,1,0:T(8,128)(2,1)} %get-tuple-element.911), channel_id=1, source_target_pairs={{0,20},{1,21},{2,22},{3,23},{4,16},{5,17},{6,18},{7,19},{8,28},{9,... | collective-permute-start | bytes 1769480 | tf_op jit(solution)/shard_map/ppermute | solution.py:1173
  362.3 20.2 %collective-permute-start.60 = (bf16[4,2,192,768]{3,2,1,0:T(8,128)(2,1)}, bf16[4,2,192,768]{3,2,1,0:T(8,128)(2,1)}, u32[]{:S(2)}, u32[]{:S(2)}) collective-permute-start(bf16[4,2,192,768]{3,2,1,0:T(8,128)(2,1)} %get-tuple-element.914), channel_id=1, source_target_pairs={{0,8},{1,9},{2,10},{3,11},{4,12},{5,13},{6,14},{7,15},{8,0},{9,1},... | collective-permute-start | bytes 7077896 | tf_op jit(solution)/shard_map/ppermute | solution.py:1169
  419.6 23.9 %collective-permute-start.70 = (bf16[4,24,768]{2,1,0:T(8,128)(2,1)}, bf16[4,24,768]{2,1,0:T(8,128)(2,1)S(1)}, u32[]{:S(2)}, u32[]{:S(2)}) collective-permute-start(bf16[4,24,768]{2,1,0:T(8,128)(2,1)} %get-tuple-element.1167), channel_id=1, source_target_pairs={{0,3},{1,0},{2,1},{3,2},{4,7},{5,4},{6,5},{7,6},{8,11},{9,8},{10,9... | collective-permute-start | bytes 442376 | tf_op jit(solution)/shard_map/ppermute | solution.py:1218
  419.6 26.6 %collective-permute-start.71 = (bf16[4,24,768]{2,1,0:T(8,128)(2,1)}, bf16[4,24,768]{2,1,0:T(8,128)(2,1)S(1)}, u32[]{:S(2)}, u32[]{:S(2)}) collective-permute-start(bf16[4,24,768]{2,1,0:T(8,128)(2,1)} %get-tuple-element.1168), channel_id=1, source_target_pairs={{0,2},{1,3},{2,0},{3,1},{4,6},{5,7},{6,4},{7,5},{8,10},{9,11},{10,... | collective-permute-start | bytes 442376 | tf_op jit(solution)/shard_map/ppermute | solution.py:1218
  419.6 26.6 %collective-permute-start.72 = (bf16[4,24,768]{2,1,0:T(8,128)(2,1)S(1)}, bf16[4,24,768]{2,1,0:T(8,128)(2,1)}, u32[]{:S(2)}, u32[]{:S(2)}) collective-permute-start(bf16[4,24,768]{2,1,0:T(8,128)(2,1)S(1)} %get-tuple-element.1166), channel_id=1, source_target_pairs={{0,1},{1,2},{2,3},{3,0},{4,5},{5,6},{6,7},{7,4},{8,9},{9,10},{10,1... | collective-permute-start | bytes 442376 | tf_op jit(solution)/shard_map/ppermute | solution.py:1218
  425.4 20.8 %collective-permute-start.69 = (bf16[416,768]{1,0:T(8,128)(2,1)}, bf16[416,768]{1,0:T(8,128)(2,1)}, u32[]{:S(2)}, u32[]{:S(2)}) collective-permute-start(bf16[416,768]{1,0:T(8,128)(2,1)} %fusion.13), channel_id=1, source_target_pairs={{0,1},{1,2},{2,3},{3,0},{4,5},{5,6},{6,7},{7,4},{8,9},{9,10},{10,1... | collective-permute-start | bytes 1916936 | tf_op jit(solution)/shard_map/ppermute | solution.py:1183
  448.7 22.1 %collective-permute-start.74 = (bf16[4,24,768]{2,1,0:T(8,128)(2,1)S(1)}, bf16[4,24,768]{2,1,0:T(8,128)(2,1)S(1)}, u32[]{:S(2)}, u32[]{:S(2)}) collective-permute-start(bf16[4,24,768]{2,1,0:T(8,128)(2,1)S(1)} %pad_maximum_fusion.19), channel_id=1, source_target_pairs={{0,1},{1,2},{2,3},{3,0},{4,5},{5,6},{6,7},{7,4},{8,9},{9,10},{10,1... | collective-permute-start | bytes 442376 | tf_op jit(solution)/shard_map/ppermute | solution.py:1218
  448.7 26.7 %collective-permute-start.75 = (bf16[4,24,768]{2,1,0:T(8,128)(2,1)S(1)}, bf16[4,24,768]{2,1,0:T(8,128)(2,1)S(1)}, u32[]{:S(2)}, u32[]{:S(2)}) collective-permute-start(bf16[4,24,768]{2,1,0:T(8,128)(2,1)S(1)} %pad_maximum_fusion.19), channel_id=1, source_target_pairs={{0,2},{1,3},{2,0},{3,1},{4,6},{5,7},{6,4},{7,5},{8,10},{9,11},{10,... | collective-permute-start | bytes 442376 | tf_op jit(solution)/shard_map/ppermute | solution.py:1218
  450.7 24.8 %collective-permute-start.76 = (bf16[4,24,768]{2,1,0:T(8,128)(2,1)S(1)}, bf16[4,24,768]{2,1,0:T(8,128)(2,1)S(1)}, u32[]{:S(2)}, u32[]{:S(2)}) collective-permute-start(bf16[4,24,768]{2,1,0:T(8,128)(2,1)S(1)} %pad_maximum_fusion.19), channel_id=1, source_target_pairs={{0,3},{1,0},{2,1},{3,2},{4,7},{5,4},{6,5},{7,6},{8,11},{9,8},{10,9... | collective-permute-start | bytes 442376 | tf_op jit(solution)/shard_map/ppermute | solution.py:1218
  453.6 17.2 %collective-permute-start.78 = (f32[4,768]{1,0:T(4,128)S(1)}, f32[4,768]{1,0:T(4,128)S(1)}, u32[]{:S(2)}, u32[]{:S(2)}) collective-permute-start(f32[4,768]{1,0:T(4,128)S(1)} %add.382), channel_id=1, source_target_pairs={{0,4},{1,5},{2,6},{3,7},{4,0},{5,1},{6,2},{7,3},{8,12},{9,13},{10,... | collective-permute-start | bytes 36872 | tf_op jit(solution)/shard_map/ppermute | solution.py:1173
  457.1 18.4 %collective-permute-start.77 = (bf16[416,768]{1,0:T(8,128)(2,1)}, bf16[416,768]{1,0:T(8,128)(2,1)S(1)}, u32[]{:S(2)}, u32[]{:S(2)}) collective-permute-start(bf16[416,768]{1,0:T(8,128)(2,1)} %fusion.5), channel_id=1, source_target_pairs={{0,1},{1,2},{2,3},{3,0},{4,5},{5,6},{6,7},{7,4},{8,9},{9,10},{10,1... | collective-permute-start | bytes 1916936 | tf_op jit(solution)/shard_map/ppermute | solution.py:1183
  481.6 17.3 %collective-permute-start.80 = (bf16[6,256,256]{2,1,0:T(8,128)(2,1)}, bf16[6,256,256]{2,1,0:T(8,128)(2,1)S(1)}, u32[]{:S(2)}, u32[]{:S(2)}) collective-permute-start(bf16[6,256,256]{2,1,0:T(8,128)(2,1)} %wide_last.1.refs_0_), channel_id=1, source_target_pairs={{0,3},{1,0},{4,7},{5,4},{10,9},{11,10},{14,13},{15,14},{16,19},{17... | collective-permute-start | bytes 2359304 | tf_op jit(solution)/shard_map/ppermute | solution.py:1204
  521.4 31.5 %collective-permute-start.92 = (f32[4,768]{1,0:T(4,128)S(1)}, f32[4,768]{1,0:T(4,128)S(1)}, u32[]{:S(2)}, u32[]{:S(2)}) collective-permute-start(f32[4,768]{1,0:T(4,128)S(1)} %add.388), channel_id=1, source_target_pairs={{0,2},{1,3},{2,0},{3,1},{4,6},{5,7},{6,4},{7,5},{8,10},{9,11},{10,... | collective-permute-start | bytes 36872 | tf_op jit(solution)/shard_map/ppermute | solution.py:1179
  531.3 26.8 %collective-permute-start.88 = (bf16[416,768]{1,0:T(8,128)(2,1)S(1)}, bf16[416,768]{1,0:T(8,128)(2,1)S(1)}, u32[]{:S(2)}, u32[]{:S(2)}) collective-permute-start(bf16[416,768]{1,0:T(8,128)(2,1)S(1)} %fusion.4), channel_id=1, source_target_pairs={{0,1},{1,2},{2,3},{3,0},{4,5},{5,6},{6,7},{7,4},{8,9},{9,10},{10,1... | collective-permute-start | bytes 1916936 | tf_op jit(solution)/shard_map/ppermute | solution.py:1183
  531.4 21.6 %collective-permute-start.89 = (bf16[2,2,96,768]{3,2,1,0:T(8,128)(2,1)}, bf16[2,2,96,768]{3,2,1,0:T(8,128)(2,1)}, u32[]{:S(2)}, u32[]{:S(2)}) collective-permute-start(bf16[2,2,96,768]{3,2,1,0:T(8,128)(2,1)} %get-tuple-element.1053), channel_id=1, source_target_pairs={{0,4},{1,5},{2,6},{3,7},{4,0},{5,1},{6,2},{7,3},{8,12},{9,13},{10,... | collective-permute-start | bytes 1769480 | tf_op jit(solution)/shard_map/ppermute | solution.py:1173
  532.4 25.7 %collective-permute-start.90 = (bf16[2,2,96,768]{3,2,1,0:T(8,128)(2,1)}, bf16[2,2,96,768]{3,2,1,0:T(8,128)(2,1)}, u32[]{:S(2)}, u32[]{:S(2)}) collective-permute-start(bf16[2,2,96,768]{3,2,1,0:T(8,128)(2,1)} %get-tuple-element.1054), channel_id=1, source_target_pairs={{0,16},{1,17},{2,18},{3,19},{4,20},{5,21},{6,22},{7,23},{8,24},{9,... | collective-permute-start | bytes 1769480 | tf_op jit(solution)/shard_map/ppermute | solution.py:1173
  533.5 24.6 %collective-permute-start.91 = (bf16[2,2,96,768]{3,2,1,0:T(8,128)(2,1)}, bf16[2,2,96,768]{3,2,1,0:T(8,128)(2,1)}, u32[]{:S(2)}, u32[]{:S(2)}) collective-permute-start(bf16[2,2,96,768]{3,2,1,0:T(8,128)(2,1)} %get-tuple-element.1055), channel_id=1, source_target_pairs={{0,20},{1,21},{2,22},{3,23},{4,16},{5,17},{6,18},{7,19},{8,28},{9,... | collective-permute-start | bytes 1769480 | tf_op jit(solution)/shard_map/ppermute | solution.py:1173
  (123 other events, 1185.3 us)

commit v2 on v1

--- a/solution.py
+++ b/solution.py
@@ -540,7 +540,7 @@
 
 def push_kernel(place, own, *refs):
     gots, moments, refs = refs[:2], refs[2:6], refs[6:]
-    pushes, outs, (total,) = refs[:2], refs[2:6], refs[6:]
+    pushes, bands, outs, (total,) = refs[:2], refs[2:5], refs[5:9], refs[9:]
     chip, core, tp = place[0], place[1], place[2]
     keep = 1.0 - momentum_decay
     depth = outs[0].shape[2]
@@ -566,6 +566,9 @@
                     def _():
                         pushes[spot][rows, :] = pushed
 
+    for place, band in enumerate(bands):
+        band[...] = pushes[0][pl.ds(place * TILE, TILE), :]
+
 
 def push_rows(place, own, gots, moments):
     size, width = own.shape[1:]
@@ -575,8 +578,10 @@
     return pl.pallas_call(
         push_kernel,
         in_specs=[pl.BlockSpec(memory_space=pltpu.SMEM)] + [vmem] * 7,
-        out_specs=[vmem] * 6,
-        out_shape=[jax.ShapeDtypeStruct((size, width), jnp.bfloat16)] * 2 + [rows] * 4,
+        out_specs=[vmem] * 9,
+        out_shape=[jax.ShapeDtypeStruct((size, width), jnp.bfloat16)] * 2
+        + [jax.ShapeDtypeStruct((TILE, width), jnp.bfloat16)] * 3
+        + [rows] * 4,
         scratch_shapes=[pltpu.VMEM((size, width), jnp.float32)],
         compiler_params=pltpu.CompilerParams(vmem_limit_bytes=VMEM_ASK),
         cost_estimate=pl.CostEstimate(
@@ -778,23 +783,20 @@
     @pl.when(expert == count - 1)
     def _():
         for side, part in enumerate((part_own, part_other)):
-
-            def collect(place, carry):
+            for place in range(blocks // 2):
                 block = side * (blocks // 2) + place
+                ways, rows_of = spread.at[place % 2], found.at[place % 2]
                 for each in range(count):
                     start = pl.multiple_of(starts[each * (blocks + 1) + block], 16)
-                    hot = one_hot(rank[each, pl.ds(block, 1), :])
+                    hot = one_hot(rank[each, block : block + 1, :])
                     rows = moved[each, pl.ds(start, SPAN), :]
                     if gated:
-                        weight = gate_of(hot, gate[each, pl.ds(block, 1), :])
+                        weight = gate_of(hot, gate[each, block : block + 1, :])
                         rows = (rows.astype(jnp.float32) * weight).astype(low)
                     band = pl.ds(each * SPAN, SPAN)
-                    spread[band, :] = jnp.where(hot, 1.0, 0.0).astype(low)
-                    found[band, :] = rows
-                part[place] = dot_tn(spread[...], found[...]).astype(low)
-                return carry
-
-            lax.fori_loop(0, blocks // 2, collect, 0)
+                    ways[band, :] = jnp.where(hot, 1.0, 0.0).astype(low)
+                    rows_of[band, :] = rows
+                part[place] = dot_tn(ways[...], rows_of[...]).astype(low)
 
 
 def pass_shapes(rank, pieces):
@@ -874,14 +876,14 @@
         grid_spec=pltpu.PrefetchScalarGridSpec(
             num_scalar_prefetch=1,
             grid=(count,),
-            in_specs=[vectors, vectors, pl.BlockSpec((1, tiles * TILE, width), of_expert)]
+            in_specs=[vectors, vectors, pl.BlockSpec((1,) + acts.shape[1:], of_expert)]
             + piece_specs,
             out_specs=[parts, parts],
             scratch_shapes=[
                 pltpu.VMEM((features, width), low),
                 pltpu.VMEM((count, most + TILE, features), low),
-                pltpu.VMEM((count * SPAN, padded), low),
-                pltpu.VMEM((count * SPAN, features), low),
+                pltpu.VMEM((2, count * SPAN, padded), low),
+                pltpu.VMEM((2, count * SPAN, features), low),
             ],
         ),
         out_shape=[part_shape, part_shape],
@@ -928,77 +930,68 @@
     place, tokens, norms, w0, w1, w2, w3, others_near, others_far,
     normed_out, qkv_out, blended_out, residual_out, second_out, weights,
 ):
-    features = tokens.shape[2]
+    features = tokens.shape[1]
     low = jnp.bfloat16
 
-    @pl.when(pl.program_id(0) == 0)
-    def _():
-        chip, core = place[0], place[1]
-        depth = features // 8
-        others = (others_near.at[0], others_near.at[1], others_far.at[0], others_far.at[1])
-        for side, pieces in enumerate(((w0, w1, w2, w3), others)):
-            for turn, piece in enumerate(pieces):
-                other = jnp.bitwise_xor(chip, turn)
-                row = ((other // 2) * 2 + jnp.bitwise_xor(core, side)) * 2 + other % 2
-                rows = pl.ds(pl.multiple_of(row * depth, 16), depth)
-                for which in range(4):
-                    weights[which, rows, :] = piece[which]
+    chip, core = place[0], place[1]
+    depth = features // 8
+    others = (others_near.at[0], others_near.at[1], others_far.at[0], others_far.at[1])
+    for side, pieces in enumerate(((w0, w1, w2, w3), others)):
+        for turn, piece in enumerate(pieces):
+            other = jnp.bitwise_xor(chip, turn)
+            row = ((other // 2) * 2 + jnp.bitwise_xor(core, side)) * 2 + other % 2
+            rows = pl.ds(pl.multiple_of(row * depth, 16), depth)
+            for which in range(4):
+                weights[which, rows, :] = piece[which]
 
     normed, unused, unused = row_norm(
-        tokens[0].astype(jnp.float32), norms[0:1, :], norms[2:3, :]
-    )
-    normed_out[0] = normed.astype(low)
+        tokens[...].astype(jnp.float32), norms[0:1, :], norms[2:3, :]
+    )
+    normed_out[...] = normed.astype(low)
     for which in range(3):
-        qkv_out[0, which] = dot_nn(normed_out[0], weights[which]).astype(low)
+        qkv_out[which] = dot_nn(normed_out[...], weights[which]).astype(low)
     keys_used = lax.broadcasted_iota(jnp.int32, (IMAGE, IMAGE), 1) < LEN
     first = lax.broadcasted_iota(jnp.int32, (IMAGE, 2 * HEAD_DIM), 1) < HEAD_DIM
-    for start in range(0, features, 2 * HEAD_DIM):
-        cols = pl.ds(start, 2 * HEAD_DIM)
-        query, key, value = (qkv_out[0, which, :, cols] for which in range(3))
-        mixed = []
-        for here in (first, jnp.logical_not(first)):
-            soft = head_soft(query, key, here, keys_used).astype(low)
-            mixed.append(dot_nn(soft, value))
-        blended_out[0, :, cols] = jnp.where(first, mixed[0], mixed[1]).astype(low)
-    residual = tokens[0].astype(jnp.float32) + dot_nn(blended_out[0], weights[3])
-    residual_out[0] = residual
+
+    def attend(image, carry):
+        rows = pl.ds(pl.multiple_of(image * IMAGE, 16), IMAGE)
+        for start in range(0, features, 2 * HEAD_DIM):
+            cols = pl.ds(start, 2 * HEAD_DIM)
+            query, key, value = (qkv_out[which, rows, cols] for which in range(3))
+            mixed = []
+            for here in (first, jnp.logical_not(first)):
+                soft = head_soft(query, key, here, keys_used).astype(low)
+                mixed.append(dot_nn(soft, value))
+            blended_out[rows, cols] = jnp.where(first, mixed[0], mixed[1]).astype(low)
+        return carry
+
+    lax.fori_loop(0, tokens.shape[0] // IMAGE, attend, 0)
+    residual = tokens[...].astype(jnp.float32) + dot_nn(blended_out[...], weights[3])
+    residual_out[...] = residual
     second, unused, unused = row_norm(residual, norms[1:2, :], norms[3:4, :])
-    second_out[0] = second.astype(low)
+    second_out[...] = second.astype(low)
 
 
 def attention_forward(place, tokens, norms, pieces, others):
-    images, rows, features = tokens.shape
+    rows, features = tokens.shape
     low = jnp.bfloat16
-    image = pl.BlockSpec((1, rows, features), lambda i, place: (i, 0, 0))
-    shape = jax.ShapeDtypeStruct((images, rows, features), low)
+    vmem = pl.BlockSpec(memory_space=pltpu.VMEM)
+    shape = jax.ShapeDtypeStruct((rows, features), low)
     return pl.pallas_call(
         forward_kernel,
-        grid_spec=pltpu.PrefetchScalarGridSpec(
-            num_scalar_prefetch=1,
-            grid=(images,),
-            in_specs=[image, pl.BlockSpec(norms.shape, lambda i, place: (0, 0))]
-            + [pl.BlockSpec(pieces[0].shape, lambda i, place: (0, 0, 0))] * 4
-            + [pl.BlockSpec(others[0].shape, lambda i, place: (0, 0, 0, 0))] * 2,
-            out_specs=[
-                image,
-                pl.BlockSpec((1, 3, rows, features), lambda i, place: (i, 0, 0, 0)),
-                image,
-                image,
-                image,
-                pl.BlockSpec((4, features, features), lambda i, place: (0, 0, 0)),
-            ],
-        ),
+        in_specs=[pl.BlockSpec(memory_space=pltpu.SMEM)] + [vmem] * 8,
+        out_specs=[vmem] * 6,
         out_shape=[
             shape,
-            jax.ShapeDtypeStruct((images, 3, rows, features), low),
+            jax.ShapeDtypeStruct((3, rows, features), low),
             shape,
-            jax.ShapeDtypeStruct((images, rows, features), jnp.float32),
+            jax.ShapeDtypeStruct((rows, features), jnp.float32),
             shape,
             jax.ShapeDtypeStruct((4, features, features), low),
         ],
         compiler_params=pltpu.CompilerParams(vmem_limit_bytes=VMEM_ASK),
         cost_estimate=pl.CostEstimate(
-            flops=10 * images * rows * features * features,
+            flops=10 * rows * features * features,
             bytes_accessed=16 * 1024 * 1024,
             transcendentals=0,
         ),
@@ -1010,138 +1003,102 @@
     place, tokens, cots, residual, blended, normed, qkv, weights, norms,
     second0, second1, second2, second3,
     input_grad, mine, theirs, vectors,
-    parts, d_heads, d_qkv, d_sum,
+    part, d_heads, d_qkv, d_sum,
 ):
-    image = pl.program_id(0)
-    features = tokens.shape[2]
+    rows_all, features = tokens.shape
     low = jnp.bfloat16
     core = place[1]
-    seconds = (second0, second1, second2, second3)
-    last = image == pl.num_programs(0) - 1
-
-    @pl.when(image == 0)
-    def _():
-        vectors[...] = jnp.zeros_like(vectors)
-
-    d_second = seconds[0][0].astype(jnp.float32)
-    for piece in seconds[1:]:
-        d_second = d_second + piece[0].astype(jnp.float32)
-    unused, unit, inverse = row_norm(residual[0], norms[1:2, :], norms[3:4, :])
-    vectors[1:2, :] += jnp.sum(d_second * unit, axis=0, keepdims=True)
-    vectors[3:4, :] += jnp.sum(d_second, axis=0, keepdims=True)
-    d_sum[...] = cots[0].astype(jnp.float32) + row_norm_back(
+
+    def store_part(which, value):
+        part[...] = value
+        slab = mine.shape[2]
+        for side in range(2):
+            own = pl.ds(pl.multiple_of((2 * side + core) * slab, slab), slab)
+            other = pl.ds(pl.multiple_of((2 * side + 1 - core) * slab, slab), slab)
+            mine[which, side] = part[own, :].astype(low)
+            theirs[which, side] = part[other, :].astype(low)
+
+    d_second = second0[...].astype(jnp.float32)
+    for piece in (second1, second2, second3):
+        d_second = d_second + piece[...].astype(jnp.float32)
+    unused, unit, inverse = row_norm(residual[...], norms[1:2, :], norms[3:4, :])
+    vectors[...] = jnp.zeros_like(vectors)
+    vectors[1:2, :] = jnp.sum(d_second * unit, axis=0, keepdims=True)
+    vectors[3:4, :] = jnp.sum(d_second, axis=0, keepdims=True)
+    d_sum[...] = cots[...].astype(jnp.float32) + row_norm_back(
         d_second, unit, inverse, norms[1:2, :]
     )
     d_attended = d_sum[...].astype(low)
     d_heads[...] = dot_nt(d_attended, weights[3]).astype(low)
-    out_part = dot_tn(blended[0], d_attended)
-
-    @pl.when(image == 0)
-    def _():
-        parts[3] = out_part
-
-    @pl.when(image > 0)
-    def _():
-        parts[3] = parts[3] + out_part
+    store_part(3, dot_tn(blended[...], d_attended))
 
     keys_used = lax.broadcasted_iota(jnp.int32, (IMAGE, IMAGE), 1) < LEN
     first = lax.broadcasted_iota(jnp.int32, (IMAGE, 2 * HEAD_DIM), 1) < HEAD_DIM
     scale = HEAD_DIM ** (-0.5)
-    for start in range(0, features, 2 * HEAD_DIM):
-        cols = pl.ds(start, 2 * HEAD_DIM)
-        query, key, value = (qkv[0, which, :, cols] for which in range(3))
-        upper = d_heads[:, cols]
-        found = []
-        for here in (first, jnp.logical_not(first)):
-            soft = head_soft(query, key, here, keys_used)
-            d_soft = dot_nt(jnp.where(here, upper, jnp.zeros_like(upper)), value)
-            inner = jnp.sum(soft * d_soft, axis=1, keepdims=True)
-            d_scores = (soft * (d_soft - inner)).astype(low)
-            found.append(
-                (
-                    dot_nn(d_scores, key) * scale,
-                    dot_tn(d_scores, query) * scale,
-                    dot_tn(soft.astype(low), upper),
+
+    def attend(image, carry):
+        rows = pl.ds(pl.multiple_of(image * IMAGE, 16), IMAGE)
+        for start in range(0, features, 2 * HEAD_DIM):
+            cols = pl.ds(start, 2 * HEAD_DIM)
+            query, key, value = (qkv[which, rows, cols] for which in range(3))
+            upper = d_heads[rows, cols]
+            found = []
+            for here in (first, jnp.logical_not(first)):
+                soft = head_soft(query, key, here, keys_used)
+                d_soft = dot_nt(jnp.where(here, upper, jnp.zeros_like(upper)), value)
+                inner = jnp.sum(soft * d_soft, axis=1, keepdims=True)
+                d_scores = (soft * (d_soft - inner)).astype(low)
+                found.append(
+                    (
+                        dot_nn(d_scores, key) * scale,
+                        dot_tn(d_scores, query) * scale,
+                        dot_tn(soft.astype(low), upper),
+                    )
                 )
-            )
-        for which in range(3):
-            d_qkv[which, :, cols] = jnp.where(first, found[0][which], found[1][which]).astype(low)
+            for which in range(3):
+                d_qkv[which, rows, cols] = jnp.where(
+                    first, found[0][which], found[1][which]
+                ).astype(low)
+        return carry
+
+    lax.fori_loop(0, rows_all // IMAGE, attend, 0)
     d_normed = dot_nt(d_qkv[0], weights[0])
     for which in range(1, 3):
         d_normed = d_normed + dot_nt(d_qkv[which], weights[which])
     for which in range(3):
-        in_part = dot_tn(normed[0], d_qkv[which])
-
-        @pl.when(image == 0)
-        def _():
-            parts[which] = in_part
-
-        @pl.when(image > 0)
-        def _():
-            parts[which] = parts[which] + in_part
-
+        store_part(which, dot_tn(normed[...], d_qkv[which]))
     unused, unit, inverse = row_norm(
-        tokens[0].astype(jnp.float32), norms[0:1, :], norms[2:3, :]
-    )
-    vectors[0:1, :] += jnp.sum(d_normed * unit, axis=0, keepdims=True)
-    vectors[2:3, :] += jnp.sum(d_normed, axis=0, keepdims=True)
-    input_grad[0] = d_sum[...] + row_norm_back(d_normed, unit, inverse, norms[0:1, :])
-
-    @pl.when(last)
-    def _():
-        slab = mine.shape[2]
-        for which in range(4):
-            for side in range(2):
-                own = pl.ds(pl.multiple_of((2 * side + core) * slab, slab), slab)
-                other = pl.ds(pl.multiple_of((2 * side + 1 - core) * slab, slab), slab)
-                mine[which, side] = parts[which, own, :].astype(low)
-                theirs[which, side] = parts[which, other, :].astype(low)
+        tokens[...].astype(jnp.float32), norms[0:1, :], norms[2:3, :]
+    )
+    vectors[0:1, :] = jnp.sum(d_normed * unit, axis=0, keepdims=True)
+    vectors[2:3, :] = jnp.sum(d_normed, axis=0, keepdims=True)
+    input_grad[...] = d_sum[...] + row_norm_back(d_normed, unit, inverse, norms[0:1, :])
 
 
 def attention_backward(place, tokens, cots, residual, blended, normed, qkv, seconds, weights, norms):
-    images, rows, features = tokens.shape
+    rows, features = tokens.shape
     low = jnp.bfloat16
-    image = pl.BlockSpec((1, rows, features), lambda i, place: (i, 0, 0))
+    vmem = pl.BlockSpec(memory_space=pltpu.VMEM)
     half_shape = jax.ShapeDtypeStruct((4, 2, features // 4, features), low)
-    half = pl.BlockSpec(half_shape.shape, lambda i, place: (0, 0, 0, 0))
     return pl.pallas_call(
         backward_kernel,
-        grid_spec=pltpu.PrefetchScalarGridSpec(
-            num_scalar_prefetch=1,
-            grid=(images,),
-            in_specs=[
-                image,
-                image,
-                image,
-                image,
-                image,
-                pl.BlockSpec((1, 3, rows, features), lambda i, place: (i, 0, 0, 0)),
-                pl.BlockSpec(weights.shape, lambda i, place: (0, 0, 0)),
-                pl.BlockSpec(norms.shape, lambda i, place: (0, 0)),
-            ]
-            + [image] * 4,
-            out_specs=[
-                image,
-                half,
-                half,
-                pl.BlockSpec((8, features), lambda i, place: (0, 0)),
-            ],
-            scratch_shapes=[
-                pltpu.VMEM((4, features, features), jnp.float32),
-                pltpu.VMEM((rows, features), low),
-                pltpu.VMEM((3, rows, features), low),
-                pltpu.VMEM((rows, features), jnp.float32),
-            ],
-        ),
+        in_specs=[pl.BlockSpec(memory_space=pltpu.SMEM)] + [vmem] * 12,
+        out_specs=[vmem] * 4,
+        scratch_shapes=[
+            pltpu.VMEM((features, features), jnp.float32),
+            pltpu.VMEM((rows, features), low),
+            pltpu.VMEM((3, rows, features), low),
+            pltpu.VMEM((rows, features), jnp.float32),
+        ],
         out_shape=[
-            jax.ShapeDtypeStruct((images, rows, features), jnp.float32),
+            jax.ShapeDtypeStruct((rows, features), jnp.float32),
             half_shape,
             half_shape,
             jax.ShapeDtypeStruct((8, features), jnp.float32),
         ],
         compiler_params=pltpu.CompilerParams(vmem_limit_bytes=VMEM_ASK),
         cost_estimate=pl.CostEstimate(
-            flops=40 * images * rows * features * features,
+            flops=40 * rows * features * features,
             bytes_accessed=24 * 1024 * 1024,
             transcendentals=0,
         ),
@@ -1303,12 +1260,14 @@
     cols_local = upward.shape[2]
 
     v = Live()
-    place = jnp.stack([chip, core, tp]).astype(jnp.int32)
+    device = jnp.stack([chip, core, tp]).astype(jnp.int32)
     y_here, x_here = shard // 2, ctx
     padded = seqs * IMAGE
     half = tps // 2
     own_tokens, own_cot = (
-        jnp.pad(value[0].reshape(seqs, LEN, features), ((0, 0), (0, IMAGE - LEN), (0, 0)))
+        jnp.pad(
+            value[0].reshape(seqs, LEN, features), ((0, 0), (0, IMAGE - LEN), (0, 0))
+        ).reshape(padded, features)
         for value in (tokens, cotangent)
     )
 
@@ -1325,7 +1284,7 @@
     v.up_x, v.down_y = [swap_chip(v.up[0], 1)], [swap_chip(v.down[0], 2)]
     v.column = direct_gather(jnp.concatenate([inward, outward[None]]))
     v.sent = jnp.stack([up_sent, down_sent])
-    v.cots = [own_cot.reshape(padded, features)]
+    v.cots = [own_cot]
 
     packed = jnp.concatenate([routing[0].astype(jnp.float32).T, gating[0].T])
     packed = jnp.pad(
@@ -1371,7 +1330,7 @@
     counts = jnp.sum(chosen.astype(jnp.int32), axis=2)
     counts = (counts + 15) // 16 * 16
     starts = jnp.cumsum(jnp.pad(counts, ((0, 0), (1, 0))), axis=1).astype(jnp.int32).reshape(-1)
-    v.routes = (jnp.concatenate([starts, place[:2]]), rank, gate_tok)
+    v.routes = (jnp.concatenate([starts, device[:2]]), rank, gate_tok)
     v = hold(v)
     far = jnp.concatenate(v.drop.far)
     v.pieces = v.pieces + [far]
@@ -1386,9 +1345,9 @@
     norms = norms.transpose(4, 0, 2, 1, 3, 5).reshape(4, features)
 
     normed, qkv, blended, residual, second, full_weights = attention_forward(
-        place, own_tokens, norms, v.drop.pieces, v.drop.others
-    )
-    v.seconds = [second.reshape(padded, features)]
+        device, own_tokens, norms, v.drop.pieces, v.drop.others
+    )
+    v.seconds = [second]
     v.up_xy, v.down_xy = [swap_chip(v.up_x[0], 2)], [swap_chip(v.down_y[0], 1)]
     v.cots.append(pass_on(v.cots[-1]))
     v.cots_other = [swap_core(each) for each in v.cots[:2]]
@@ -1447,10 +1406,11 @@
     v.mixed = tokens_pass(*v.drop.routes, v.drop.hidden, v.drop.downs, True)
     v = hold(v)
 
-    *pushes, rows0, rows1, rows2, rows3 = push_rows(
-        place, v.drop.own, (v.drop.along_x, v.drop.along_y), v.drop.moments
-    )
-    v.push, v.rows = pushes, [rows0, rows1, rows2, rows3]
+    push, push_next, band0, band1, band2, *rows = push_rows(
+        device, v.drop.own, (v.drop.along_x, v.drop.along_y), v.drop.moments
+    )
+    v.push, v.blocks, v.rows = [push, push_next], [band0, band1, band2], rows
+    v.mixed = [v.mixed[0], swap_core(v.mixed[1])]
     v = hold(v)
 
     def rows_out(rows):
@@ -1466,11 +1426,10 @@
         return joined.astype(jnp.float32)
 
     v.joined = [v.push[0]] + [to_worker(v.push[1], turn) for turn in (1, 3)]
-    v.block = v.push[0]
     v.rows = rows_out(v.rows)
     v.input_grad, v.own, v.gone, v.vectors = attention_backward(
-        place, own_tokens, own_cot, residual, blended, normed, qkv,
-        [each.reshape(seqs, IMAGE, features) for each in v.drop.seconds],
+        device, own_tokens, own_cot, residual, blended, normed, qkv,
+        v.drop.seconds,
         full_weights, norms,
     )
     v = hold(v)
@@ -1478,45 +1437,56 @@
     def added(value, got):
         return value.astype(jnp.float32) + got.astype(jnp.float32)
 
-    third = features // 3
+    shape = (4, 2, 2, tps, rows_attn, features)
     v.gone = swap_core(v.gone)
-    v.blocks = [to_worker(v.block[:third], 2)]
-    v.rows = rows_between(v.rows)
-    v = hold(v)
-    sums = added(v.drop.own, v.drop.gone).reshape(4, 2, 2, tps, rows_attn, features)
-    first, last = sums[:, :, :, :half], sums[:, :, :, half:]
-    v.first = [pick(first, x_here, 2), swap_chip(pick(first, 1 - x_here, 2).astype(low), 1)]
-    v.last = [pick(last, y_here, 1), swap_chip(pick(last, 1 - y_here, 1).astype(low), 2)]
-    v.blocks.append(to_worker(v.block[third : 2 * third], 2))
+    v.blocks[:2] = [to_worker(block, 2) for block in v.blocks[:2]]
+    vectors = v.vectors[:4]
+    v.vectors = [vectors, swap_core(vectors)]
+    v.input_grad = v.input_grad.reshape(seqs, IMAGE, features)[:, :LEN].reshape(rows_here, features)
+    mixed = added(*v.mixed)
+    v.mixed = [mixed[0]] + [mixed[turn].astype(low) for turn in range(1, tps)]
+    v = hold(v)
+    own, gone = v.drop.own.reshape(shape), v.drop.gone.reshape(shape)
+
+    def first_part(x):
+        return added(pick(own, x, 2)[:, :, :half], pick(gone, x, 2)[:, :, :half])
+
+    def last_part(y):
+        return added(pick(own, y, 1)[:, :, half:], pick(gone, y, 1)[:, :, half:])
+
+    v.first = [first_part(x_here), swap_chip(first_part(1 - x_here).astype(low), 1)]
+    v.last = [last_part(y_here), swap_chip(last_part(1 - y_here).astype(low), 2)]
+    v.mixed.append(pass_on(v.mixed[1]))
+    vectors = sum(v.vectors)
+    v.vectors = [vectors, swap_chip(vectors, 1)]
     v = hold(v)
     first, last = added(*v.first), added(*v.last)
     v.first = [pick(first, y_here, 1), swap_chip(pick(first, 1 - y_here, 1).astype(low), 2)]
     v.last = [pick(last, x_here, 1), swap_chip(pick(last, 1 - x_here, 1).astype(low), 1)]
-    v.blocks.append(to_worker(v.drop.block[2 * third :], 2))
-    v.mixed = [v.mixed[0], swap_core(v.mixed[1])]
+    v.blocks[2] = to_worker(v.blocks[2], 2)
+    vectors = sum(v.vectors)
+    v.vectors = [vectors, swap_chip(vectors, 2)]
     v = hold(v)
 
     sums = jnp.concatenate([added(*v.drop.first), added(*v.drop.last)], axis=1)
-    parts = [pick(sums, (tp - turn) % tps, 1) for turn in range(tps)]
-    v.sums = [parts[0]] + [
-        pass_by(parts[turn].astype(low), -turn) for turn in range(1, tps)
+    vectors = jnp.pad(sum(v.drop.vectors)[:, None], ((0, 0), (0, 7), (0, 0)))
+    parts = [
+        jnp.concatenate([pick(sums, (tp - turn) % tps, 1), vectors], axis=1).astype(low)
+        for turn in range(tps)
     ]
-    mixed = added(*v.mixed)
-    v.mixed = [mixed, pass_on(mixed[1].astype(low))]
+    v.sums = [parts[0]] + [pass_by(parts[turn], -turn) for turn in range(1, tps)]
     v.mixers = wide_first(v.drop.joined + v.drop.blocks)
-    vectors = v.vectors[:4]
-    v.vectors = [vectors, swap_core(vectors)]
     v = hold(v)
     sums = sum(part.astype(jnp.float32) for part in v.drop.sums)
+    v.vectors = lax.dynamic_slice(
+        sums[:, rows_attn], (0, lax.axis_index(axes) * rows_attn), (4, rows_attn)
+    )
+    sums = sums[:, :rows_attn]
     inward_grad, outward_grad = sums[:3], sums[3]
     inward_state, inward_push = advance(inward_grad, inward_moment)
     outward_state, outward_push = advance(outward_grad, outward_moment)
     v.column = direct_gather(jnp.concatenate([inward_push, outward_push[None]]).astype(low))
     v.mixers = [wide_last(*v.mixers)]
-    mixed, got = v.mixed
-    v.mixed = [mixed, pass_on(added(mixed[2], got).astype(low))]
-    vectors = sum(v.vectors)
-    v.vectors = [vectors, swap_chip(vectors, 1)]
     v = hold(v)
     column = by_tp(v.drop.column, tp).transpose(1, 0, 2, 3)
     gone = relative(column, chip)
@@ -1527,44 +1497,35 @@
     pushes = place_chips(v.pushes, chip)
     v.pushes = [pushes, swap_core(pushes)]
     v.mixers.insert(2, from_worker(v.mixers[1], 2))
-    vectors = sum(v.vectors)
-    v.vectors = [vectors, swap_chip(vectors, 2)]
-    v.input_grad = v.input_grad[:, :LEN].reshape(rows_here, features)
+    v.rows = rows_between(v.rows)
+    v = hold(v)
+    pushes = place_cores(*v.drop.pushes, core)
+    pushes = pushes.reshape(2, 2, 2, tps, rows_attn, features).transpose(1, 0, 2, 3, 4, 5)
+    v.pushes = pushes.reshape(features, features)
+    v.new = apply_mixers(device, v.drop.mixers, v.drop.push, rows_local)
+    v = hold(v)
+
+    v.new = rows_out(v.new)
+    v.mixed[4] = pass_on(added(v.mixed[2], v.mixed[4]).astype(low))
+    v.moved = orthogonal_square(v.drop.pushes)
+    v = hold(v)
+    moved = v.drop.moved.reshape(2, 2, 2, tps, rows_attn, features)
+    moved = pick(pick(moved, core, 1), tp, 2).reshape(4, rows_attn, features)
+    gone = relative(moved, chip)
+    v.moved = [gone[0]] + [swap_chip(gone[turn], turn) for turn in range(1, 4)]
+    v.new = rows_between(v.new)
     upward_grad, downward_grad = rows_in(*v.drop.rows)
     v.states = [
         (upward_grad, advance(upward_grad, upward_moment)[0]),
         (downward_grad, advance(downward_grad, downward_moment)[0]),
     ]
-    v = hold(v)
-    pushes = place_cores(*v.drop.pushes, core)
-    pushes = pushes.reshape(2, 2, 2, tps, rows_attn, features).transpose(1, 0, 2, 3, 4, 5)
-    v.pushes = pushes.reshape(features, features)
-    vectors = sum(v.vectors)
-    v.vectors = [vectors, swap_tp(vectors, 1)]
-    v.new = apply_mixers(place, v.drop.mixers, v.drop.push, rows_local)
-    v = hold(v)
-
-    v.new = rows_out(v.new)
-    mixed, got = v.mixed
-    v.mixed = [mixed, pass_on(added(mixed[3], got).astype(low))]
-    vectors = sum(v.vectors)
-    v.vectors = [vectors, swap_tp(vectors, 2)]
-    v.moved = orthogonal_square(v.drop.pushes)
-    v = hold(v)
-    moved = v.drop.moved.reshape(2, 2, 2, tps, rows_attn, features)
-    moved = pick(pick(moved, core, 1), tp, 2).reshape(4, rows_attn, features)
-    gone = relative(moved, chip)
-    v.moved = [gone[0]] + [swap_chip(gone[turn], turn) for turn in range(1, 4)]
-    v.new = rows_between(v.new)
-    mixed, got = v.drop.mixed
-    result = (residual.reshape(padded, features) + added(mixed[0], got)).astype(low)
-    v.result = result.reshape(seqs, IMAGE, features)[:, :LEN].reshape(rows_here, features)
-    vectors = lax.dynamic_slice(
-        sum(v.drop.vectors), (0, lax.axis_index(axes) * rows_attn), (4, rows_attn)
-    )
-    v = hold(v)
-    result, input_grad = v.result, v.input_grad
-    scales_grad, shifts_grad = vectors[:2], vectors[2:]
+    v.mixed[4] = pass_on(added(v.mixed[3], v.mixed[4]).astype(low))
+    v = hold(v)
+    mixed = v.drop.mixed
+    result = (residual + added(mixed[0], mixed[4])).astype(low)
+    result = result.reshape(seqs, IMAGE, features)[:, :LEN].reshape(rows_here, features)
+    input_grad = v.input_grad
+    scales_grad, shifts_grad = v.vectors[:2], v.vectors[2:]
     scales_state, scales_push = advance(scales_grad, scales_moment)
     shifts_state, shifts_push = advance(shifts_grad, shifts_moment)
     up_new, down_new = rows_in(*v.new)

time: 590 us -> 584 us (0.990)
  Pallas kernels: 213 us -> 192 us
  waiting for transfers between devices: 169 us -> 179 us
  local copies, waits for them, and re-layouts: 35.1 us -> 42.1 us
    ppermute x43, waiting for transfers between devices: 91 us -> 104 us  [swap_chip(): lax.ppermute(value, axes, route_to(lambda s, c, t: (s ^ turn & 2, c ^ tur...]
    ppermute x5, waiting for transfers between devices: 22.6 us -> 9.55 us  [to_worker(): lax.ppermute(value, axes, worker_route(lambda w: w + turn, lambda w: w))]
    ppermute x2 -> x0, starting transfers between devices: 12.7 us -> none  [swap_tp(): return lax.ppermute(value, axes, route_to(lambda s, c, t: (s, c, t ^ turn)))]
    pallas_call x2, Pallas kernels: 49.9 us -> 41.3 us  [tokens_pass(): pl.pallas_call(functools.partial(tokens_kernel, gated), grid_spec=pltpu.P...]
    ppermute x9, starting transfers between devices: 6.59 us -> 13.9 us  [pass_on(): return lax.ppermute(value, axes, route_to(lambda s, c, t: (s, c, t + 1)))]
    ppermute x9, waiting for transfers between devices: 5.91 us -> 12.8 us  [pass_on(): return lax.ppermute(value, axes, route_to(lambda s, c, t: (s, c, t + 1)))]
    pallas_call x1, Pallas kernels: 55.1 us -> 48.4 us  [experts_pass(): pl.pallas_call(experts_kernel, grid_spec=pltpu.PrefetchScalarGridSpec(num...]
    ppermute x20, starting transfers between devices: 2.72 us -> 9 us  [swap_core(): return lax.ppermute(value, axes, route_to(lambda s, c, t: (s ^ 1, c, t)))]
  transfers between devices with their start and end apart: 97 -> 95, of which waited for: 33 -> 35; matrix products, arithmetic and copies ran while one was open for 9% -> 9% of each run, Pallas kernels for 35% -> 32%
where the time goes in v2:
time: 584 us; the launch traced here: 575 us
  Pallas kernels  192 us (33%)
  waiting for transfers between devices  179 us (31%)
  starting transfers between devices  109 us (19%)
  other arithmetic  49 us (8%)
  local copies, waits for them, and re-layouts  42.1 us (7%)
    ppermute x43, waiting for transfers between devices, swap_chip(): lax.ppermute(value, axes, route_to(lambda s, c, t: (s ^ turn & 2, c ^ tur...  104 us
    pallas_call x1, Pallas kernels, experts_pass(): pl.pallas_call(experts_kernel, grid_spec=pltpu.PrefetchScalarGridSpec(num...  48.4 us
    ppermute x43, starting transfers between devices, swap_chip(): lax.ppermute(value, axes, route_to(lambda s, c, t: (s ^ turn & 2, c ^ tur...  47.9 us
    pallas_call x2, Pallas kernels, tokens_pass(): pl.pallas_call(functools.partial(tokens_kernel, gated), grid_spec=pltpu.P...  41.3 us
    ppermute x15, waiting for transfers between devices, pass_by(): lax.ppermute(value, axes, route_to(lambda s, c, t: (s, c, t + steps)))  36.1 us
    pallas_call x2, Pallas kernels, wide_call(): pl.pallas_call(kernel, out_shape=out_shape, in_specs=[vmem] * len(inputs)...  30 us
    pallas_call x1, Pallas kernels, attention_backward(): pl.pallas_call(backward_kernel, in_specs=[pl.BlockSpec(memory_space=pltpu...  26.5 us
    ppermute x15, starting transfers between devices, pass_by(): lax.ppermute(value, axes, route_to(lambda s, c, t: (s, c, t + steps)))  22.7 us
  transfers between devices with their start and end apart: 95, of which 35 were waited for; matrix products, arithmetic and copies ran while one was open for 9% of the time, Pallas kernels for 32%

profile of v2, /device:TPU:0, one launch (start us, length us, event | category | flops | bytes accessed | tf_op | source)
XLA Modules:
  0.0 575.0 jit_solution(6600530772239546322)
XLA Ops:
  3.3 2.9 collective-permute-start.7
  10.5 2.6 collective-permute-start.5
  18.5 2.3 collective-permute-start.2
  24.1 3.8 collective-permute-done.1
  28.1 3.1 collective-permute-start.8
  35.1 12.9 %collective-permute-done.11.w1 = bf16[4,96,768]{2,1,0:T(8,128)(2,1)S(1)} collective-permute-done((bf16[4,96,768]{2,1,0:T(8,128)(2,1)S(1)}, bf16[4,96,768]{2,1,0:T(8,128)(2,1)S(1)}, u32[]{:S(2)}, u32[]{:S(2)}) %collective-permute-start.11) | collective-permute-done | bytes 589856 | tf_op jit(solution)/shard_map/ppermute | solution.py:1130
  57.4 2.5 collective-permute-done.13
  64.3 12.9 %collective-permute-done.19 = f32[2,2,4,4,24]{4,3,2,1,0:T(4,128)S(1)} collective-permute-done((f32[2,2,4,4,24]{4,3,2,1,0:T(4,128)S(1)}, f32[2,2,4,4,24]{4,3,2,1,0:T(4,128)S(1)}, u32[]{:S(2)}, u32[]{:S(2)}) %collective-permute-start.19) | collective-permute-done | bytes 6176 | tf_op jit(solution)/shard_map/ppermute | solution.py:1130
  84.3 11.9 %attention_forward.1 = (bf16[416,768]{1,0:T(8,128)(2,1)}, bf16[3,416,768]{2,1,0:T(8,128)(2,1)}, bf16[416,768]{1,0:T(8,128)(2,1)}, f32[416,768]{1,0:T(8,128)}, bf...) custom-call(s32[3]{0:T(128)} %pad_add_fusion.place, bf16[416,768]{1,0:T(8,128)(2,1)} %bitcast.284, ...), custom_call_target="tpu_custom_call" | custom-call | flops 2453667840 | bytes 16777216 | tf_op jit(solution)/shard_map/attention_forward/pallas_call | solution.py:980
  102.0 9.1 %collective-permute-done.29.refs_15_.refs_7_ = bf16[4,96,768]{2,1,0:T(8,128)(2,1)S(1)} collective-permute-done((bf16[4,96,768]{2,1,0:T(8,128)(2,1)S(1)}, bf16[4,96,768]{2,1,0:T(8,128)(2,1)S(1)}, u32[]{:S(2)}, u32[]{:S(2)}) %collective-permute-start.29) | collective-permute-done | bytes 589856 | tf_op jit(solution)/shard_map/ppermute | solution.py:1130
  111.2 5.0 collective-permute-done.31.refs_7_
  116.2 2.9 collective-permute-done.30.refs_17_
  121.4 13.8 %collective-permute-done.32.refs_10_.refs_2_ = bf16[4,96,768]{2,1,0:T(8,128)(2,1)S(1)} collective-permute-done((bf16[4,96,768]{2,1,0:T(8,128)(2,1)}, bf16[4,96,768]{2,1,0:T(8,128)(2,1)S(1)}, u32[]{:S(2)}, u32[]{:S(2)}) %collective-permute-start.32) | collective-permute-done | bytes 589856 | tf_op jit(solution)/shard_map/ppermute | solution.py:1130
  143.2 11.1 %collective-permute-done.37.refs_11_.refs_3_ = bf16[4,96,768]{2,1,0:T(8,128)(2,1)S(1)} collective-permute-done((bf16[4,96,768]{2,1,0:T(8,128)(2,1)}, bf16[4,96,768]{2,1,0:T(8,128)(2,1)S(1)}, u32[]{:S(2)}, u32[]{:S(2)}) %collective-permute-start.37) | collective-permute-done | bytes 589856 | tf_op jit(solution)/shard_map/ppermute | solution.py:1130
  161.3 48.4 %experts_pass.1 = (bf16[4,1792,768]{2,1,0:T(8,128)(2,1)}, bf16[4,1792,768]{2,1,0:T(8,128)(2,1)}, bf16[2,768,768]{2,1,0:T(8,128)(2,1)}, bf16[2,768,768]{2,1,0:T(8...) custom-call(s32[38]{0:T(128)} %pad_add_fusion.1.starts, ...), custom_call_target="tpu_custom_call" | custom-call | flops 15703474176 | bytes 62914560 | tf_op jit(solution)/shard_map/experts_pass/pallas_call | solution.py:831
  210.7 2.2 collective-permute-start.46
  212.9 20.1 %tokens_plain.1 = (bf16[4,416,768]{2,1,0:T(8,128)(2,1)}, bf16[4,416,768]{2,1,0:T(8,128)(2,1)}) custom-call(s32[38]{0:T(128)} %pad_add_fusion.1.starts, s32[4,8,416]{2,1,0:T(8,128)} %fusion.6.rank, f32[4,8,416]{2,1,0:T(8,128)} %fusion.23.gate, bf16[4,1792,768]{2,1,0:T(8,128)(2,1)} %get-tuple-element.847.acts, bf16[4,96,768]{2,1,0:T(8,128)(2,1)} %pad_maximum_fusion.10.refs_0_, ...), custom_call_target="tpu_custom_call" | custom-call | flops 7851737088 | bytes 31457280 | tf_op jit(solution)/shard_map/tokens_plain/pallas_call | solution.py:874
  233.1 3.3 collective-permute-done.46
  236.4 2.8 collective-permute-done.47
  239.1 2.8 collective-permute-start.48
  246.0 2.8 fusion.3
  255.3 21.2 %tokens_gated.1 = (bf16[4,416,768]{2,1,0:T(8,128)(2,1)}, bf16[4,416,768]{2,1,0:T(8,128)(2,1)}) custom-call(s32[38]{0:T(128)} %pad_add_fusion.1.starts, s32[4,8,416]{2,1,0:T(8,128)} %fusion.6.rank, f32[4,8,416]{2,1,0:T(8,128)} %fusion.23.gate, bf16[4,1792,768]{2,1,0:T(8,128)(2,1)} %get-tuple-element.886.acts, ...), custom_call_target="tpu_custom_call" | custom-call | flops 7851737088 | bytes 31457280 | tf_op jit(solution)/shard_map/tokens_gated/pallas_call | solution.py:874
  276.5 32.2 %collective-permute-done.52.second2 = bf16[416,768]{1,0:T(8,128)(2,1)} collective-permute-done((bf16[416,768]{1,0:T(8,128)(2,1)S(1)}, bf16[416,768]{1,0:T(8,128)(2,1)}, u32[]{:S(2)}, u32[]{:S(2)}) %collective-permute-start.52) | collective-permute-done | bytes 639008 | tf_op jit(solution)/shard_map/ppermute | solution.py:1175
  308.7 9.1 %push_rows.1 = (bf16[768,768]{1,0:T(8,128)(2,1)}, bf16[768,768]{1,0:T(8,128)(2,1)}, bf16[256,768]{1,0:T(8,128)(2,1)}, bf16[256,768]{1,0:T(8,128)(2,1)}, bf16[256...) custom-call(s32[3]{0:T(128)} %pad_add_fusion.place, ...), custom_call_target="tpu_custom_call" | custom-call | flops 11796480 | bytes 14155776 | tf_op jit(solution)/shard_map/push_rows/pallas_call | solution.py:578
  319.2 5.0 collective-permute-start.56
  327.7 26.5 %attention_backward.1 = (f32[416,768]{1,0:T(8,128)}, bf16[4,2,192,768]{3,2,1,0:T(8,128)(2,1)}, bf16[4,2,192,768]{3,2,1,0:T(8,128)(2,1)}, f32[8,768]{1,0:T(8,128)}) custom-call(s32[3]{0:T(128)} %pad_add_fusion.place, bf16[416,768]{1,0:T(8,128)(2,1)} %bitcast.285, bf16[416,768]{1,0:T(8,128)(2,1)} %bitcast.5.refs_24_.cots, ...), custom_call_target="tpu_custom_call" | custom-call | flops 9814671360 | bytes 25165824 | tf_op jit(solution)/shard_map/attention_backward/pallas_call | solution.py:1083
  357.1 3.2 fusion.34
  361.5 3.0 collective-permute-start.63
  366.8 2.5 reshape.244
  369.2 4.3 collective-permute-done.60.part0
  373.6 4.3 collective-permute-done.61.part1
  387.6 11.3 %collective-permute-done.67 = f32[4,768]{1,0:T(4,128)S(1)} collective-permute-done((f32[4,768]{1,0:T(4,128)S(1)}, f32[4,768]{1,0:T(4,128)S(1)}, u32[]{:S(2)}, u32[]{:S(2)}) %collective-permute-start.67) | collective-permute-done | bytes 12320 | tf_op jit(solution)/shard_map/ppermute | solution.py:1130
  410.2 5.8 %collective-permute-done.71 = f32[4,768]{1,0:T(4,128)S(1)} collective-permute-done((f32[4,768]{1,0:T(4,128)S(1)}, f32[4,768]{1,0:T(4,128)S(1)}, u32[]{:S(2)}, u32[]{:S(2)}) %collective-permute-start.71) | collective-permute-done | bytes 12320 | tf_op jit(solution)/shard_map/ppermute | solution.py:1130
  422.2 16.6 %wide_first.1 = (f32[768,768]{1,0:T(8,128)}, f32[768,768]{1,0:T(8,128)}) custom-call(bf16[768,768]{1,0:T(8,128)(2,1)} %get-tuple-element.1098.block0.refs_4_, bf16[768,768]{1,0:T(8,128)(2,1)} %collective-permute-done.55.block1, bf16[768,768]{1,0:T(8,128)(2,1)} %collective-permute-done.56.block3, bf16[256,768]{1,0:T(8,128)(2,1)} %copy-done.67, ...), custom_call_target="tpu_custom_call" | custom-call | flops 9059696640 | bytes 4718592 | tf_op jit(solution)/shard_map/wide_first/pallas_call | solution.py:456
  442.9 2.8 collective-permute-start.77
  445.8 13.4 %wide_last.1.refs_0_ = bf16[6,256,256]{2,1,0:T(8,128)(2,1)} custom-call(f32[768,768]{1,0:T(8,128)} %get-tuple-element.1045.gram_in, f32[768,768]{1,0:T(8,128)} %get-tuple-element.1046.whole_in), custom_call_target="tpu_custom_call" | custom-call | flops 9059696640 | bytes 4718592 | tf_op jit(solution)/shard_map/wide_last/pallas_call | solution.py:456
  459.3 2.2 collective-permute-start.78
  464.6 2.7 collective-permute-start.82
  470.9 10.3 %collective-permute-done.79.refs_3_ = bf16[6,256,256]{2,1,0:T(8,128)(2,1)S(1)} collective-permute-done((bf16[6,256,256]{2,1,0:T(8,128)(2,1)}, bf16[6,256,256]{2,1,0:T(8,128)(2,1)S(1)}, u32[]{:S(2)}, u32[]{:S(2)}) %collective-permute-start.79) | collective-permute-done | bytes 786464 | tf_op jit(solution)/shard_map/ppermute | solution.py:1161
  490.9 2.9 maximum_select_fusion.2
  493.8 7.1 %apply_mixers.1 = (bf16[2,2,96,768]{3,2,1,0:T(8,128)(2,1)}, bf16[2,2,96,768]{3,2,1,0:T(8,128)(2,1)}, bf16[2,2,96,768]{3,2,1,0:T(8,128)(2,1)}, bf16[2,2,96,768]{3,2,1,0:T(8,128)(2,1)}) custom-call(s32[3]{0:T(128)} %pad_add_fusion.place, bf16[6,256,256]{2,1,0:T(8,128)(2,1)} %wide_last.1.refs_0_, bf16[6,256,256]{2,1,0:T(8,128)(2,1)} %collective-permute-done.78.refs_1_, ...), custom_call_target="tpu_custom_call" | custom-call | flops 1811939328 | bytes 5898240 | tf_op jit(solution)/shard_map/apply_mixers/pallas_call | solution.py:524
  500.9 2.3 add_convert_fusion.3
  503.1 8.4 %collective-permute-start.86 = (bf16[416,768]{1,0:T(8,128)(2,1)}, bf16[416,768]{1,0:T(8,128)(2,1)}, u32[]{:S(2)}, u32[]{:S(2)}) collective-permute-start(bf16[416,768]{1,0:T(8,128)(2,1)} %add_convert_fusion.3), channel_id=1, source_target_pairs={{0,1},{1,2},{2,3},{3,0},{4,5},{5,6},{6,7},{7,4},{8,9},{9,10},{10,1... | collective-permute-start | bytes 1916936 | tf_op jit(solution)/shard_map/ppermute | solution.py:1140
  512.3 2.7 collective-permute-start.89
  515.0 18.0 %square_orthogonal.1 = bf16[768,768]{1,0:T(8,128)(2,1)} custom-call(bf16[768,768]{1,0:T(8,128)(2,1)} %bitcast.283), custom_call_target="tpu_custom_call" | custom-call | flops 13589544960 | bytes 2359296 | tf_op jit(solution)/shard_map/square_orthogonal/pallas_call | solution.py:626
  533.0 7.7 %collective-permute-done.88 = bf16[2,2,96,768]{3,2,1,0:T(8,128)(2,1)} collective-permute-done((bf16[2,2,96,768]{3,2,1,0:T(8,128)(2,1)}, bf16[2,2,96,768]{3,2,1,0:T(8,128)(2,1)}, u32[]{:S(2)}, u32[]{:S(2)}) %collective-permute-start.88) | collective-permute-done | bytes 589856 | tf_op jit(solution)/shard_map/ppermute | solution.py:1130
  557.7 6.0 %collective-permute-done.90 = bf16[416,768]{1,0:T(8,128)(2,1)S(1)} collective-permute-done((bf16[416,768]{1,0:T(8,128)(2,1)S(1)}, bf16[416,768]{1,0:T(8,128)(2,1)S(1)}, u32[]{:S(2)}, u32[]{:S(2)}) %collective-permute-start.90) | collective-permute-done | bytes 639008 | tf_op jit(solution)/shard_map/ppermute | solution.py:1140
  571.7 2.3 copy.92
  (441 shorter events, 159.3 us)
Async XLA Ops:
  3.3 24.7 %collective-permute-start.7 = (bf16[4,96,768]{2,1,0:T(8,128)(2,1)}, bf16[4,96,768]{2,1,0:T(8,128)(2,1)}, u32[]{:S(2)}, u32[]{:S(2)}) collective-permute-start(bf16[4,96,768]{2,1,0:T(8,128)(2,1)} %pad_maximum_fusion.10.refs_0_), channel_id=1, source_target_pairs={{0,4},{1,5},{2,6},{3,7},{4,0},{5,1},{6,2},{7,3},{8,12},{9,13},{10,... | collective-permute-start | bytes 1769480 | tf_op jit(solution)/shard_map/ppermute | solution.py:1130
  7.1 20.8 %collective-permute-start.3 = (bf16[4,96,768]{2,1,0:T(8,128)(2,1)}, bf16[4,96,768]{2,1,0:T(8,128)(2,1)}, u32[]{:S(2)}, u32[]{:S(2)}) collective-permute-start(bf16[4,96,768]{2,1,0:T(8,128)(2,1)} %pad_maximum_fusion.9.refs_8_.refs_0_), channel_id=1, source_target_pairs={{0,16},{1,17},{2,18},{3,19},{4,20},{5,21},{6,22},{7,23},{8,24},{9,... | collective-permute-start | bytes 1769480 | tf_op jit(solution)/shard_map/ppermute | solution.py:1130
  28.0 20.3 %collective-permute-start.9 = (bf16[2,4,96,768]{3,2,1,0:T(8,128)(2,1)}, bf16[2,4,96,768]{3,2,1,0:T(8,128)(2,1)}, u32[]{:S(2)}, u32[]{:S(2)}) collective-permute-start(bf16[2,4,96,768]{3,2,1,0:T(8,128)(2,1)} %pad_maximum_fusion.5), channel_id=1, source_target_pairs={{0,8},{1,9},{2,10},{3,11},{4,12},{5,13},{6,14},{7,15},{8,0},{9,1},... | collective-permute-start | bytes 3538952 | tf_op jit(solution)/shard_map/ppermute | solution.py:1126
  28.1 20.1 %collective-permute-start.8 = (bf16[416,768]{1,0:T(8,128)(2,1)}, bf16[416,768]{1,0:T(8,128)(2,1)}, u32[]{:S(2)}, u32[]{:S(2)}) collective-permute-start(bf16[416,768]{1,0:T(8,128)(2,1)} %bitcast.5.refs_24_.cots), channel_id=1, source_target_pairs={{0,1},{1,2},{2,3},{3,0},{4,5},{5,6},{6,7},{7,4},{8,9},{9,10},{10,1... | collective-permute-start | bytes 1916936 | tf_op jit(solution)/shard_map/ppermute | solution.py:1140
  60.4 19.0 %collective-permute-start.20 = (bf16[2,4,96,768]{3,2,1,0:T(8,128)(2,1)S(1)}, bf16[2,4,96,768]{3,2,1,0:T(8,128)(2,1)}, u32[]{:S(2)}, u32[]{:S(2)}) collective-permute-start(bf16[2,4,96,768]{3,2,1,0:T(8,128)(2,1)S(1)} %pad_maximum_fusion.7), channel_id=1, source_target_pairs={{0,8},{1,9},{2,10},{3,11},{4,12},{5,13},{6,14},{7,15},{8,0},{9,1},... | collective-permute-start | bytes 3538952 | tf_op jit(solution)/shard_map/ppermute | solution.py:1126
  61.2 18.2 %collective-permute-start.17 = (bf16[416,768]{1,0:T(8,128)(2,1)}, bf16[416,768]{1,0:T(8,128)(2,1)}, u32[]{:S(2)}, u32[]{:S(2)}) collective-permute-start(bf16[416,768]{1,0:T(8,128)(2,1)} %collective-permute-done.8.refs_25_), channel_id=1, source_target_pairs={{0,1},{1,2},{2,3},{3,0},{4,5},{5,6},{6,7},{7,4},{8,9},{9,10},{10,1... | collective-permute-start | bytes 1916936 | tf_op jit(solution)/shard_map/ppermute | solution.py:1140
  79.4 17.3 %collective-permute-start.22 = (bf16[416,768]{1,0:T(8,128)(2,1)}, bf16[416,768]{1,0:T(8,128)(2,1)}, u32[]{:S(2)}, u32[]{:S(2)}) collective-permute-start(bf16[416,768]{1,0:T(8,128)(2,1)} %collective-permute-done.17.refs_26_), channel_id=1, source_target_pairs={{0,1},{1,2},{2,3},{3,0},{4,5},{5,6},{6,7},{7,4},{8,9},{9,10},{10,1... | collective-permute-start | bytes 1916936 | tf_op jit(solution)/shard_map/ppermute | solution.py:1140
  79.4 17.3 %collective-permute-start.23 = (bf16[416,768]{1,0:T(8,128)(2,1)}, bf16[416,768]{1,0:T(8,128)(2,1)}, u32[]{:S(2)}, u32[]{:S(2)}) collective-permute-start(bf16[416,768]{1,0:T(8,128)(2,1)} %bitcast.5.refs_24_.cots), channel_id=1, source_target_pairs={{0,8},{1,9},{2,10},{3,11},{4,12},{5,13},{6,14},{7,15},{8,0},{9,1},... | collective-permute-start | bytes 1916936 | tf_op jit(solution)/shard_map/ppermute | solution.py:1126
  79.4 17.3 %collective-permute-start.24 = (bf16[416,768]{1,0:T(8,128)(2,1)}, bf16[416,768]{1,0:T(8,128)(2,1)}, u32[]{:S(2)}, u32[]{:S(2)}) collective-permute-start(bf16[416,768]{1,0:T(8,128)(2,1)} %collective-permute-done.8.refs_25_), channel_id=1, source_target_pairs={{0,8},{1,9},{2,10},{3,11},{4,12},{5,13},{6,14},{7,15},{8,0},{9,1},... | collective-permute-start | bytes 1916936 | tf_op jit(solution)/shard_map/ppermute | solution.py:1126
  79.9 16.4 %collective-permute-start.25 = (bf16[4,96,768]{2,1,0:T(8,128)(2,1)}, bf16[4,96,768]{2,1,0:T(8,128)(2,1)}, u32[]{:S(2)}, u32[]{:S(2)}) collective-permute-start(bf16[4,96,768]{2,1,0:T(8,128)(2,1)} %collective-permute-done.3.refs_12_.refs_4_), channel_id=1, source_target_pairs={{0,4},{1,5},{2,6},{3,7},{4,0},{5,1},{6,2},{7,3},{8,12},{9,13},{10,... | collective-permute-start | bytes 1769480 | tf_op jit(solution)/shard_map/ppermute | solution.py:1130
  100.0 16.1 %collective-permute-start.27 = (bf16[416,768]{1,0:T(8,128)(2,1)}, bf16[416,768]{1,0:T(8,128)(2,1)S(1)}, u32[]{:S(2)}, u32[]{:S(2)}) collective-permute-start(bf16[416,768]{1,0:T(8,128)(2,1)} %collective-permute-done.17.refs_26_), channel_id=1, source_target_pairs={{0,8},{1,9},{2,10},{3,11},{4,12},{5,13},{6,14},{7,15},{8,0},{9,1},... | collective-permute-start | bytes 1916936 | tf_op jit(solution)/shard_map/ppermute | solution.py:1126
  100.9 18.1 %collective-permute-start.30 = (bf16[416,768]{1,0:T(8,128)(2,1)S(1)}, bf16[416,768]{1,0:T(8,128)(2,1)S(1)}, u32[]{:S(2)}, u32[]{:S(2)}) collective-permute-start(bf16[416,768]{1,0:T(8,128)(2,1)S(1)} %copy-done.50), channel_id=1, source_target_pairs={{0,1},{1,2},{2,3},{3,0},{4,5},{5,6},{6,7},{7,4},{8,9},{9,10},{10,1... | collective-permute-start | bytes 1916936 | tf_op jit(solution)/shard_map/ppermute | solution.py:1140
  119.1 17.3 %collective-permute-start.34 = (bf16[416,768]{1,0:T(8,128)(2,1)S(1)}, bf16[416,768]{1,0:T(8,128)(2,1)S(1)}, u32[]{:S(2)}, u32[]{:S(2)}) collective-permute-start(bf16[416,768]{1,0:T(8,128)(2,1)S(1)} %collective-permute-done.30.refs_17_), channel_id=1, source_target_pairs={{0,1},{1,2},{2,3},{3,0},{4,5},{5,6},{6,7},{7,4},{8,9},{9,10},{10,1... | collective-permute-start | bytes 1916936 | tf_op jit(solution)/shard_map/ppermute | solution.py:1140
  119.1 17.2 %collective-permute-start.35 = (bf16[416,768]{1,0:T(8,128)(2,1)S(1)}, bf16[416,768]{1,0:T(8,128)(2,1)S(1)}, u32[]{:S(2)}, u32[]{:S(2)}) collective-permute-start(bf16[416,768]{1,0:T(8,128)(2,1)S(1)} %copy-done.50), channel_id=1, source_target_pairs={{0,8},{1,9},{2,10},{3,11},{4,12},{5,13},{6,14},{7,15},{8,0},{9,1},... | collective-permute-start | bytes 1916936 | tf_op jit(solution)/shard_map/ppermute | solution.py:1126
  136.4 19.1 %collective-permute-start.38 = (bf16[416,768]{1,0:T(8,128)(2,1)S(1)}, bf16[416,768]{1,0:T(8,128)(2,1)S(1)}, u32[]{:S(2)}, u32[]{:S(2)}) collective-permute-start(bf16[416,768]{1,0:T(8,128)(2,1)S(1)} %collective-permute-done.34.refs_18_), channel_id=1, source_target_pairs={{0,1},{1,2},{2,3},{3,0},{4,5},{5,6},{6,7},{7,4},{8,9},{9,10},{10,1... | collective-permute-start | bytes 1916936 | tf_op jit(solution)/shard_map/ppermute | solution.py:1140
  138.4 17.2 %collective-permute-start.40 = (bf16[416,768]{1,0:T(8,128)(2,1)S(1)}, bf16[416,768]{1,0:T(8,128)(2,1)S(1)}, u32[]{:S(2)}, u32[]{:S(2)}) collective-permute-start(bf16[416,768]{1,0:T(8,128)(2,1)S(1)} %collective-permute-done.34.refs_18_), channel_id=1, source_target_pairs={{0,8},{1,9},{2,10},{3,11},{4,12},{5,13},{6,14},{7,15},{8,0},{9,1},... | collective-permute-start | bytes 1916936 | tf_op jit(solution)/shard_map/ppermute | solution.py:1126
  138.4 17.1 %collective-permute-start.39 = (bf16[416,768]{1,0:T(8,128)(2,1)S(1)}, bf16[416,768]{1,0:T(8,128)(2,1)S(1)}, u32[]{:S(2)}, u32[]{:S(2)}) collective-permute-start(bf16[416,768]{1,0:T(8,128)(2,1)S(1)} %collective-permute-done.30.refs_17_), channel_id=1, source_target_pairs={{0,8},{1,9},{2,10},{3,11},{4,12},{5,13},{6,14},{7,15},{8,0},{9,1},... | collective-permute-start | bytes 1916936 | tf_op jit(solution)/shard_map/ppermute | solution.py:1126
  157.7 52.0 %collective-permute-start.43 = (bf16[4,96,768]{2,1,0:T(8,128)(2,1)}, bf16[4,96,768]{2,1,0:T(8,128)(2,1)S(1)}, u32[]{:S(2)}, u32[]{:S(2)}) collective-permute-start(bf16[4,96,768]{2,1,0:T(8,128)(2,1)} %get-tuple-element.820), channel_id=1, source_target_pairs={{0,4},{1,5},{2,6},{3,7},{4,0},{5,1},{6,2},{7,3},{8,12},{9,13},{10,... | collective-permute-start | bytes 1769480 | tf_op jit(solution)/shard_map/ppermute | solution.py:1130
  158.3 51.4 %collective-permute-start.44 = (bf16[4,96,768]{2,1,0:T(8,128)(2,1)}, bf16[4,96,768]{2,1,0:T(8,128)(2,1)S(1)}, u32[]{:S(2)}, u32[]{:S(2)}) collective-permute-start(bf16[4,96,768]{2,1,0:T(8,128)(2,1)} %get-tuple-element.821), channel_id=1, source_target_pairs={{0,16},{1,17},{2,18},{3,19},{4,20},{5,21},{6,22},{7,23},{8,24},{9,... | collective-permute-start | bytes 1769480 | tf_op jit(solution)/shard_map/ppermute | solution.py:1130
  159.2 50.6 %collective-permute-start.45 = (bf16[4,96,768]{2,1,0:T(8,128)(2,1)}, bf16[4,96,768]{2,1,0:T(8,128)(2,1)S(1)}, u32[]{:S(2)}, u32[]{:S(2)}) collective-permute-start(bf16[4,96,768]{2,1,0:T(8,128)(2,1)} %get-tuple-element.822), channel_id=1, source_target_pairs={{0,20},{1,21},{2,22},{3,23},{4,16},{5,17},{6,18},{7,19},{8,28},{9,... | collective-permute-start | bytes 1769480 | tf_op jit(solution)/shard_map/ppermute | solution.py:1130
  210.7 25.6 %collective-permute-start.46 = (bf16[768,768]{1,0:T(8,128)(2,1)}, bf16[768,768]{1,0:T(8,128)(2,1)S(1)}, u32[]{:S(2)}, u32[]{:S(2)}) collective-permute-start(bf16[768,768]{1,0:T(8,128)(2,1)} %get-tuple-element.834), channel_id=1, source_target_pairs={{0,4},{1,5},{2,6},{3,7},{4,0},{5,1},{6,2},{7,3},{8,12},{9,13},{10,... | collective-permute-start | bytes 3538952 | tf_op jit(solution)/shard_map/ppermute | solution.py:1130
  212.9 26.2 %collective-permute-start.47 = (bf16[768,768]{1,0:T(8,128)(2,1)}, bf16[768,768]{1,0:T(8,128)(2,1)}, u32[]{:S(2)}, u32[]{:S(2)}) collective-permute-start(bf16[768,768]{1,0:T(8,128)(2,1)} %get-tuple-element.835), channel_id=1, source_target_pairs={{0,16},{1,17},{2,18},{3,19},{4,20},{5,21},{6,22},{7,23},{8,24},{9,... | collective-permute-start | bytes 3538952 | tf_op jit(solution)/shard_map/ppermute | solution.py:1130
  248.7 59.9 %collective-permute-start.49 = (bf16[2,768,768]{2,1,0:T(8,128)(2,1)}, bf16[2,768,768]{2,1,0:T(8,128)(2,1)}, u32[]{:S(2)}, u32[]{:S(2)}) collective-permute-start(bf16[2,768,768]{2,1,0:T(8,128)(2,1)} %fusion.3), channel_id=1, source_target_pairs={{0,4},{1,5},{2,6},{3,7},{4,0},{5,1},{6,2},{7,3},{8,12},{9,13},{10,... | collective-permute-start | bytes 7077896 | tf_op jit(solution)/shard_map/ppermute | solution.py:1130
  248.7 59.9 %collective-permute-start.50 = (bf16[2,768,768]{2,1,0:T(8,128)(2,1)}, bf16[2,768,768]{2,1,0:T(8,128)(2,1)}, u32[]{:S(2)}, u32[]{:S(2)}) collective-permute-start(bf16[2,768,768]{2,1,0:T(8,128)(2,1)} %fusion.5), channel_id=1, source_target_pairs={{0,16},{1,17},{2,18},{3,19},{4,20},{5,21},{6,22},{7,23},{8,24},{9,... | collective-permute-start | bytes 7077896 | tf_op jit(solution)/shard_map/ppermute | solution.py:1130
  251.4 25.1 %collective-permute-start.51 = (bf16[416,768]{1,0:T(8,128)(2,1)}, bf16[416,768]{1,0:T(8,128)(2,1)}, u32[]{:S(2)}, u32[]{:S(2)}) collective-permute-start(bf16[416,768]{1,0:T(8,128)(2,1)} %get-tuple-element.1211), channel_id=1, source_target_pairs={{0,3},{1,0},{2,1},{3,2},{4,7},{5,4},{6,5},{7,6},{8,11},{9,8},{10,9... | collective-permute-start | bytes 1916936 | tf_op jit(solution)/shard_map/ppermute | solution.py:1175
  253.1 55.5 %collective-permute-start.52 = (bf16[416,768]{1,0:T(8,128)(2,1)S(1)}, bf16[416,768]{1,0:T(8,128)(2,1)}, u32[]{:S(2)}, u32[]{:S(2)}) collective-permute-start(bf16[416,768]{1,0:T(8,128)(2,1)S(1)} %get-tuple-element.1210), channel_id=1, source_target_pairs={{0,2},{1,3},{2,0},{3,1},{4,6},{5,7},{6,4},{7,5},{8,10},{9,11},{10,... | collective-permute-start | bytes 1916936 | tf_op jit(solution)/shard_map/ppermute | solution.py:1175
  253.3 55.4 %collective-permute-start.53 = (bf16[416,768]{1,0:T(8,128)(2,1)S(1)}, bf16[416,768]{1,0:T(8,128)(2,1)}, u32[]{:S(2)}, u32[]{:S(2)}) collective-permute-start(bf16[416,768]{1,0:T(8,128)(2,1)S(1)} %get-tuple-element.1209), channel_id=1, source_target_pairs={{0,1},{1,2},{2,3},{3,0},{4,5},{5,6},{6,7},{7,4},{8,9},{9,10},{10,1... | collective-permute-start | bytes 1916936 | tf_op jit(solution)/shard_map/ppermute | solution.py:1175
  317.9 36.4 %collective-permute-start.55 = (bf16[768,768]{1,0:T(8,128)(2,1)}, bf16[768,768]{1,0:T(8,128)(2,1)}, u32[]{:S(2)}, u32[]{:S(2)}) collective-permute-start(bf16[768,768]{1,0:T(8,128)(2,1)} %get-tuple-element.1099.refs_5_), channel_id=1, source_target_pairs={{1,0},{2,1},{5,4},{6,5},{11,10},{8,11},{15,14},{12,15},{17,16},{18... | collective-permute-start | bytes 3538952 | tf_op jit(solution)/shard_map/ppermute | solution.py:1156
  319.2 35.1 %collective-permute-start.56 = (bf16[768,768]{1,0:T(8,128)(2,1)}, bf16[768,768]{1,0:T(8,128)(2,1)}, u32[]{:S(2)}, u32[]{:S(2)}) collective-permute-start(bf16[768,768]{1,0:T(8,128)(2,1)} %get-tuple-element.1099.refs_5_), channel_id=1, source_target_pairs={{3,0},{0,1},{7,4},{4,5},{9,10},{10,11},{13,14},{14,15},{19,16},{16... | collective-permute-start | bytes 3538952 | tf_op jit(solution)/shard_map/ppermute | solution.py:1156
  324.1 30.1 %collective-permute-start.57 = (bf16[2,2,96,768]{3,2,1,0:T(8,128)(2,1)}, bf16[2,2,96,768]{3,2,1,0:T(8,128)(2,1)}, u32[]{:S(2)}, u32[]{:S(2)}) collective-permute-start(bf16[2,2,96,768]{3,2,1,0:T(8,128)(2,1)} %get-tuple-element.945), channel_id=1, source_target_pairs={{0,4},{1,5},{2,6},{3,7},{4,0},{5,1},{6,2},{7,3},{8,12},{9,13},{10,... | collective-permute-start | bytes 1769480 | tf_op jit(solution)/shard_map/ppermute | solution.py:1130
  325.8 28.5 %collective-permute-start.58 = (bf16[2,2,96,768]{3,2,1,0:T(8,128)(2,1)}, bf16[2,2,96,768]{3,2,1,0:T(8,128)(2,1)}, u32[]{:S(2)}, u32[]{:S(2)}) collective-permute-start(bf16[2,2,96,768]{3,2,1,0:T(8,128)(2,1)} %get-tuple-element.946), channel_id=1, source_target_pairs={{0,16},{1,17},{2,18},{3,19},{4,20},{5,21},{6,22},{7,23},{8,24},{9,... | collective-permute-start | bytes 1769480 | tf_op jit(solution)/shard_map/ppermute | solution.py:1130
  327.5 26.7 %collective-permute-start.59 = (bf16[2,2,96,768]{3,2,1,0:T(8,128)(2,1)}, bf16[2,2,96,768]{3,2,1,0:T(8,128)(2,1)}, u32[]{:S(2)}, u32[]{:S(2)}) collective-permute-start(bf16[2,2,96,768]{3,2,1,0:T(8,128)(2,1)} %get-tuple-element.947), channel_id=1, source_target_pairs={{0,20},{1,21},{2,22},{3,23},{4,16},{5,17},{6,18},{7,19},{8,28},{9,... | collective-permute-start | bytes 1769480 | tf_op jit(solution)/shard_map/ppermute | solution.py:1130
  354.3 23.6 %collective-permute-start.62 = (bf16[4,2,192,768]{3,2,1,0:T(8,128)(2,1)}, bf16[4,2,192,768]{3,2,1,0:T(8,128)(2,1)}, u32[]{:S(2)}, u32[]{:S(2)}) collective-permute-start(bf16[4,2,192,768]{3,2,1,0:T(8,128)(2,1)} %get-tuple-element.952), channel_id=1, source_target_pairs={{0,8},{1,9},{2,10},{3,11},{4,12},{5,13},{6,14},{7,15},{8,0},{9,1},... | collective-permute-start | bytes 7077896 | tf_op jit(solution)/shard_map/ppermute | solution.py:1126
  354.4 19.2 %collective-permute-start.60 = (bf16[256,768]{1,0:T(8,128)(2,1)}, bf16[256,768]{1,0:T(8,128)(2,1)S(1)}, u32[]{:S(2)}, u32[]{:S(2)}) collective-permute-start(bf16[256,768]{1,0:T(8,128)(2,1)} %get-tuple-element.949), channel_id=1, source_target_pairs={{2,0},{3,1},{6,4},{7,5},{8,10},{9,11},{12,14},{13,15},{18,16},{19,... | collective-permute-start | bytes 1179656 | tf_op jit(solution)/shard_map/ppermute | solution.py:1156
  355.7 22.2 %collective-permute-start.61 = (bf16[256,768]{1,0:T(8,128)(2,1)}, bf16[256,768]{1,0:T(8,128)(2,1)}, u32[]{:S(2)}, u32[]{:S(2)}) collective-permute-start(bf16[256,768]{1,0:T(8,128)(2,1)} %get-tuple-element.950), channel_id=1, source_target_pairs={{2,0},{3,1},{6,4},{7,5},{8,10},{9,11},{12,14},{13,15},{18,16},{19,... | collective-permute-start | bytes 1179656 | tf_op jit(solution)/shard_map/ppermute | solution.py:1156
  419.3 19.5 %collective-permute-start.72 = (bf16[4,32,768]{2,1,0:T(8,128)(2,1)S(1)}, bf16[4,32,768]{2,1,0:T(8,128)(2,1)S(1)}, u32[]{:S(2)}, u32[]{:S(2)}) collective-permute-start(bf16[4,32,768]{2,1,0:T(8,128)(2,1)S(1)} %get-tuple-element.1292), channel_id=1, source_target_pairs={{0,3},{1,0},{2,1},{3,2},{4,7},{5,4},{6,5},{7,6},{8,11},{9,8},{10,9... | collective-permute-start | bytes 589832 | tf_op jit(solution)/shard_map/ppermute | solution.py:1175
  419.4 19.4 %collective-permute-start.73 = (bf16[4,32,768]{2,1,0:T(8,128)(2,1)S(1)}, bf16[4,32,768]{2,1,0:T(8,128)(2,1)S(1)}, u32[]{:S(2)}, u32[]{:S(2)}) collective-permute-start(bf16[4,32,768]{2,1,0:T(8,128)(2,1)S(1)} %get-tuple-element.1293), channel_id=1, source_target_pairs={{0,2},{1,3},{2,0},{3,1},{4,6},{5,7},{6,4},{7,5},{8,10},{9,11},{10,... | collective-permute-start | bytes 589832 | tf_op jit(solution)/shard_map/ppermute | solution.py:1175
  420.3 18.5 %collective-permute-start.74 = (bf16[4,32,768]{2,1,0:T(8,128)(2,1)S(1)}, bf16[4,32,768]{2,1,0:T(8,128)(2,1)S(1)}, u32[]{:S(2)}, u32[]{:S(2)}) collective-permute-start(bf16[4,32,768]{2,1,0:T(8,128)(2,1)S(1)} %get-tuple-element.1291), channel_id=1, source_target_pairs={{0,1},{1,2},{2,3},{3,0},{4,5},{5,6},{6,7},{7,4},{8,9},{9,10},{10,1... | collective-permute-start | bytes 589832 | tf_op jit(solution)/shard_map/ppermute | solution.py:1175
  440.4 18.9 %collective-permute-start.75 = (bf16[4,24,768]{2,1,0:T(8,128)(2,1)S(1)}, bf16[4,24,768]{2,1,0:T(8,128)(2,1)S(1)}, u32[]{:S(2)}, u32[]{:S(2)}) collective-permute-start(bf16[4,24,768]{2,1,0:T(8,128)(2,1)S(1)} %pad_maximum_fusion.23), channel_id=1, source_target_pairs={{0,1},{1,2},{2,3},{3,0},{4,5},{5,6},{6,7},{7,4},{8,9},{9,10},{10,1... | collective-permute-start | bytes 442376 | tf_op jit(solution)/shard_map/ppermute | solution.py:1175
  441.2 18.1 %collective-permute-start.76 = (bf16[4,24,768]{2,1,0:T(8,128)(2,1)S(1)}, bf16[4,24,768]{2,1,0:T(8,128)(2,1)S(1)}, u32[]{:S(2)}, u32[]{:S(2)}) collective-permute-start(bf16[4,24,768]{2,1,0:T(8,128)(2,1)S(1)} %pad_maximum_fusion.23), channel_id=1, source_target_pairs={{0,2},{1,3},{2,0},{3,1},{4,6},{5,7},{6,4},{7,5},{8,10},{9,11},{10,... | collective-permute-start | bytes 442376 | tf_op jit(solution)/shard_map/ppermute | solution.py:1175
  442.9 16.4 %collective-permute-start.77 = (bf16[4,24,768]{2,1,0:T(8,128)(2,1)S(1)}, bf16[4,24,768]{2,1,0:T(8,128)(2,1)S(1)}, u32[]{:S(2)}, u32[]{:S(2)}) collective-permute-start(bf16[4,24,768]{2,1,0:T(8,128)(2,1)S(1)} %pad_maximum_fusion.23), channel_id=1, source_target_pairs={{0,3},{1,0},{2,1},{3,2},{4,7},{5,4},{6,5},{7,6},{8,11},{9,8},{10,9... | collective-permute-start | bytes 442376 | tf_op jit(solution)/shard_map/ppermute | solution.py:1175
  461.5 19.7 %collective-permute-start.79 = (bf16[6,256,256]{2,1,0:T(8,128)(2,1)}, bf16[6,256,256]{2,1,0:T(8,128)(2,1)S(1)}, u32[]{:S(2)}, u32[]{:S(2)}) collective-permute-start(bf16[6,256,256]{2,1,0:T(8,128)(2,1)} %wide_last.1.refs_0_), channel_id=1, source_target_pairs={{0,3},{1,0},{4,7},{5,4},{10,9},{11,10},{14,13},{15,14},{16,19},{17... | collective-permute-start | bytes 2359304 | tf_op jit(solution)/shard_map/ppermute | solution.py:1161
  503.1 37.6 %collective-permute-start.86 = (bf16[416,768]{1,0:T(8,128)(2,1)}, bf16[416,768]{1,0:T(8,128)(2,1)}, u32[]{:S(2)}, u32[]{:S(2)}) collective-permute-start(bf16[416,768]{1,0:T(8,128)(2,1)} %add_convert_fusion.3), channel_id=1, source_target_pairs={{0,1},{1,2},{2,3},{3,0},{4,5},{5,6},{6,7},{7,4},{8,9},{9,10},{10,1... | collective-permute-start | bytes 1916936 | tf_op jit(solution)/shard_map/ppermute | solution.py:1140
  511.5 21.5 %collective-permute-start.87 = (bf16[2,2,96,768]{3,2,1,0:T(8,128)(2,1)}, bf16[2,2,96,768]{3,2,1,0:T(8,128)(2,1)}, u32[]{:S(2)}, u32[]{:S(2)}) collective-permute-start(bf16[2,2,96,768]{3,2,1,0:T(8,128)(2,1)} %get-tuple-element.1116), channel_id=1, source_target_pairs={{0,4},{1,5},{2,6},{3,7},{4,0},{5,1},{6,2},{7,3},{8,12},{9,13},{10,... | collective-permute-start | bytes 1769480 | tf_op jit(solution)/shard_map/ppermute | solution.py:1130
  511.8 28.9 %collective-permute-start.88 = (bf16[2,2,96,768]{3,2,1,0:T(8,128)(2,1)}, bf16[2,2,96,768]{3,2,1,0:T(8,128)(2,1)}, u32[]{:S(2)}, u32[]{:S(2)}) collective-permute-start(bf16[2,2,96,768]{3,2,1,0:T(8,128)(2,1)} %get-tuple-element.1117), channel_id=1, source_target_pairs={{0,16},{1,17},{2,18},{3,19},{4,20},{5,21},{6,22},{7,23},{8,24},{9,... | collective-permute-start | bytes 1769480 | tf_op jit(solution)/shard_map/ppermute | solution.py:1130
  512.3 28.5 %collective-permute-start.89 = (bf16[2,2,96,768]{3,2,1,0:T(8,128)(2,1)}, bf16[2,2,96,768]{3,2,1,0:T(8,128)(2,1)}, u32[]{:S(2)}, u32[]{:S(2)}) collective-permute-start(bf16[2,2,96,768]{3,2,1,0:T(8,128)(2,1)} %get-tuple-element.1118), channel_id=1, source_target_pairs={{0,20},{1,21},{2,22},{3,23},{4,16},{5,17},{6,18},{7,19},{8,28},{9,... | collective-permute-start | bytes 1769480 | tf_op jit(solution)/shard_map/ppermute | solution.py:1130
  543.3 20.4 %collective-permute-start.94 = (bf16[4,2,96,768]{3,2,1,0:T(8,128)(2,1)S(1)}, bf16[4,2,96,768]{3,2,1,0:T(8,128)(2,1)S(1)}, u32[]{:S(2)}, u32[]{:S(2)}) collective-permute-start(bf16[4,2,96,768]{3,2,1,0:T(8,128)(2,1)S(1)} %get-tuple-element.1213), channel_id=1, source_target_pairs={{0,8},{1,9},{2,10},{3,11},{4,12},{5,13},{6,14},{7,15},{8,0},{9,1},... | collective-permute-start | bytes 3538952 | tf_op jit(solution)/shard_map/ppermute | solution.py:1126
  545.4 18.3 %collective-permute-start.90 = (bf16[416,768]{1,0:T(8,128)(2,1)S(1)}, bf16[416,768]{1,0:T(8,128)(2,1)S(1)}, u32[]{:S(2)}, u32[]{:S(2)}) collective-permute-start(bf16[416,768]{1,0:T(8,128)(2,1)S(1)} %add_convert_fusion.2), channel_id=1, source_target_pairs={{0,1},{1,2},{2,3},{3,0},{4,5},{5,6},{6,7},{7,4},{8,9},{9,10},{10,1... | collective-permute-start | bytes 1916936 | tf_op jit(solution)/shard_map/ppermute | solution.py:1140
  (115 other events, 1001.6 us)

commit v3 on v2

--- a/solution.py
+++ b/solution.py
@@ -665,6 +665,26 @@
         whole[pl.ds(pl.multiple_of(row * depth, 16), depth), :] = piece[0]
 
 
+def each_band(count, work):
+    wide = (count + 127) // 512
+
+    def step(place, carry):
+        work(pl.ds(pl.multiple_of(place * 512, 512), 512))
+        return carry
+
+    lax.fori_loop(0, wide, step, 0)
+    rest = count - wide * 512
+    start = wide * 512
+
+    @pl.when(rest > 128)
+    def _():
+        work(pl.ds(pl.multiple_of(start, 512), 256))
+
+    @pl.when(jnp.logical_or(rest > 256, jnp.logical_and(rest > 0, rest <= 128)))
+    def _():
+        work(pl.ds(pl.multiple_of(start + jnp.where(rest > 256, 256, 0), 128), 128))
+
+
 def gate_of(hot, gate):
     return jnp.sum(jnp.where(hot, gate, 0.0), axis=1, keepdims=True)
 
@@ -721,8 +741,7 @@
     upper_sum[...] = jnp.zeros_like(upper_sum)
     lower_sum[...] = jnp.zeros_like(lower_sum)
 
-    def work(tile, carry):
-        band = pl.ds(pl.multiple_of(tile * TILE, TILE), TILE)
+    def work(band):
         slot_rows, slot_grads = slots[band, :], grads[band, :]
         hidden, slope = gelu_pair(dot_nn(slot_rows, upper[...]))
         hidden = hidden.astype(low)
@@ -731,9 +750,8 @@
         before_out[0, band, :] = d_before
         upper_sum[...] += dot_tn(slot_rows, d_before)
         lower_sum[...] += dot_tn(slot_grads, hidden)
-        return carry
-
-    lax.fori_loop(0, (starts[base + blocks] + TILE - 1) // TILE, work, 0)
+
+    each_band(starts[base + blocks], work)
 
     for turn, target in enumerate(targets):
 
@@ -773,12 +791,10 @@
 
     assemble(chip, core, pieces, whole)
 
-    def work(tile, carry):
-        band = pl.ds(pl.multiple_of(tile * TILE, TILE), TILE)
+    def work(band):
         moved[expert, band, :] = dot_nt(acts[0, band, :], whole[...]).astype(low)
-        return carry
-
-    lax.fori_loop(0, (starts[base + blocks] + TILE - 1) // TILE, work, 0)
+
+    each_band(starts[base + blocks], work)
 
     @pl.when(expert == count - 1)
     def _():
@@ -1440,6 +1456,7 @@
     shape = (4, 2, 2, tps, rows_attn, features)
     v.gone = swap_core(v.gone)
     v.blocks[:2] = [to_worker(block, 2) for block in v.blocks[:2]]
+    v.rows = rows_between(v.rows)
     vectors = v.vectors[:4]
     v.vectors = [vectors, swap_core(vectors)]
     v.input_grad = v.input_grad.reshape(seqs, IMAGE, features)[:, :LEN].reshape(rows_here, features)
@@ -1456,7 +1473,7 @@
 
     v.first = [first_part(x_here), swap_chip(first_part(1 - x_here).astype(low), 1)]
     v.last = [last_part(y_here), swap_chip(last_part(1 - y_here).astype(low), 2)]
-    v.mixed.append(pass_on(v.mixed[1]))
+    v.mixed.append(pass_by(v.mixed[2], -1))
     vectors = sum(v.vectors)
     v.vectors = [vectors, swap_chip(vectors, 1)]
     v = hold(v)
@@ -1491,13 +1508,17 @@
     column = by_tp(v.drop.column, tp).transpose(1, 0, 2, 3)
     gone = relative(column, chip)
     v.pushes = [gone[0]] + [swap_chip(gone[turn], turn) for turn in range(1, 4)]
+    upward_grad, downward_grad = rows_in(*v.drop.rows)
+    v.states = [
+        (upward_grad, advance(upward_grad, upward_moment)[0]),
+        (downward_grad, advance(downward_grad, downward_moment)[0]),
+    ]
     v.mixers.append(from_worker(v.mixers[0], 1))
     v.mixers.append(from_worker(v.mixers[0], -1))
     v = hold(v)
     pushes = place_chips(v.pushes, chip)
     v.pushes = [pushes, swap_core(pushes)]
     v.mixers.insert(2, from_worker(v.mixers[1], 2))
-    v.rows = rows_between(v.rows)
     v = hold(v)
     pushes = place_cores(*v.drop.pushes, core)
     pushes = pushes.reshape(2, 2, 2, tps, rows_attn, features).transpose(1, 0, 2, 3, 4, 5)
@@ -1506,7 +1527,8 @@
     v = hold(v)
 
     v.new = rows_out(v.new)
-    v.mixed[4] = pass_on(added(v.mixed[2], v.mixed[4]).astype(low))
+    own_part, next_part, unused, far_part, got = v.mixed
+    v.mixed = [own_part, pass_by(added(next_part, got).astype(low), -1), pass_on(far_part)]
     v.moved = orthogonal_square(v.drop.pushes)
     v = hold(v)
     moved = v.drop.moved.reshape(2, 2, 2, tps, rows_attn, features)
@@ -1514,15 +1536,9 @@
     gone = relative(moved, chip)
     v.moved = [gone[0]] + [swap_chip(gone[turn], turn) for turn in range(1, 4)]
     v.new = rows_between(v.new)
-    upward_grad, downward_grad = rows_in(*v.drop.rows)
-    v.states = [
-        (upward_grad, advance(upward_grad, upward_moment)[0]),
-        (downward_grad, advance(downward_grad, downward_moment)[0]),
-    ]
-    v.mixed[4] = pass_on(added(v.mixed[3], v.mixed[4]).astype(low))
     v = hold(v)
     mixed = v.drop.mixed
-    result = (residual + added(mixed[0], mixed[4])).astype(low)
+    result = (residual + mixed[0] + added(mixed[1], mixed[2])).astype(low)
     result = result.reshape(seqs, IMAGE, features)[:, :LEN].reshape(rows_here, features)
     input_grad = v.input_grad
     scales_grad, shifts_grad = v.vectors[:2], v.vectors[2:]

time: 584 us -> 570 us (0.976)
  waiting for transfers between devices: 179 us -> 160 us
    ppermute x15 -> x17, starting transfers between devices: 22.7 us -> 36.1 us  [pass_by(): lax.ppermute(value, axes, route_to(lambda s, c, t: (s, c, t + steps)))]
    ppermute x9 -> x7, starting transfers between devices: 13.9 us -> 5.25 us  [pass_on(): return lax.ppermute(value, axes, route_to(lambda s, c, t: (s, c, t + 1)))]
    ppermute x9 -> x7, waiting for transfers between devices: 12.8 us -> 5.7 us  [pass_on(): return lax.ppermute(value, axes, route_to(lambda s, c, t: (s, c, t + 1)))]
    ppermute x3, waiting for transfers between devices: 10.4 us -> 4.4 us  [from_worker(): lax.ppermute(value, axes, worker_route(lambda w: w + turn - step, lambda...]
    ppermute x15 -> x17, waiting for transfers between devices: 36.1 us -> 36.5 us  [pass_by(): lax.ppermute(value, axes, route_to(lambda s, c, t: (s, c, t + steps)))]
  transfers between devices with their start and end apart: 95 -> 95, of which waited for: 35 -> 34; matrix products, arithmetic and copies ran while one was open for 9% -> 9% of each run, Pallas kernels for 32% -> 34%
where the time goes in v3:
time: 570 us; the launch traced here: 560 us
  Pallas kernels  195 us (34%)
  waiting for transfers between devices  160 us (28%)
  starting transfers between devices  112 us (20%)
  other arithmetic  48.6 us (9%)
  local copies, waits for them, and re-layouts  41.1 us (7%)
    ppermute x43, waiting for transfers between devices, swap_chip(): lax.ppermute(value, axes, route_to(lambda s, c, t: (s ^ turn & 2, c ^ tur...  99.3 us
    pallas_call x1, Pallas kernels, experts_pass(): pl.pallas_call(experts_kernel, grid_spec=pltpu.PrefetchScalarGridSpec(num...  50.4 us
    ppermute x43, starting transfers between devices, swap_chip(): lax.ppermute(value, axes, route_to(lambda s, c, t: (s ^ turn & 2, c ^ tur...  48.7 us
    pallas_call x2, Pallas kernels, tokens_pass(): pl.pallas_call(functools.partial(tokens_kernel, gated), grid_spec=pltpu.P...  41.6 us
    ppermute x17, waiting for transfers between devices, pass_by(): lax.ppermute(value, axes, route_to(lambda s, c, t: (s, c, t + steps)))  36.5 us
    ppermute x17, starting transfers between devices, pass_by(): lax.ppermute(value, axes, route_to(lambda s, c, t: (s, c, t + steps)))  36.1 us
    pallas_call x2, Pallas kernels, wide_call(): pl.pallas_call(kernel, out_shape=out_shape, in_specs=[vmem] * len(inputs)...  30.1 us
    pallas_call x1, Pallas kernels, attention_backward(): pl.pallas_call(backward_kernel, in_specs=[pl.BlockSpec(memory_space=pltpu...  27.1 us
  transfers between devices with their start and end apart: 95, of which 34 were waited for; matrix products, arithmetic and copies ran while one was open for 9% of the time, Pallas kernels for 34%

profile of v3, /device:TPU:0, one launch (start us, length us, event | category | flops | bytes accessed | tf_op | source)
XLA Modules:
  0.0 559.9 jit_solution(17295991112243401771)
XLA Ops:
  3.3 2.9 collective-permute-start.7
  10.5 2.6 collective-permute-start.5
  15.8 2.0 collective-permute-start.1
  18.5 2.3 collective-permute-start.2
  24.1 3.8 collective-permute-done.1
  28.1 3.1 collective-permute-start.8
  35.1 12.9 %collective-permute-done.11.w1 = bf16[4,96,768]{2,1,0:T(8,128)(2,1)S(1)} collective-permute-done((bf16[4,96,768]{2,1,0:T(8,128)(2,1)S(1)}, bf16[4,96,768]{2,1,0:T(8,128)(2,1)S(1)}, u32[]{:S(2)}, u32[]{:S(2)}) %collective-permute-start.11) | collective-permute-done | bytes 589856 | tf_op jit(solution)/shard_map/ppermute | solution.py:1146
  55.7 4.2 collective-permute-done.13
  64.6 13.4 %collective-permute-done.19 = f32[2,2,4,4,24]{4,3,2,1,0:T(4,128)S(1)} collective-permute-done((f32[2,2,4,4,24]{4,3,2,1,0:T(4,128)S(1)}, f32[2,2,4,4,24]{4,3,2,1,0:T(4,128)S(1)}, u32[]{:S(2)}, u32[]{:S(2)}) %collective-permute-start.19) | collective-permute-done | bytes 6176 | tf_op jit(solution)/shard_map/ppermute | solution.py:1146
  85.4 11.9 %attention_forward.1 = (bf16[416,768]{1,0:T(8,128)(2,1)}, bf16[3,416,768]{2,1,0:T(8,128)(2,1)}, bf16[416,768]{1,0:T(8,128)(2,1)}, f32[416,768]{1,0:T(8,128)}, bf...) custom-call(s32[3]{0:T(128)} %pad_add_fusion.place, bf16[416,768]{1,0:T(8,128)(2,1)} %bitcast.285, ...), custom_call_target="tpu_custom_call" | custom-call | flops 2453667840 | bytes 16777216 | tf_op jit(solution)/shard_map/attention_forward/pallas_call | solution.py:996
  103.8 9.1 %collective-permute-done.29.refs_15_.refs_7_ = bf16[4,96,768]{2,1,0:T(8,128)(2,1)S(1)} collective-permute-done((bf16[4,96,768]{2,1,0:T(8,128)(2,1)}, bf16[4,96,768]{2,1,0:T(8,128)(2,1)S(1)}, u32[]{:S(2)}, u32[]{:S(2)}) %collective-permute-start.29) | collective-permute-done | bytes 589856 | tf_op jit(solution)/shard_map/ppermute | solution.py:1146
  112.9 4.6 collective-permute-done.31.refs_7_
  117.5 2.6 collective-permute-done.30.refs_17_
  123.2 13.0 %collective-permute-done.32.refs_10_.refs_2_ = bf16[4,96,768]{2,1,0:T(8,128)(2,1)S(1)} collective-permute-done((bf16[4,96,768]{2,1,0:T(8,128)(2,1)}, bf16[4,96,768]{2,1,0:T(8,128)(2,1)S(1)}, u32[]{:S(2)}, u32[]{:S(2)}) %collective-permute-start.32) | collective-permute-done | bytes 589856 | tf_op jit(solution)/shard_map/ppermute | solution.py:1146
  144.0 10.9 %collective-permute-done.37.refs_11_.refs_3_ = bf16[4,96,768]{2,1,0:T(8,128)(2,1)S(1)} collective-permute-done((bf16[4,96,768]{2,1,0:T(8,128)(2,1)S(1)}, bf16[4,96,768]{2,1,0:T(8,128)(2,1)S(1)}, u32[]{:S(2)}, u32[]{:S(2)}) %collective-permute-start.37) | collective-permute-done | bytes 589856 | tf_op jit(solution)/shard_map/ppermute | solution.py:1146
  156.2 2.1 collective-permute-done.42.refs_23_
  159.8 2.0 collective-permute-start.45
  161.8 50.4 %experts_pass.1 = (bf16[4,1792,768]{2,1,0:T(8,128)(2,1)}, bf16[4,1792,768]{2,1,0:T(8,128)(2,1)}, bf16[2,768,768]{2,1,0:T(8,128)(2,1)}, bf16[2,768,768]{2,1,0:T(8...) custom-call(s32[38]{0:T(128)} %pad_add_fusion.1.starts, ...), custom_call_target="tpu_custom_call" | custom-call | flops 15703474176 | bytes 62914560 | tf_op jit(solution)/shard_map/experts_pass/pallas_call | solution.py:847
  215.7 20.4 %tokens_plain.1 = (bf16[4,416,768]{2,1,0:T(8,128)(2,1)}, bf16[4,416,768]{2,1,0:T(8,128)(2,1)}) custom-call(s32[38]{0:T(128)} %pad_add_fusion.1.starts, s32[4,8,416]{2,1,0:T(8,128)} %fusion.6.rank, f32[4,8,416]{2,1,0:T(8,128)} %fusion.23.gate, bf16[4,1792,768]{2,1,0:T(8,128)(2,1)} %get-tuple-element.844.acts, bf16[4,96,768]{2,1,0:T(8,128)(2,1)} %pad_maximum_fusion.10.refs_0_, ...), custom_call_target="tpu_custom_call" | custom-call | flops 7851737088 | bytes 31457280 | tf_op jit(solution)/shard_map/tokens_plain/pallas_call | solution.py:890
  241.6 2.8 fusion.3
  248.8 2.5 collective-permute-start.51
  253.1 21.2 %tokens_gated.1 = (bf16[4,416,768]{2,1,0:T(8,128)(2,1)}, bf16[4,416,768]{2,1,0:T(8,128)(2,1)}) custom-call(s32[38]{0:T(128)} %pad_add_fusion.1.starts, s32[4,8,416]{2,1,0:T(8,128)} %fusion.6.rank, f32[4,8,416]{2,1,0:T(8,128)} %fusion.23.gate, bf16[4,1792,768]{2,1,0:T(8,128)(2,1)} %get-tuple-element.883.acts, ...), custom_call_target="tpu_custom_call" | custom-call | flops 7851737088 | bytes 31457280 | tf_op jit(solution)/shard_map/tokens_gated/pallas_call | solution.py:890
  274.4 32.6 %collective-permute-done.52.second2 = bf16[416,768]{1,0:T(8,128)(2,1)} collective-permute-done((bf16[416,768]{1,0:T(8,128)(2,1)}, bf16[416,768]{1,0:T(8,128)(2,1)}, u32[]{:S(2)}, u32[]{:S(2)}) %collective-permute-start.52) | collective-permute-done | bytes 639008 | tf_op jit(solution)/shard_map/ppermute | solution.py:1191
  307.1 9.1 %push_rows.1 = (bf16[768,768]{1,0:T(8,128)(2,1)}, bf16[768,768]{1,0:T(8,128)(2,1)}, bf16[256,768]{1,0:T(8,128)(2,1)}, bf16[256,768]{1,0:T(8,128)(2,1)}, bf16[256...) custom-call(s32[3]{0:T(128)} %pad_add_fusion.place, ...), custom_call_target="tpu_custom_call" | custom-call | flops 11796480 | bytes 14155776 | tf_op jit(solution)/shard_map/push_rows/pallas_call | solution.py:578
  317.5 4.6 collective-permute-start.56
  325.6 27.1 %attention_backward.1 = (f32[416,768]{1,0:T(8,128)}, bf16[4,2,192,768]{3,2,1,0:T(8,128)(2,1)}, bf16[4,2,192,768]{3,2,1,0:T(8,128)(2,1)}, f32[8,768]{1,0:T(8,128)}) custom-call(s32[3]{0:T(128)} %pad_add_fusion.place, bf16[416,768]{1,0:T(8,128)(2,1)} %bitcast.286, bf16[416,768]{1,0:T(8,128)(2,1)} %bitcast.5.refs_24_.cots, ...), custom_call_target="tpu_custom_call" | custom-call | flops 9814671360 | bytes 25165824 | tf_op jit(solution)/shard_map/attention_backward/pallas_call | solution.py:1099
  359.3 3.2 fusion.34
  363.9 3.8 collective-permute-start.64
  369.9 2.5 reshape.244
  372.4 3.5 collective-permute-done.60.part0
  375.9 4.2 collective-permute-done.61.part1
  380.1 1.9 constant_dynamic-slice_fusion.18
  390.2 12.9 %collective-permute-done.68 = f32[4,768]{1,0:T(4,128)S(1)} collective-permute-done((f32[4,768]{1,0:T(4,128)S(1)}, f32[4,768]{1,0:T(4,128)S(1)}, u32[]{:S(2)}, u32[]{:S(2)}) %collective-permute-start.68) | collective-permute-done | bytes 12320 | tf_op jit(solution)/shard_map/ppermute | solution.py:1146
  412.8 5.0 collective-permute-done.72
  422.5 2.0 collective-permute-start.75
  424.5 16.6 %wide_first.1 = (f32[768,768]{1,0:T(8,128)}, f32[768,768]{1,0:T(8,128)}) custom-call(bf16[768,768]{1,0:T(8,128)(2,1)} %get-tuple-element.1085.block0.refs_4_, bf16[768,768]{1,0:T(8,128)(2,1)} %collective-permute-done.55.block1, bf16[768,768]{1,0:T(8,128)(2,1)} %collective-permute-done.56.block3, bf16[256,768]{1,0:T(8,128)(2,1)} %collective-permute-done.60.part0, ...), custom_call_target="tpu_custom_call" | custom-call | flops 9059696640 | bytes 4718592 | tf_op jit(solution)/shard_map/wide_first/pallas_call | solution.py:456
  448.4 2.8 collective-permute-start.78
  451.3 13.5 %wide_last.1.refs_0_ = bf16[6,256,256]{2,1,0:T(8,128)(2,1)} custom-call(f32[768,768]{1,0:T(8,128)} %get-tuple-element.1036.gram_in, f32[768,768]{1,0:T(8,128)} %get-tuple-element.1037.whole_in), custom_call_target="tpu_custom_call" | custom-call | flops 9059696640 | bytes 4718592 | tf_op jit(solution)/shard_map/wide_last/pallas_call | solution.py:456
  466.2 1.9 collective-permute-start.80
  468.1 2.1 convert_bitcast_fusion.1
  481.3 4.4 collective-permute-done.80.refs_3_
  490.9 7.2 %apply_mixers.1 = (bf16[2,2,96,768]{3,2,1,0:T(8,128)(2,1)}, bf16[2,2,96,768]{3,2,1,0:T(8,128)(2,1)}, bf16[2,2,96,768]{3,2,1,0:T(8,128)(2,1)}, bf16[2,2,96,768]{3,2,1,0:T(8,128)(2,1)}) custom-call(s32[3]{0:T(128)} %pad_add_fusion.place, bf16[6,256,256]{2,1,0:T(8,128)(2,1)} %wide_last.1.refs_0_, bf16[6,256,256]{2,1,0:T(8,128)(2,1)} %copy-done.63, ...), custom_call_target="tpu_custom_call" | custom-call | flops 1811939328 | bytes 5898240 | tf_op jit(solution)/shard_map/apply_mixers/pallas_call | solution.py:524
  498.2 13.0 %collective-permute-start.86 = (bf16[416,768]{1,0:T(8,128)(2,1)S(1)}, bf16[416,768]{1,0:T(8,128)(2,1)S(1)}, u32[]{:S(2)}, u32[]{:S(2)}) collective-permute-start(bf16[416,768]{1,0:T(8,128)(2,1)S(1)} %add_convert_fusion.2), channel_id=1, source_target_pairs={{0,3},{1,0},{2,1},{3,2},{4,7},{5,4},{6,5},{7,6},{8,11},{9,8},{10,9... | collective-permute-start | bytes 1916936 | tf_op jit(solution)/shard_map/ppermute | solution.py:1191
  514.8 18.0 %square_orthogonal.1 = bf16[768,768]{1,0:T(8,128)(2,1)} custom-call(bf16[768,768]{1,0:T(8,128)(2,1)} %bitcast.284), custom_call_target="tpu_custom_call" | custom-call | flops 13589544960 | bytes 2359296 | tf_op jit(solution)/shard_map/square_orthogonal/pallas_call | solution.py:626
  532.8 3.6 collective-permute-done.90
  536.4 2.0 pad_maximum_fusion.3
  545.0 2.4 collective-permute-done.93
  556.6 2.3 copy.92
  (468 shorter events, 154.1 us)
Async XLA Ops:
  3.3 24.7 %collective-permute-start.7 = (bf16[4,96,768]{2,1,0:T(8,128)(2,1)}, bf16[4,96,768]{2,1,0:T(8,128)(2,1)}, u32[]{:S(2)}, u32[]{:S(2)}) collective-permute-start(bf16[4,96,768]{2,1,0:T(8,128)(2,1)} %pad_maximum_fusion.10.refs_0_), channel_id=1, source_target_pairs={{0,4},{1,5},{2,6},{3,7},{4,0},{5,1},{6,2},{7,3},{8,12},{9,13},{10,... | collective-permute-start | bytes 1769480 | tf_op jit(solution)/shard_map/ppermute | solution.py:1146
  7.1 20.8 %collective-permute-start.3 = (bf16[4,96,768]{2,1,0:T(8,128)(2,1)}, bf16[4,96,768]{2,1,0:T(8,128)(2,1)}, u32[]{:S(2)}, u32[]{:S(2)}) collective-permute-start(bf16[4,96,768]{2,1,0:T(8,128)(2,1)} %pad_maximum_fusion.9.refs_8_.refs_0_), channel_id=1, source_target_pairs={{0,16},{1,17},{2,18},{3,19},{4,20},{5,21},{6,22},{7,23},{8,24},{9,... | collective-permute-start | bytes 1769480 | tf_op jit(solution)/shard_map/ppermute | solution.py:1146
  28.0 20.3 %collective-permute-start.9 = (bf16[2,4,96,768]{3,2,1,0:T(8,128)(2,1)}, bf16[2,4,96,768]{3,2,1,0:T(8,128)(2,1)}, u32[]{:S(2)}, u32[]{:S(2)}) collective-permute-start(bf16[2,4,96,768]{3,2,1,0:T(8,128)(2,1)} %pad_maximum_fusion.5), channel_id=1, source_target_pairs={{0,8},{1,9},{2,10},{3,11},{4,12},{5,13},{6,14},{7,15},{8,0},{9,1},... | collective-permute-start | bytes 3538952 | tf_op jit(solution)/shard_map/ppermute | solution.py:1142
  28.1 20.1 %collective-permute-start.8 = (bf16[416,768]{1,0:T(8,128)(2,1)}, bf16[416,768]{1,0:T(8,128)(2,1)}, u32[]{:S(2)}, u32[]{:S(2)}) collective-permute-start(bf16[416,768]{1,0:T(8,128)(2,1)} %bitcast.5.refs_24_.cots), channel_id=1, source_target_pairs={{0,1},{1,2},{2,3},{3,0},{4,5},{5,6},{6,7},{7,4},{8,9},{9,10},{10,1... | collective-permute-start | bytes 1916936 | tf_op jit(solution)/shard_map/ppermute | solution.py:1156
  61.5 18.9 %collective-permute-start.20 = (bf16[2,4,96,768]{3,2,1,0:T(8,128)(2,1)}, bf16[2,4,96,768]{3,2,1,0:T(8,128)(2,1)}, u32[]{:S(2)}, u32[]{:S(2)}) collective-permute-start(bf16[2,4,96,768]{3,2,1,0:T(8,128)(2,1)} %pad_maximum_fusion.7), channel_id=1, source_target_pairs={{0,8},{1,9},{2,10},{3,11},{4,12},{5,13},{6,14},{7,15},{8,0},{9,1},... | collective-permute-start | bytes 3538952 | tf_op jit(solution)/shard_map/ppermute | solution.py:1142
  61.5 18.9 %collective-permute-start.17 = (bf16[416,768]{1,0:T(8,128)(2,1)}, bf16[416,768]{1,0:T(8,128)(2,1)}, u32[]{:S(2)}, u32[]{:S(2)}) collective-permute-start(bf16[416,768]{1,0:T(8,128)(2,1)} %collective-permute-done.8.refs_25_), channel_id=1, source_target_pairs={{0,1},{1,2},{2,3},{3,0},{4,5},{5,6},{6,7},{7,4},{8,9},{9,10},{10,1... | collective-permute-start | bytes 1916936 | tf_op jit(solution)/shard_map/ppermute | solution.py:1156
  80.4 18.1 %collective-permute-start.22 = (bf16[416,768]{1,0:T(8,128)(2,1)}, bf16[416,768]{1,0:T(8,128)(2,1)}, u32[]{:S(2)}, u32[]{:S(2)}) collective-permute-start(bf16[416,768]{1,0:T(8,128)(2,1)} %collective-permute-done.17.refs_26_), channel_id=1, source_target_pairs={{0,1},{1,2},{2,3},{3,0},{4,5},{5,6},{6,7},{7,4},{8,9},{9,10},{10,1... | collective-permute-start | bytes 1916936 | tf_op jit(solution)/shard_map/ppermute | solution.py:1156
  80.4 18.1 %collective-permute-start.23 = (bf16[416,768]{1,0:T(8,128)(2,1)}, bf16[416,768]{1,0:T(8,128)(2,1)}, u32[]{:S(2)}, u32[]{:S(2)}) collective-permute-start(bf16[416,768]{1,0:T(8,128)(2,1)} %bitcast.5.refs_24_.cots), channel_id=1, source_target_pairs={{0,8},{1,9},{2,10},{3,11},{4,12},{5,13},{6,14},{7,15},{8,0},{9,1},... | collective-permute-start | bytes 1916936 | tf_op jit(solution)/shard_map/ppermute | solution.py:1142
  80.4 18.1 %collective-permute-start.24 = (bf16[416,768]{1,0:T(8,128)(2,1)}, bf16[416,768]{1,0:T(8,128)(2,1)}, u32[]{:S(2)}, u32[]{:S(2)}) collective-permute-start(bf16[416,768]{1,0:T(8,128)(2,1)} %collective-permute-done.8.refs_25_), channel_id=1, source_target_pairs={{0,8},{1,9},{2,10},{3,11},{4,12},{5,13},{6,14},{7,15},{8,0},{9,1},... | collective-permute-start | bytes 1916936 | tf_op jit(solution)/shard_map/ppermute | solution.py:1142
  102.2 17.9 %collective-permute-start.30 = (bf16[416,768]{1,0:T(8,128)(2,1)S(1)}, bf16[416,768]{1,0:T(8,128)(2,1)S(1)}, u32[]{:S(2)}, u32[]{:S(2)}) collective-permute-start(bf16[416,768]{1,0:T(8,128)(2,1)S(1)} %copy-done.66), channel_id=1, source_target_pairs={{0,1},{1,2},{2,3},{3,0},{4,5},{5,6},{6,7},{7,4},{8,9},{9,10},{10,1... | collective-permute-start | bytes 1916936 | tf_op jit(solution)/shard_map/ppermute | solution.py:1156
  120.1 17.1 %collective-permute-start.34 = (bf16[416,768]{1,0:T(8,128)(2,1)S(1)}, bf16[416,768]{1,0:T(8,128)(2,1)S(1)}, u32[]{:S(2)}, u32[]{:S(2)}) collective-permute-start(bf16[416,768]{1,0:T(8,128)(2,1)S(1)} %collective-permute-done.30.refs_17_), channel_id=1, source_target_pairs={{0,1},{1,2},{2,3},{3,0},{4,5},{5,6},{6,7},{7,4},{8,9},{9,10},{10,1... | collective-permute-start | bytes 1916936 | tf_op jit(solution)/shard_map/ppermute | solution.py:1156
  120.1 17.1 %collective-permute-start.35 = (bf16[416,768]{1,0:T(8,128)(2,1)S(1)}, bf16[416,768]{1,0:T(8,128)(2,1)S(1)}, u32[]{:S(2)}, u32[]{:S(2)}) collective-permute-start(bf16[416,768]{1,0:T(8,128)(2,1)S(1)} %copy-done.66), channel_id=1, source_target_pairs={{0,8},{1,9},{2,10},{3,11},{4,12},{5,13},{6,14},{7,15},{8,0},{9,1},... | collective-permute-start | bytes 1916936 | tf_op jit(solution)/shard_map/ppermute | solution.py:1142
  137.3 18.8 %collective-permute-start.38 = (bf16[416,768]{1,0:T(8,128)(2,1)S(1)}, bf16[416,768]{1,0:T(8,128)(2,1)S(1)}, u32[]{:S(2)}, u32[]{:S(2)}) collective-permute-start(bf16[416,768]{1,0:T(8,128)(2,1)S(1)} %collective-permute-done.34.refs_18_), channel_id=1, source_target_pairs={{0,1},{1,2},{2,3},{3,0},{4,5},{5,6},{6,7},{7,4},{8,9},{9,10},{10,1... | collective-permute-start | bytes 1916936 | tf_op jit(solution)/shard_map/ppermute | solution.py:1156
  139.2 16.9 %collective-permute-start.40 = (bf16[416,768]{1,0:T(8,128)(2,1)S(1)}, bf16[416,768]{1,0:T(8,128)(2,1)S(1)}, u32[]{:S(2)}, u32[]{:S(2)}) collective-permute-start(bf16[416,768]{1,0:T(8,128)(2,1)S(1)} %collective-permute-done.34.refs_18_), channel_id=1, source_target_pairs={{0,8},{1,9},{2,10},{3,11},{4,12},{5,13},{6,14},{7,15},{8,0},{9,1},... | collective-permute-start | bytes 1916936 | tf_op jit(solution)/shard_map/ppermute | solution.py:1142
  139.2 16.9 %collective-permute-start.39 = (bf16[416,768]{1,0:T(8,128)(2,1)S(1)}, bf16[416,768]{1,0:T(8,128)(2,1)S(1)}, u32[]{:S(2)}, u32[]{:S(2)}) collective-permute-start(bf16[416,768]{1,0:T(8,128)(2,1)S(1)} %collective-permute-done.30.refs_17_), channel_id=1, source_target_pairs={{0,8},{1,9},{2,10},{3,11},{4,12},{5,13},{6,14},{7,15},{8,0},{9,1},... | collective-permute-start | bytes 1916936 | tf_op jit(solution)/shard_map/ppermute | solution.py:1142
  158.3 54.0 %collective-permute-start.43 = (bf16[4,96,768]{2,1,0:T(8,128)(2,1)}, bf16[4,96,768]{2,1,0:T(8,128)(2,1)S(1)}, u32[]{:S(2)}, u32[]{:S(2)}) collective-permute-start(bf16[4,96,768]{2,1,0:T(8,128)(2,1)} %get-tuple-element.817), channel_id=1, source_target_pairs={{0,4},{1,5},{2,6},{3,7},{4,0},{5,1},{6,2},{7,3},{8,12},{9,13},{10,... | collective-permute-start | bytes 1769480 | tf_op jit(solution)/shard_map/ppermute | solution.py:1146
  158.9 53.5 %collective-permute-start.44 = (bf16[4,96,768]{2,1,0:T(8,128)(2,1)}, bf16[4,96,768]{2,1,0:T(8,128)(2,1)S(1)}, u32[]{:S(2)}, u32[]{:S(2)}) collective-permute-start(bf16[4,96,768]{2,1,0:T(8,128)(2,1)} %get-tuple-element.818), channel_id=1, source_target_pairs={{0,16},{1,17},{2,18},{3,19},{4,20},{5,21},{6,22},{7,23},{8,24},{9,... | collective-permute-start | bytes 1769480 | tf_op jit(solution)/shard_map/ppermute | solution.py:1146
  159.8 52.5 %collective-permute-start.45 = (bf16[4,96,768]{2,1,0:T(8,128)(2,1)}, bf16[4,96,768]{2,1,0:T(8,128)(2,1)}, u32[]{:S(2)}, u32[]{:S(2)}) collective-permute-start(bf16[4,96,768]{2,1,0:T(8,128)(2,1)} %get-tuple-element.819), channel_id=1, source_target_pairs={{0,20},{1,21},{2,22},{3,23},{4,16},{5,17},{6,18},{7,19},{8,28},{9,... | collective-permute-start | bytes 1769480 | tf_op jit(solution)/shard_map/ppermute | solution.py:1146
  213.4 23.8 %collective-permute-start.46 = (bf16[768,768]{1,0:T(8,128)(2,1)}, bf16[768,768]{1,0:T(8,128)(2,1)S(1)}, u32[]{:S(2)}, u32[]{:S(2)}) collective-permute-start(bf16[768,768]{1,0:T(8,128)(2,1)} %get-tuple-element.831), channel_id=1, source_target_pairs={{0,4},{1,5},{2,6},{3,7},{4,0},{5,1},{6,2},{7,3},{8,12},{9,13},{10,... | collective-permute-start | bytes 3538952 | tf_op jit(solution)/shard_map/ppermute | solution.py:1146
  214.8 22.7 %collective-permute-start.47 = (bf16[768,768]{1,0:T(8,128)(2,1)}, bf16[768,768]{1,0:T(8,128)(2,1)}, u32[]{:S(2)}, u32[]{:S(2)}) collective-permute-start(bf16[768,768]{1,0:T(8,128)(2,1)} %get-tuple-element.832), channel_id=1, source_target_pairs={{0,16},{1,17},{2,18},{3,19},{4,20},{5,21},{6,22},{7,23},{8,24},{9,... | collective-permute-start | bytes 3538952 | tf_op jit(solution)/shard_map/ppermute | solution.py:1146
  244.3 62.6 %collective-permute-start.49 = (bf16[2,768,768]{2,1,0:T(8,128)(2,1)}, bf16[2,768,768]{2,1,0:T(8,128)(2,1)}, u32[]{:S(2)}, u32[]{:S(2)}) collective-permute-start(bf16[2,768,768]{2,1,0:T(8,128)(2,1)} %fusion.3), channel_id=1, source_target_pairs={{0,4},{1,5},{2,6},{3,7},{4,0},{5,1},{6,2},{7,3},{8,12},{9,13},{10,... | collective-permute-start | bytes 7077896 | tf_op jit(solution)/shard_map/ppermute | solution.py:1146
  245.8 61.2 %collective-permute-start.50 = (bf16[2,768,768]{2,1,0:T(8,128)(2,1)}, bf16[2,768,768]{2,1,0:T(8,128)(2,1)}, u32[]{:S(2)}, u32[]{:S(2)}) collective-permute-start(bf16[2,768,768]{2,1,0:T(8,128)(2,1)} %fusion.5), channel_id=1, source_target_pairs={{0,16},{1,17},{2,18},{3,19},{4,20},{5,21},{6,22},{7,23},{8,24},{9,... | collective-permute-start | bytes 7077896 | tf_op jit(solution)/shard_map/ppermute | solution.py:1146
  248.8 25.6 %collective-permute-start.51 = (bf16[416,768]{1,0:T(8,128)(2,1)}, bf16[416,768]{1,0:T(8,128)(2,1)}, u32[]{:S(2)}, u32[]{:S(2)}) collective-permute-start(bf16[416,768]{1,0:T(8,128)(2,1)} %get-tuple-element.1205), channel_id=1, source_target_pairs={{0,3},{1,0},{2,1},{3,2},{4,7},{5,4},{6,5},{7,6},{8,11},{9,8},{10,9... | collective-permute-start | bytes 1916936 | tf_op jit(solution)/shard_map/ppermute | solution.py:1191
  251.3 55.7 %collective-permute-start.52 = (bf16[416,768]{1,0:T(8,128)(2,1)}, bf16[416,768]{1,0:T(8,128)(2,1)}, u32[]{:S(2)}, u32[]{:S(2)}) collective-permute-start(bf16[416,768]{1,0:T(8,128)(2,1)} %get-tuple-element.1204), channel_id=1, source_target_pairs={{0,2},{1,3},{2,0},{3,1},{4,6},{5,7},{6,4},{7,5},{8,10},{9,11},{10,... | collective-permute-start | bytes 1916936 | tf_op jit(solution)/shard_map/ppermute | solution.py:1191
  251.3 55.7 %collective-permute-start.53 = (bf16[416,768]{1,0:T(8,128)(2,1)S(1)}, bf16[416,768]{1,0:T(8,128)(2,1)}, u32[]{:S(2)}, u32[]{:S(2)}) collective-permute-start(bf16[416,768]{1,0:T(8,128)(2,1)S(1)} %get-tuple-element.1203), channel_id=1, source_target_pairs={{0,1},{1,2},{2,3},{3,0},{4,5},{5,6},{6,7},{7,4},{8,9},{9,10},{10,1... | collective-permute-start | bytes 1916936 | tf_op jit(solution)/shard_map/ppermute | solution.py:1191
  316.2 36.6 %collective-permute-start.55 = (bf16[768,768]{1,0:T(8,128)(2,1)}, bf16[768,768]{1,0:T(8,128)(2,1)}, u32[]{:S(2)}, u32[]{:S(2)}) collective-permute-start(bf16[768,768]{1,0:T(8,128)(2,1)} %get-tuple-element.1086.refs_5_), channel_id=1, source_target_pairs={{1,0},{2,1},{5,4},{6,5},{11,10},{8,11},{15,14},{12,15},{17,16},{18... | collective-permute-start | bytes 3538952 | tf_op jit(solution)/shard_map/ppermute | solution.py:1172
  317.5 35.3 %collective-permute-start.56 = (bf16[768,768]{1,0:T(8,128)(2,1)}, bf16[768,768]{1,0:T(8,128)(2,1)}, u32[]{:S(2)}, u32[]{:S(2)}) collective-permute-start(bf16[768,768]{1,0:T(8,128)(2,1)} %get-tuple-element.1086.refs_5_), channel_id=1, source_target_pairs={{3,0},{0,1},{7,4},{4,5},{9,10},{10,11},{13,14},{14,15},{19,16},{16... | collective-permute-start | bytes 3538952 | tf_op jit(solution)/shard_map/ppermute | solution.py:1172
  322.1 30.7 %collective-permute-start.57 = (bf16[2,2,96,768]{3,2,1,0:T(8,128)(2,1)}, bf16[2,2,96,768]{3,2,1,0:T(8,128)(2,1)S(1)}, u32[]{:S(2)}, u32[]{:S(2)}) collective-permute-start(bf16[2,2,96,768]{3,2,1,0:T(8,128)(2,1)} %get-tuple-element.942), channel_id=1, source_target_pairs={{0,4},{1,5},{2,6},{3,7},{4,0},{5,1},{6,2},{7,3},{8,12},{9,13},{10,... | collective-permute-start | bytes 1769480 | tf_op jit(solution)/shard_map/ppermute | solution.py:1146
  323.6 29.1 %collective-permute-start.58 = (bf16[2,2,96,768]{3,2,1,0:T(8,128)(2,1)}, bf16[2,2,96,768]{3,2,1,0:T(8,128)(2,1)}, u32[]{:S(2)}, u32[]{:S(2)}) collective-permute-start(bf16[2,2,96,768]{3,2,1,0:T(8,128)(2,1)} %get-tuple-element.943), channel_id=1, source_target_pairs={{0,16},{1,17},{2,18},{3,19},{4,20},{5,21},{6,22},{7,23},{8,24},{9,... | collective-permute-start | bytes 1769480 | tf_op jit(solution)/shard_map/ppermute | solution.py:1146
  324.1 28.6 %collective-permute-start.59 = (bf16[2,2,96,768]{3,2,1,0:T(8,128)(2,1)}, bf16[2,2,96,768]{3,2,1,0:T(8,128)(2,1)}, u32[]{:S(2)}, u32[]{:S(2)}) collective-permute-start(bf16[2,2,96,768]{3,2,1,0:T(8,128)(2,1)} %get-tuple-element.944), channel_id=1, source_target_pairs={{0,20},{1,21},{2,22},{3,23},{4,16},{5,17},{6,18},{7,19},{8,28},{9,... | collective-permute-start | bytes 1769480 | tf_op jit(solution)/shard_map/ppermute | solution.py:1146
  352.8 27.3 %collective-permute-start.62 = (bf16[4,2,192,768]{3,2,1,0:T(8,128)(2,1)}, bf16[4,2,192,768]{3,2,1,0:T(8,128)(2,1)}, u32[]{:S(2)}, u32[]{:S(2)}) collective-permute-start(bf16[4,2,192,768]{3,2,1,0:T(8,128)(2,1)} %get-tuple-element.949), channel_id=1, source_target_pairs={{0,8},{1,9},{2,10},{3,11},{4,12},{5,13},{6,14},{7,15},{8,0},{9,1},... | collective-permute-start | bytes 7077896 | tf_op jit(solution)/shard_map/ppermute | solution.py:1142
  356.1 24.0 %collective-permute-start.63 = (bf16[4,2,96,768]{3,2,1,0:T(8,128)(2,1)}, bf16[4,2,96,768]{3,2,1,0:T(8,128)(2,1)}, u32[]{:S(2)}, u32[]{:S(2)}) collective-permute-start(bf16[4,2,96,768]{3,2,1,0:T(8,128)(2,1)} %get-tuple-element.1221), channel_id=1, source_target_pairs={{0,8},{1,9},{2,10},{3,11},{4,12},{5,13},{6,14},{7,15},{8,0},{9,1},... | collective-permute-start | bytes 3538952 | tf_op jit(solution)/shard_map/ppermute | solution.py:1142
  356.6 19.3 %collective-permute-start.60 = (bf16[256,768]{1,0:T(8,128)(2,1)}, bf16[256,768]{1,0:T(8,128)(2,1)}, u32[]{:S(2)}, u32[]{:S(2)}) collective-permute-start(bf16[256,768]{1,0:T(8,128)(2,1)} %get-tuple-element.946), channel_id=1, source_target_pairs={{2,0},{3,1},{6,4},{7,5},{8,10},{9,11},{12,14},{13,15},{18,16},{19,... | collective-permute-start | bytes 1179656 | tf_op jit(solution)/shard_map/ppermute | solution.py:1172
  357.9 22.2 %collective-permute-start.61 = (bf16[256,768]{1,0:T(8,128)(2,1)}, bf16[256,768]{1,0:T(8,128)(2,1)}, u32[]{:S(2)}, u32[]{:S(2)}) collective-permute-start(bf16[256,768]{1,0:T(8,128)(2,1)} %get-tuple-element.947), channel_id=1, source_target_pairs={{2,0},{3,1},{6,4},{7,5},{8,10},{9,11},{12,14},{13,15},{18,16},{19,... | collective-permute-start | bytes 1179656 | tf_op jit(solution)/shard_map/ppermute | solution.py:1172
  385.0 18.2 %collective-permute-start.66 = (bf16[4,2,2,24,768]{4,3,0,2,1:T(8,128)(2,1)S(1)}, bf16[4,2,2,24,768]{4,3,0,2,1:T(8,128)(2,1)S(1)}, u32[]{:S(2)}, u32[]{:S(2)}) collective-permute-start(bf16[4,2,2,24,768]{4,3,0,2,1:T(8,128)(2,1)S(1)} %add_convert_fusion.3), channel_id=1, source_target_pairs={{0,16},{1,17},{2,18},{3,19},{4,20},{5,21},{6,22},{7,23},{8,24},{9,... | collective-permute-start | bytes 1769480 | tf_op jit(solution)/shard_map/ppermute | solution.py:1146
  386.6 16.5 %collective-permute-start.67 = (bf16[416,768]{1,0:T(8,128)(2,1)S(1)}, bf16[416,768]{1,0:T(8,128)(2,1)S(1)}, u32[]{:S(2)}, u32[]{:S(2)}) collective-permute-start(bf16[416,768]{1,0:T(8,128)(2,1)S(1)} %copy-done.28), channel_id=1, source_target_pairs={{0,3},{1,0},{2,1},{3,2},{4,7},{5,4},{6,5},{7,6},{8,11},{9,8},{10,9... | collective-permute-start | bytes 1916936 | tf_op jit(solution)/shard_map/ppermute | solution.py:1191
  422.1 19.0 %collective-permute-start.73 = (bf16[4,32,768]{2,1,0:T(8,128)(2,1)}, bf16[4,32,768]{2,1,0:T(8,128)(2,1)S(1)}, u32[]{:S(2)}, u32[]{:S(2)}) collective-permute-start(bf16[4,32,768]{2,1,0:T(8,128)(2,1)} %get-tuple-element.1286), channel_id=1, source_target_pairs={{0,3},{1,0},{2,1},{3,2},{4,7},{5,4},{6,5},{7,6},{8,11},{9,8},{10,9... | collective-permute-start | bytes 589832 | tf_op jit(solution)/shard_map/ppermute | solution.py:1191
  422.3 18.8 %collective-permute-start.74 = (bf16[4,32,768]{2,1,0:T(8,128)(2,1)}, bf16[4,32,768]{2,1,0:T(8,128)(2,1)S(1)}, u32[]{:S(2)}, u32[]{:S(2)}) collective-permute-start(bf16[4,32,768]{2,1,0:T(8,128)(2,1)} %get-tuple-element.1287), channel_id=1, source_target_pairs={{0,2},{1,3},{2,0},{3,1},{4,6},{5,7},{6,4},{7,5},{8,10},{9,11},{10,... | collective-permute-start | bytes 589832 | tf_op jit(solution)/shard_map/ppermute | solution.py:1191
  422.5 18.6 %collective-permute-start.75 = (bf16[4,32,768]{2,1,0:T(8,128)(2,1)}, bf16[4,32,768]{2,1,0:T(8,128)(2,1)}, u32[]{:S(2)}, u32[]{:S(2)}) collective-permute-start(bf16[4,32,768]{2,1,0:T(8,128)(2,1)} %get-tuple-element.1285), channel_id=1, source_target_pairs={{0,1},{1,2},{2,3},{3,0},{4,5},{5,6},{6,7},{7,4},{8,9},{9,10},{10,1... | collective-permute-start | bytes 589832 | tf_op jit(solution)/shard_map/ppermute | solution.py:1191
  445.6 19.3 %collective-permute-start.76 = (bf16[4,24,768]{2,1,0:T(8,128)(2,1)S(1)}, bf16[4,24,768]{2,1,0:T(8,128)(2,1)}, u32[]{:S(2)}, u32[]{:S(2)}) collective-permute-start(bf16[4,24,768]{2,1,0:T(8,128)(2,1)S(1)} %pad_maximum_fusion.23), channel_id=1, source_target_pairs={{0,1},{1,2},{2,3},{3,0},{4,5},{5,6},{6,7},{7,4},{8,9},{9,10},{10,1... | collective-permute-start | bytes 442376 | tf_op jit(solution)/shard_map/ppermute | solution.py:1191
  447.2 17.7 %collective-permute-start.77 = (bf16[4,24,768]{2,1,0:T(8,128)(2,1)S(1)}, bf16[4,24,768]{2,1,0:T(8,128)(2,1)}, u32[]{:S(2)}, u32[]{:S(2)}) collective-permute-start(bf16[4,24,768]{2,1,0:T(8,128)(2,1)S(1)} %pad_maximum_fusion.23), channel_id=1, source_target_pairs={{0,2},{1,3},{2,0},{3,1},{4,6},{5,7},{6,4},{7,5},{8,10},{9,11},{10,... | collective-permute-start | bytes 442376 | tf_op jit(solution)/shard_map/ppermute | solution.py:1191
  464.9 16.5 %collective-permute-start.79 = (bf16[6,256,256]{2,1,0:T(8,128)(2,1)}, bf16[6,256,256]{2,1,0:T(8,128)(2,1)S(1)}, u32[]{:S(2)}, u32[]{:S(2)}) collective-permute-start(bf16[6,256,256]{2,1,0:T(8,128)(2,1)} %wide_last.1.refs_0_), channel_id=1, source_target_pairs={{0,1},{1,2},{4,5},{5,6},{10,11},{11,8},{14,15},{15,12},{16,17},{17... | collective-permute-start | bytes 2359304 | tf_op jit(solution)/shard_map/ppermute | solution.py:1177
  466.2 19.5 %collective-permute-start.80 = (bf16[6,256,256]{2,1,0:T(8,128)(2,1)}, bf16[6,256,256]{2,1,0:T(8,128)(2,1)S(1)}, u32[]{:S(2)}, u32[]{:S(2)}) collective-permute-start(bf16[6,256,256]{2,1,0:T(8,128)(2,1)} %wide_last.1.refs_0_), channel_id=1, source_target_pairs={{0,3},{1,0},{4,7},{5,4},{10,9},{11,10},{14,13},{15,14},{16,19},{17... | collective-permute-start | bytes 2359304 | tf_op jit(solution)/shard_map/ppermute | solution.py:1177
  498.2 38.2 %collective-permute-start.86 = (bf16[416,768]{1,0:T(8,128)(2,1)S(1)}, bf16[416,768]{1,0:T(8,128)(2,1)S(1)}, u32[]{:S(2)}, u32[]{:S(2)}) collective-permute-start(bf16[416,768]{1,0:T(8,128)(2,1)S(1)} %add_convert_fusion.2), channel_id=1, source_target_pairs={{0,3},{1,0},{2,1},{3,2},{4,7},{5,4},{6,5},{7,6},{8,11},{9,8},{10,9... | collective-permute-start | bytes 1916936 | tf_op jit(solution)/shard_map/ppermute | solution.py:1191
  511.3 25.1 %collective-permute-start.87 = (bf16[416,768]{1,0:T(8,128)(2,1)S(1)}, bf16[416,768]{1,0:T(8,128)(2,1)S(1)}, u32[]{:S(2)}, u32[]{:S(2)}) collective-permute-start(bf16[416,768]{1,0:T(8,128)(2,1)S(1)} %copy-done.27), channel_id=1, source_target_pairs={{0,1},{1,2},{2,3},{3,0},{4,5},{5,6},{6,7},{7,4},{8,9},{9,10},{10,1... | collective-permute-start | bytes 1916936 | tf_op jit(solution)/shard_map/ppermute | solution.py:1156
  511.3 21.5 %collective-permute-start.88 = (bf16[2,2,96,768]{3,2,1,0:T(8,128)(2,1)}, bf16[2,2,96,768]{3,2,1,0:T(8,128)(2,1)S(1)}, u32[]{:S(2)}, u32[]{:S(2)}) collective-permute-start(bf16[2,2,96,768]{3,2,1,0:T(8,128)(2,1)} %get-tuple-element.1105), channel_id=1, source_target_pairs={{0,4},{1,5},{2,6},{3,7},{4,0},{5,1},{6,2},{7,3},{8,12},{9,13},{10,... | collective-permute-start | bytes 1769480 | tf_op jit(solution)/shard_map/ppermute | solution.py:1146
  512.5 20.3 %collective-permute-start.89 = (bf16[2,2,96,768]{3,2,1,0:T(8,128)(2,1)}, bf16[2,2,96,768]{3,2,1,0:T(8,128)(2,1)}, u32[]{:S(2)}, u32[]{:S(2)}) collective-permute-start(bf16[2,2,96,768]{3,2,1,0:T(8,128)(2,1)} %get-tuple-element.1106), channel_id=1, source_target_pairs={{0,16},{1,17},{2,18},{3,19},{4,20},{5,21},{6,22},{7,23},{8,24},{9,... | collective-permute-start | bytes 1769480 | tf_op jit(solution)/shard_map/ppermute | solution.py:1146
  513.9 22.5 %collective-permute-start.90 = (bf16[2,2,96,768]{3,2,1,0:T(8,128)(2,1)}, bf16[2,2,96,768]{3,2,1,0:T(8,128)(2,1)}, u32[]{:S(2)}, u32[]{:S(2)}) collective-permute-start(bf16[2,2,96,768]{3,2,1,0:T(8,128)(2,1)} %get-tuple-element.1107), channel_id=1, source_target_pairs={{0,20},{1,21},{2,22},{3,23},{4,16},{5,17},{6,18},{7,19},{8,28},{9,... | collective-permute-start | bytes 1769480 | tf_op jit(solution)/shard_map/ppermute | solution.py:1146
  (129 other events, 1161.3 us)

commit v4 on v3

--- a/solution.py
+++ b/solution.py
@@ -1023,16 +1023,22 @@
 ):
     rows_all, features = tokens.shape
     low = jnp.bfloat16
-    core = place[1]
+    chip, core = place[0], place[1]
 
     def store_part(which, value):
         part[...] = value
-        slab = mine.shape[2]
-        for side in range(2):
-            own = pl.ds(pl.multiple_of((2 * side + core) * slab, slab), slab)
-            other = pl.ds(pl.multiple_of((2 * side + 1 - core) * slab, slab), slab)
-            mine[which, side] = part[own, :].astype(low)
-            theirs[which, side] = part[other, :].astype(low)
+        slab = mine.shape[3]
+        y_here, x_here = chip // 2, lax.rem(chip, 2)
+        for out, side in ((mine, core), (theirs, 1 - core)):
+            for kind in range(4):
+                for turn in range(2):
+                    if kind < 2:
+                        y, x = jnp.bitwise_xor(y_here, turn), jnp.bitwise_xor(x_here, kind)
+                    else:
+                        y, x = jnp.bitwise_xor(y_here, kind - 2), jnp.bitwise_xor(x_here, turn)
+                    row = (((y * 2 + side) * 2 + x) * 2 + kind // 2) * slab
+                    rows = pl.ds(pl.multiple_of(row, 16), slab)
+                    out[kind, which, turn] = part[rows, :].astype(low)
 
     d_second = second0[...].astype(jnp.float32)
     for piece in (second1, second2, second3):
@@ -1095,7 +1101,7 @@
     rows, features = tokens.shape
     low = jnp.bfloat16
     vmem = pl.BlockSpec(memory_space=pltpu.VMEM)
-    half_shape = jax.ShapeDtypeStruct((4, 2, features // 4, features), low)
+    half_shape = jax.ShapeDtypeStruct((4, 4, 2, features // 16, features), low)
     return pl.pallas_call(
         backward_kernel,
         in_specs=[pl.BlockSpec(memory_space=pltpu.SMEM)] + [vmem] * 12,
@@ -1279,7 +1285,6 @@
     device = jnp.stack([chip, core, tp]).astype(jnp.int32)
     y_here, x_here = shard // 2, ctx
     padded = seqs * IMAGE
-    half = tps // 2
     own_tokens, own_cot = (
         jnp.pad(
             value[0].reshape(seqs, LEN, features), ((0, 0), (0, IMAGE - LEN), (0, 0))
@@ -1419,14 +1424,14 @@
     kept = join(*v.drop.part)
     v.along_x, v.along_y = swap_chip(v.along_x, 1), swap_chip(v.along_y, 2)
     v.seconds = [kept[0]] + [pass_by(kept[turn], -turn) for turn in range(1, tps)]
-    v.mixed = tokens_pass(*v.drop.routes, v.drop.hidden, v.drop.downs, True)
+    v.summed = tokens_pass(*v.drop.routes, v.drop.hidden, v.drop.downs, True)
     v = hold(v)
 
     push, push_next, band0, band1, band2, *rows = push_rows(
         device, v.drop.own, (v.drop.along_x, v.drop.along_y), v.drop.moments
     )
     v.push, v.blocks, v.rows = [push, push_next], [band0, band1, band2], rows
-    v.mixed = [v.mixed[0], swap_core(v.mixed[1])]
+    v.summed = [v.summed[0], swap_core(v.summed[1])]
     v = hold(v)
 
     def rows_out(rows):
@@ -1453,39 +1458,33 @@
     def added(value, got):
         return value.astype(jnp.float32) + got.astype(jnp.float32)
 
-    shape = (4, 2, 2, tps, rows_attn, features)
     v.gone = swap_core(v.gone)
     v.blocks[:2] = [to_worker(block, 2) for block in v.blocks[:2]]
     v.rows = rows_between(v.rows)
     vectors = v.vectors[:4]
     v.vectors = [vectors, swap_core(vectors)]
-    v.input_grad = v.input_grad.reshape(seqs, IMAGE, features)[:, :LEN].reshape(rows_here, features)
-    mixed = added(*v.mixed)
-    v.mixed = [mixed[0]] + [mixed[turn].astype(low) for turn in range(1, tps)]
-    v = hold(v)
-    own, gone = v.drop.own.reshape(shape), v.drop.gone.reshape(shape)
-
-    def first_part(x):
-        return added(pick(own, x, 2)[:, :, :half], pick(gone, x, 2)[:, :, :half])
-
-    def last_part(y):
-        return added(pick(own, y, 1)[:, :, half:], pick(gone, y, 1)[:, :, half:])
-
-    v.first = [first_part(x_here), swap_chip(first_part(1 - x_here).astype(low), 1)]
-    v.last = [last_part(y_here), swap_chip(last_part(1 - y_here).astype(low), 2)]
-    v.mixed.append(pass_by(v.mixed[2], -1))
+    input_grad = v.drop.input_grad
+    input_grad = input_grad.reshape(seqs, IMAGE, features)[:, :LEN].reshape(rows_here, features)
+    mixed = added(*v.summed)
+    v.summed = [mixed[0]] + [mixed[turn].astype(low) for turn in range(1, tps)]
+    v = hold(v)
+    own, gone = v.drop.own, v.drop.gone
+    v.first = [added(own[0], gone[0]), swap_chip(added(own[1], gone[1]).astype(low), 1)]
+    v.last = [added(own[2], gone[2]), swap_chip(added(own[3], gone[3]).astype(low), 2)]
+    v.summed.append(pass_by(v.summed[2], -1))
     vectors = sum(v.vectors)
     v.vectors = [vectors, swap_chip(vectors, 1)]
     v = hold(v)
     first, last = added(*v.first), added(*v.last)
-    v.first = [pick(first, y_here, 1), swap_chip(pick(first, 1 - y_here, 1).astype(low), 2)]
-    v.last = [pick(last, x_here, 1), swap_chip(pick(last, 1 - x_here, 1).astype(low), 1)]
+    v.first = [first[:, 0], swap_chip(first[:, 1].astype(low), 2)]
+    v.last = [last[:, 0], swap_chip(last[:, 1].astype(low), 1)]
     v.blocks[2] = to_worker(v.blocks[2], 2)
     vectors = sum(v.vectors)
     v.vectors = [vectors, swap_chip(vectors, 2)]
     v = hold(v)
 
     sums = jnp.concatenate([added(*v.drop.first), added(*v.drop.last)], axis=1)
+    sums = sums.reshape(4, tps, rows_attn, features)
     vectors = jnp.pad(sum(v.drop.vectors)[:, None], ((0, 0), (0, 7), (0, 0)))
     parts = [
         jnp.concatenate([pick(sums, (tp - turn) % tps, 1), vectors], axis=1).astype(low)
@@ -1527,8 +1526,8 @@
     v = hold(v)
 
     v.new = rows_out(v.new)
-    own_part, next_part, unused, far_part, got = v.mixed
-    v.mixed = [own_part, pass_by(added(next_part, got).astype(low), -1), pass_on(far_part)]
+    own_part, next_part, unused, far_part, got = v.summed
+    v.summed = [own_part, pass_by(added(next_part, got).astype(low), -1), pass_on(far_part)]
     v.moved = orthogonal_square(v.drop.pushes)
     v = hold(v)
     moved = v.drop.moved.reshape(2, 2, 2, tps, rows_attn, features)
@@ -1537,10 +1536,9 @@
     v.moved = [gone[0]] + [swap_chip(gone[turn], turn) for turn in range(1, 4)]
     v.new = rows_between(v.new)
     v = hold(v)
-    mixed = v.drop.mixed
+    mixed = v.drop.summed
     result = (residual + mixed[0] + added(mixed[1], mixed[2])).astype(low)
     result = result.reshape(seqs, IMAGE, features)[:, :LEN].reshape(rows_here, features)
-    input_grad = v.input_grad
     scales_grad, shifts_grad = v.vectors[:2], v.vectors[2:]
     scales_state, scales_push = advance(scales_grad, scales_moment)
     shifts_state, shifts_push = advance(shifts_grad, shifts_moment)

time: 570 us -> 568 us (level)
  waiting for transfers between devices: 160 us -> 175 us
  local copies, waits for them, and re-layouts: 41.1 us -> 29.3 us
    ppermute x7, waiting for transfers between devices: 5.7 us -> 14.1 us  [pass_on(): return lax.ppermute(value, axes, route_to(lambda s, c, t: (s, c, t + 1)))]
    ppermute x5, waiting for transfers between devices: 8.68 us -> 15.8 us  [to_worker(): lax.ppermute(value, axes, worker_route(lambda w: w + turn, lambda w: w))]
    ppermute x5, starting transfers between devices: 9.87 us -> 16.3 us  [to_worker(): lax.ppermute(value, axes, worker_route(lambda w: w + turn, lambda w: w))]
  transfers between devices with their start and end apart: 95 -> 95, of which waited for: 34 -> 35; matrix products, arithmetic and copies ran while one was open for 9% -> 9% of each run, Pallas kernels for 34% -> 33%
where the time goes in v4:
time: 568 us; the launch traced here: 560 us
  Pallas kernels  192 us (34%)
  waiting for transfers between devices  175 us (31%)
  starting transfers between devices  109 us (19%)
  other arithmetic  51.4 us (9%)
  local copies, waits for them, and re-layouts  29.3 us (5%)
    ppermute x43, waiting for transfers between devices, swap_chip(): lax.ppermute(value, axes, route_to(lambda s, c, t: (s ^ turn & 2, c ^ tur...  99.4 us
    pallas_call x1, Pallas kernels, experts_pass(): pl.pallas_call(experts_kernel, grid_spec=pltpu.PrefetchScalarGridSpec(num...  48.5 us
    ppermute x43, starting transfers between devices, swap_chip(): lax.ppermute(value, axes, route_to(lambda s, c, t: (s ^ turn & 2, c ^ tur...  48.3 us
    pallas_call x2, Pallas kernels, tokens_pass(): pl.pallas_call(functools.partial(tokens_kernel, gated), grid_spec=pltpu.P...  40.5 us
    ppermute x17, starting transfers between devices, pass_by(): lax.ppermute(value, axes, route_to(lambda s, c, t: (s, c, t + steps)))  34 us
    ppermute x17, waiting for transfers between devices, pass_by(): lax.ppermute(value, axes, route_to(lambda s, c, t: (s, c, t + steps)))  33.9 us
    pallas_call x2, Pallas kernels, wide_call(): pl.pallas_call(kernel, out_shape=out_shape, in_specs=[vmem] * len(inputs)...  30 us
    pallas_call x1, Pallas kernels, attention_backward(): pl.pallas_call(backward_kernel, in_specs=[pl.BlockSpec(memory_space=pltpu...  27 us
  transfers between devices with their start and end apart: 95, of which 35 were waited for; matrix products, arithmetic and copies ran while one was open for 9% of the time, Pallas kernels for 33%

profile of v4, /device:TPU:0, one launch (start us, length us, event | category | flops | bytes accessed | tf_op | source)
XLA Modules:
  0.0 560.2 jit_solution(16103147544467403319)
XLA Ops:
  3.3 3.0 collective-permute-start.3
  8.9 3.7 collective-permute-start.6
  14.2 3.8 collective-permute-start.2
  22.7 7.6 %collective-permute-done.1 = bf16[4,24,768]{2,1,0:T(8,128)(2,1)} collective-permute-done((bf16[4,24,768]{2,1,0:T(8,128)(2,1)}, bf16[4,24,768]{2,1,0:T(8,128)(2,1)}, u32[]{:S(2)}, u32[]{:S(2)}) %collective-permute-start.1) | collective-permute-done | bytes 147488 | tf_op jit(solution)/shard_map/ppermute | solution.py:1197
  34.5 13.2 %collective-permute-done.12.w2 = bf16[4,96,768]{2,1,0:T(8,128)(2,1)S(1)} collective-permute-done((bf16[4,96,768]{2,1,0:T(8,128)(2,1)S(1)}, bf16[4,96,768]{2,1,0:T(8,128)(2,1)S(1)}, u32[]{:S(2)}, u32[]{:S(2)}) %collective-permute-start.12) | collective-permute-done | bytes 589856 | tf_op jit(solution)/shard_map/ppermute | solution.py:1152
  56.6 3.4 collective-permute-done.13
  65.9 11.7 %collective-permute-done.19 = f32[2,2,4,4,24]{4,3,2,1,0:T(4,128)S(1)} collective-permute-done((f32[2,2,4,4,24]{4,3,2,1,0:T(4,128)S(1)}, f32[2,2,4,4,24]{4,3,2,1,0:T(4,128)S(1)}, u32[]{:S(2)}, u32[]{:S(2)}) %collective-permute-start.19) | collective-permute-done | bytes 6176 | tf_op jit(solution)/shard_map/ppermute | solution.py:1152
  86.3 11.9 %attention_forward.1 = (bf16[416,768]{1,0:T(8,128)(2,1)}, bf16[3,416,768]{2,1,0:T(8,128)(2,1)}, bf16[416,768]{1,0:T(8,128)(2,1)}, f32[416,768]{1,0:T(8,128)}, bf...) custom-call(s32[3]{0:T(128)} %pad_add_fusion.place, bf16[416,768]{1,0:T(8,128)(2,1)} %bitcast.275, ...), custom_call_target="tpu_custom_call" | custom-call | flops 2453667840 | bytes 16777216 | tf_op jit(solution)/shard_map/attention_forward/pallas_call | solution.py:996
  104.2 9.1 %collective-permute-done.29.refs_15_.refs_7_ = bf16[4,96,768]{2,1,0:T(8,128)(2,1)S(1)} collective-permute-done((bf16[4,96,768]{2,1,0:T(8,128)(2,1)}, bf16[4,96,768]{2,1,0:T(8,128)(2,1)S(1)}, u32[]{:S(2)}, u32[]{:S(2)}) %collective-permute-start.29) | collective-permute-done | bytes 589856 | tf_op jit(solution)/shard_map/ppermute | solution.py:1152
  113.2 3.1 collective-permute-done.31.refs_7_
  116.4 5.8 %collective-permute-done.30.refs_17_ = bf16[416,768]{1,0:T(8,128)(2,1)S(1)} collective-permute-done((bf16[416,768]{1,0:T(8,128)(2,1)S(1)}, bf16[416,768]{1,0:T(8,128)(2,1)S(1)}, u32[]{:S(2)}, u32[]{:S(2)}) %collective-permute-start.30) | collective-permute-done | bytes 639008 | tf_op jit(solution)/shard_map/ppermute | solution.py:1162
  123.7 14.4 %collective-permute-done.32.refs_10_.refs_2_ = bf16[4,96,768]{2,1,0:T(8,128)(2,1)S(1)} collective-permute-done((bf16[4,96,768]{2,1,0:T(8,128)(2,1)}, bf16[4,96,768]{2,1,0:T(8,128)(2,1)S(1)}, u32[]{:S(2)}, u32[]{:S(2)}) %collective-permute-start.32) | collective-permute-done | bytes 589856 | tf_op jit(solution)/shard_map/ppermute | solution.py:1152
  138.4 2.4 collective-permute-done.34.refs_18_
  144.6 12.5 %collective-permute-done.37.refs_11_.refs_3_ = bf16[4,96,768]{2,1,0:T(8,128)(2,1)S(1)} collective-permute-done((bf16[4,96,768]{2,1,0:T(8,128)(2,1)S(1)}, bf16[4,96,768]{2,1,0:T(8,128)(2,1)S(1)}, u32[]{:S(2)}, u32[]{:S(2)}) %collective-permute-start.37) | collective-permute-done | bytes 589856 | tf_op jit(solution)/shard_map/ppermute | solution.py:1152
  157.3 2.5 collective-permute-done.38.refs_19_
  159.8 2.1 collective-permute-done.42.refs_23_
  163.3 2.2 collective-permute-start.45
  165.4 48.5 %experts_pass.1 = (bf16[4,1792,768]{2,1,0:T(8,128)(2,1)}, bf16[4,1792,768]{2,1,0:T(8,128)(2,1)}, bf16[2,768,768]{2,1,0:T(8,128)(2,1)}, bf16[2,768,768]{2,1,0:T(8...) custom-call(s32[38]{0:T(128)} %pad_add_fusion.1.starts, ...), custom_call_target="tpu_custom_call" | custom-call | flops 15703474176 | bytes 62914560 | tf_op jit(solution)/shard_map/experts_pass/pallas_call | solution.py:847
  216.7 19.7 %tokens_plain.1 = (bf16[4,416,768]{2,1,0:T(8,128)(2,1)}, bf16[4,416,768]{2,1,0:T(8,128)(2,1)}) custom-call(s32[38]{0:T(128)} %pad_add_fusion.1.starts, s32[4,8,416]{2,1,0:T(8,128)} %fusion.6.rank, f32[4,8,416]{2,1,0:T(8,128)} %fusion.17.gate, bf16[4,1792,768]{2,1,0:T(8,128)(2,1)} %get-tuple-element.834.acts, bf16[4,96,768]{2,1,0:T(8,128)(2,1)} %pad_maximum_fusion.11.refs_0_, ...), custom_call_target="tpu_custom_call" | custom-call | flops 7851737088 | bytes 31457280 | tf_op jit(solution)/shard_map/tokens_plain/pallas_call | solution.py:890
  236.5 5.9 %collective-permute-done.46 = bf16[768,768]{1,0:T(8,128)(2,1)S(1)} collective-permute-done((bf16[768,768]{1,0:T(8,128)(2,1)}, bf16[768,768]{1,0:T(8,128)(2,1)S(1)}, u32[]{:S(2)}, u32[]{:S(2)}) %collective-permute-start.46) | collective-permute-done | bytes 1179680 | tf_op jit(solution)/shard_map/ppermute | solution.py:1152
  246.7 2.6 fusion.3
  254.6 2.0 collective-permute-start.52
  258.4 20.7 %tokens_gated.1 = (bf16[4,416,768]{2,1,0:T(8,128)(2,1)}, bf16[4,416,768]{2,1,0:T(8,128)(2,1)}) custom-call(s32[38]{0:T(128)} %pad_add_fusion.1.starts, s32[4,8,416]{2,1,0:T(8,128)} %fusion.6.rank, f32[4,8,416]{2,1,0:T(8,128)} %fusion.17.gate, bf16[4,1792,768]{2,1,0:T(8,128)(2,1)} %get-tuple-element.880.acts, ...), custom_call_target="tpu_custom_call" | custom-call | flops 7851737088 | bytes 31457280 | tf_op jit(solution)/shard_map/tokens_gated/pallas_call | solution.py:890
  279.2 21.3 %collective-permute-done.52.second2 = bf16[416,768]{1,0:T(8,128)(2,1)} collective-permute-done((bf16[416,768]{1,0:T(8,128)(2,1)}, bf16[416,768]{1,0:T(8,128)(2,1)}, u32[]{:S(2)}, u32[]{:S(2)}) %collective-permute-start.52) | collective-permute-done | bytes 639008 | tf_op jit(solution)/shard_map/ppermute | solution.py:1197
  300.5 4.2 collective-permute-done.49.refs_0_
  304.6 9.1 %push_rows.1 = (bf16[768,768]{1,0:T(8,128)(2,1)}, bf16[768,768]{1,0:T(8,128)(2,1)}, bf16[256,768]{1,0:T(8,128)(2,1)}, bf16[256,768]{1,0:T(8,128)(2,1)}, bf16[256...) custom-call(s32[3]{0:T(128)} %pad_add_fusion.place, ...), custom_call_target="tpu_custom_call" | custom-call | flops 11796480 | bytes 14155776 | tf_op jit(solution)/shard_map/push_rows/pallas_call | solution.py:578
  313.7 11.0 %collective-permute-start.56 = (bf16[768,768]{1,0:T(8,128)(2,1)}, bf16[768,768]{1,0:T(8,128)(2,1)}, u32[]{:S(2)}, u32[]{:S(2)}) collective-permute-start(bf16[768,768]{1,0:T(8,128)(2,1)} %get-tuple-element.1064.refs_5_), channel_id=1, source_target_pairs={{3,0},{0,1},{7,4},{4,5},{9,10},{10,11},{13,14},{14,15},{19,16},{16... | collective-permute-start | bytes 3538952 | tf_op jit(solution)/shard_map/ppermute | solution.py:1178
  329.6 27.0 %attention_backward.1 = (f32[416,768]{1,0:T(8,128)}, bf16[4,4,2,48,768]{4,3,2,1,0:T(8,128)(2,1)}, bf16[4,4,2,48,768]{4,3,2,1,0:T(8,128)(2,1)}, f32[8,768]{1,0:T(8,128)}) custom-call(s32[3]{0:T(128)} %pad_add_fusion.place, bf16[416,768]{1,0:T(8,128)(2,1)} %bitcast.276, bf16[416,768]{1,0:T(8,128)(2,1)} %bitcast.5.refs_24_.cots, ...), custom_call_target="tpu_custom_call" | custom-call | flops 9814671360 | bytes 25165824 | tf_op jit(solution)/shard_map/attention_backward/pallas_call | solution.py:1105
  362.6 2.4 fusion.28
  367.5 11.5 %collective-permute-done.60.part0 = bf16[256,768]{1,0:T(8,128)(2,1)S(1)} collective-permute-done((bf16[256,768]{1,0:T(8,128)(2,1)S(1)}, bf16[256,768]{1,0:T(8,128)(2,1)S(1)}, u32[]{:S(2)}, u32[]{:S(2)}) %collective-permute-start.60) | collective-permute-done | bytes 393248 | tf_op jit(solution)/shard_map/ppermute | solution.py:1178
  379.0 4.2 collective-permute-done.61.part1
  388.9 14.0 %collective-permute-done.68 = f32[4,768]{1,0:T(4,128)} collective-permute-done((f32[4,768]{1,0:T(4,128)S(1)}, f32[4,768]{1,0:T(4,128)}, u32[]{:S(2)}, u32[]{:S(2)}) %collective-permute-start.68) | collective-permute-done | bytes 12320 | tf_op jit(solution)/shard_map/ppermute | solution.py:1152
  411.9 2.7 collective-permute-done.72
  414.6 2.4 collective-permute-done.71
  418.7 3.8 collective-permute-start.73
  422.9 16.6 %wide_first.1 = (f32[768,768]{1,0:T(8,128)}, f32[768,768]{1,0:T(8,128)}) custom-call(bf16[768,768]{1,0:T(8,128)(2,1)} %get-tuple-element.1063.block0.refs_4_, bf16[768,768]{1,0:T(8,128)(2,1)} %collective-permute-done.55.block1, bf16[768,768]{1,0:T(8,128)(2,1)} %collective-permute-done.56.block3, bf16[256,768]{1,0:T(8,128)(2,1)} %copy-done.75, ...), custom_call_target="tpu_custom_call" | custom-call | flops 9059696640 | bytes 4718592 | tf_op jit(solution)/shard_map/wide_first/pallas_call | solution.py:456
  446.6 2.1 collective-permute-start.76
  448.8 13.4 %wide_last.1.refs_0_ = bf16[6,256,256]{2,1,0:T(8,128)(2,1)} custom-call(f32[768,768]{1,0:T(8,128)} %get-tuple-element.1017.gram_in, f32[768,768]{1,0:T(8,128)} %get-tuple-element.1018.whole_in), custom_call_target="tpu_custom_call" | custom-call | flops 9059696640 | bytes 4718592 | tf_op jit(solution)/shard_map/wide_last/pallas_call | solution.py:456
  462.3 3.8 collective-permute-start.80
  466.1 2.2 collective-permute-start.79
  479.3 5.5 collective-permute-done.80.refs_3_
  486.5 2.0 collective-permute-done.85
  489.8 7.1 %apply_mixers.1 = (bf16[2,2,96,768]{3,2,1,0:T(8,128)(2,1)}, bf16[2,2,96,768]{3,2,1,0:T(8,128)(2,1)}, bf16[2,2,96,768]{3,2,1,0:T(8,128)(2,1)}, bf16[2,2,96,768]{3,2,1,0:T(8,128)(2,1)}) custom-call(s32[3]{0:T(128)} %pad_add_fusion.place, bf16[6,256,256]{2,1,0:T(8,128)(2,1)} %wide_last.1.refs_0_, bf16[6,256,256]{2,1,0:T(8,128)(2,1)} %copy-done.56, ...), custom_call_target="tpu_custom_call" | custom-call | flops 1811939328 | bytes 5898240 | tf_op jit(solution)/shard_map/apply_mixers/pallas_call | solution.py:524
  501.6 12.4 %collective-permute-start.89 = (bf16[416,768]{1,0:T(8,128)(2,1)S(1)}, bf16[416,768]{1,0:T(8,128)(2,1)S(1)}, u32[]{:S(2)}, u32[]{:S(2)}) collective-permute-start(bf16[416,768]{1,0:T(8,128)(2,1)S(1)} %add_convert_fusion.2), channel_id=1, source_target_pairs={{0,3},{1,0},{2,1},{3,2},{4,7},{5,4},{6,5},{7,6},{8,11},{9,8},{10,9... | collective-permute-start | bytes 1916936 | tf_op jit(solution)/shard_map/ppermute | solution.py:1197
  514.1 18.0 %square_orthogonal.1 = bf16[768,768]{1,0:T(8,128)(2,1)} custom-call(bf16[768,768]{1,0:T(8,128)(2,1)} %bitcast.274), custom_call_target="tpu_custom_call" | custom-call | flops 13589544960 | bytes 2359296 | tf_op jit(solution)/shard_map/square_orthogonal/pallas_call | solution.py:626
  532.1 4.9 collective-permute-done.89
  545.7 2.3 broadcast_in_dim_reshape.8
  552.4 2.1 convert_bitcast_fusion
  (450 shorter events, 139.9 us)
Async XLA Ops:
  3.3 27.0 %collective-permute-start.3 = (bf16[4,96,768]{2,1,0:T(8,128)(2,1)}, bf16[4,96,768]{2,1,0:T(8,128)(2,1)}, u32[]{:S(2)}, u32[]{:S(2)}) collective-permute-start(bf16[4,96,768]{2,1,0:T(8,128)(2,1)} %pad_maximum_fusion.10.refs_8_.refs_0_), channel_id=1, source_target_pairs={{0,16},{1,17},{2,18},{3,19},{4,20},{5,21},{6,22},{7,23},{8,24},{9,... | collective-permute-start | bytes 1769480 | tf_op jit(solution)/shard_map/ppermute | solution.py:1152
  7.1 23.2 %collective-permute-start.7 = (bf16[4,96,768]{2,1,0:T(8,128)(2,1)}, bf16[4,96,768]{2,1,0:T(8,128)(2,1)}, u32[]{:S(2)}, u32[]{:S(2)}) collective-permute-start(bf16[4,96,768]{2,1,0:T(8,128)(2,1)} %pad_maximum_fusion.11.refs_0_), channel_id=1, source_target_pairs={{0,4},{1,5},{2,6},{3,7},{4,0},{5,1},{6,2},{7,3},{8,12},{9,13},{10,... | collective-permute-start | bytes 1769480 | tf_op jit(solution)/shard_map/ppermute | solution.py:1152
  30.3 19.0 %collective-permute-start.9 = (bf16[2,4,96,768]{3,2,1,0:T(8,128)(2,1)}, bf16[2,4,96,768]{3,2,1,0:T(8,128)(2,1)S(1)}, u32[]{:S(2)}, u32[]{:S(2)}) collective-permute-start(bf16[2,4,96,768]{3,2,1,0:T(8,128)(2,1)} %pad_maximum_fusion.5), channel_id=1, source_target_pairs={{0,8},{1,9},{2,10},{3,11},{4,12},{5,13},{6,14},{7,15},{8,0},{9,1},... | collective-permute-start | bytes 3538952 | tf_op jit(solution)/shard_map/ppermute | solution.py:1148
  30.5 18.8 %collective-permute-start.8 = (bf16[416,768]{1,0:T(8,128)(2,1)}, bf16[416,768]{1,0:T(8,128)(2,1)}, u32[]{:S(2)}, u32[]{:S(2)}) collective-permute-start(bf16[416,768]{1,0:T(8,128)(2,1)} %bitcast.5.refs_24_.cots), channel_id=1, source_target_pairs={{0,1},{1,2},{2,3},{3,0},{4,5},{5,6},{6,7},{7,4},{8,9},{9,10},{10,1... | collective-permute-start | bytes 1916936 | tf_op jit(solution)/shard_map/ppermute | solution.py:1162
  60.5 19.0 %collective-permute-start.20 = (bf16[2,4,96,768]{3,2,1,0:T(8,128)(2,1)S(1)}, bf16[2,4,96,768]{3,2,1,0:T(8,128)(2,1)}, u32[]{:S(2)}, u32[]{:S(2)}) collective-permute-start(bf16[2,4,96,768]{3,2,1,0:T(8,128)(2,1)S(1)} %pad_maximum_fusion.7), channel_id=1, source_target_pairs={{0,8},{1,9},{2,10},{3,11},{4,12},{5,13},{6,14},{7,15},{8,0},{9,1},... | collective-permute-start | bytes 3538952 | tf_op jit(solution)/shard_map/ppermute | solution.py:1148
  60.6 18.9 %collective-permute-start.17 = (bf16[416,768]{1,0:T(8,128)(2,1)}, bf16[416,768]{1,0:T(8,128)(2,1)}, u32[]{:S(2)}, u32[]{:S(2)}) collective-permute-start(bf16[416,768]{1,0:T(8,128)(2,1)} %collective-permute-done.8.refs_25_), channel_id=1, source_target_pairs={{0,1},{1,2},{2,3},{3,0},{4,5},{5,6},{6,7},{7,4},{8,9},{9,10},{10,1... | collective-permute-start | bytes 1916936 | tf_op jit(solution)/shard_map/ppermute | solution.py:1162
  79.5 18.8 %collective-permute-start.23 = (bf16[416,768]{1,0:T(8,128)(2,1)}, bf16[416,768]{1,0:T(8,128)(2,1)}, u32[]{:S(2)}, u32[]{:S(2)}) collective-permute-start(bf16[416,768]{1,0:T(8,128)(2,1)} %bitcast.5.refs_24_.cots), channel_id=1, source_target_pairs={{0,8},{1,9},{2,10},{3,11},{4,12},{5,13},{6,14},{7,15},{8,0},{9,1},... | collective-permute-start | bytes 1916936 | tf_op jit(solution)/shard_map/ppermute | solution.py:1148
  79.5 18.8 %collective-permute-start.24 = (bf16[416,768]{1,0:T(8,128)(2,1)}, bf16[416,768]{1,0:T(8,128)(2,1)}, u32[]{:S(2)}, u32[]{:S(2)}) collective-permute-start(bf16[416,768]{1,0:T(8,128)(2,1)} %collective-permute-done.8.refs_25_), channel_id=1, source_target_pairs={{0,8},{1,9},{2,10},{3,11},{4,12},{5,13},{6,14},{7,15},{8,0},{9,1},... | collective-permute-start | bytes 1916936 | tf_op jit(solution)/shard_map/ppermute | solution.py:1148
  80.0 18.4 %collective-permute-start.22 = (bf16[416,768]{1,0:T(8,128)(2,1)}, bf16[416,768]{1,0:T(8,128)(2,1)}, u32[]{:S(2)}, u32[]{:S(2)}) collective-permute-start(bf16[416,768]{1,0:T(8,128)(2,1)} %collective-permute-done.17.refs_26_), channel_id=1, source_target_pairs={{0,1},{1,2},{2,3},{3,0},{4,5},{5,6},{6,7},{7,4},{8,9},{9,10},{10,1... | collective-permute-start | bytes 1916936 | tf_op jit(solution)/shard_map/ppermute | solution.py:1162
  80.0 18.2 %collective-permute-start.25 = (bf16[4,96,768]{2,1,0:T(8,128)(2,1)}, bf16[4,96,768]{2,1,0:T(8,128)(2,1)S(1)}, u32[]{:S(2)}, u32[]{:S(2)}) collective-permute-start(bf16[4,96,768]{2,1,0:T(8,128)(2,1)} %collective-permute-done.3.refs_12_.refs_4_), channel_id=1, source_target_pairs={{0,4},{1,5},{2,6},{3,7},{4,0},{5,1},{6,2},{7,3},{8,12},{9,13},{10,... | collective-permute-start | bytes 1769480 | tf_op jit(solution)/shard_map/ppermute | solution.py:1152
  81.4 16.9 %collective-permute-start.26 = (bf16[4,96,768]{2,1,0:T(8,128)(2,1)}, bf16[4,96,768]{2,1,0:T(8,128)(2,1)}, u32[]{:S(2)}, u32[]{:S(2)}) collective-permute-start(bf16[4,96,768]{2,1,0:T(8,128)(2,1)} %collective-permute-done.7.refs_2_), channel_id=1, source_target_pairs={{0,16},{1,17},{2,18},{3,19},{4,20},{5,21},{6,22},{7,23},{8,24},{9,... | collective-permute-start | bytes 1769480 | tf_op jit(solution)/shard_map/ppermute | solution.py:1152
  104.1 18.1 %collective-permute-start.30 = (bf16[416,768]{1,0:T(8,128)(2,1)S(1)}, bf16[416,768]{1,0:T(8,128)(2,1)S(1)}, u32[]{:S(2)}, u32[]{:S(2)}) collective-permute-start(bf16[416,768]{1,0:T(8,128)(2,1)S(1)} %copy-done.58), channel_id=1, source_target_pairs={{0,1},{1,2},{2,3},{3,0},{4,5},{5,6},{6,7},{7,4},{8,9},{9,10},{10,1... | collective-permute-start | bytes 1916936 | tf_op jit(solution)/shard_map/ppermute | solution.py:1162
  122.2 18.6 %collective-permute-start.34 = (bf16[416,768]{1,0:T(8,128)(2,1)S(1)}, bf16[416,768]{1,0:T(8,128)(2,1)S(1)}, u32[]{:S(2)}, u32[]{:S(2)}) collective-permute-start(bf16[416,768]{1,0:T(8,128)(2,1)S(1)} %collective-permute-done.30.refs_17_), channel_id=1, source_target_pairs={{0,1},{1,2},{2,3},{3,0},{4,5},{5,6},{6,7},{7,4},{8,9},{9,10},{10,1... | collective-permute-start | bytes 1916936 | tf_op jit(solution)/shard_map/ppermute | solution.py:1162
  140.8 16.5 %collective-permute-start.40 = (bf16[416,768]{1,0:T(8,128)(2,1)S(1)}, bf16[416,768]{1,0:T(8,128)(2,1)S(1)}, u32[]{:S(2)}, u32[]{:S(2)}) collective-permute-start(bf16[416,768]{1,0:T(8,128)(2,1)S(1)} %collective-permute-done.34.refs_18_), channel_id=1, source_target_pairs={{0,8},{1,9},{2,10},{3,11},{4,12},{5,13},{6,14},{7,15},{8,0},{9,1},... | collective-permute-start | bytes 1916936 | tf_op jit(solution)/shard_map/ppermute | solution.py:1148
  140.8 19.0 %collective-permute-start.38 = (bf16[416,768]{1,0:T(8,128)(2,1)S(1)}, bf16[416,768]{1,0:T(8,128)(2,1)S(1)}, u32[]{:S(2)}, u32[]{:S(2)}) collective-permute-start(bf16[416,768]{1,0:T(8,128)(2,1)S(1)} %collective-permute-done.34.refs_18_), channel_id=1, source_target_pairs={{0,1},{1,2},{2,3},{3,0},{4,5},{5,6},{6,7},{7,4},{8,9},{9,10},{10,1... | collective-permute-start | bytes 1916936 | tf_op jit(solution)/shard_map/ppermute | solution.py:1162
  161.9 52.0 %collective-permute-start.43 = (bf16[4,96,768]{2,1,0:T(8,128)(2,1)}, bf16[4,96,768]{2,1,0:T(8,128)(2,1)S(1)}, u32[]{:S(2)}, u32[]{:S(2)}) collective-permute-start(bf16[4,96,768]{2,1,0:T(8,128)(2,1)} %get-tuple-element.807), channel_id=1, source_target_pairs={{0,4},{1,5},{2,6},{3,7},{4,0},{5,1},{6,2},{7,3},{8,12},{9,13},{10,... | collective-permute-start | bytes 1769480 | tf_op jit(solution)/shard_map/ppermute | solution.py:1152
  162.4 51.5 %collective-permute-start.44 = (bf16[4,96,768]{2,1,0:T(8,128)(2,1)}, bf16[4,96,768]{2,1,0:T(8,128)(2,1)S(1)}, u32[]{:S(2)}, u32[]{:S(2)}) collective-permute-start(bf16[4,96,768]{2,1,0:T(8,128)(2,1)} %get-tuple-element.808), channel_id=1, source_target_pairs={{0,16},{1,17},{2,18},{3,19},{4,20},{5,21},{6,22},{7,23},{8,24},{9,... | collective-permute-start | bytes 1769480 | tf_op jit(solution)/shard_map/ppermute | solution.py:1152
  163.3 50.7 %collective-permute-start.45 = (bf16[4,96,768]{2,1,0:T(8,128)(2,1)}, bf16[4,96,768]{2,1,0:T(8,128)(2,1)}, u32[]{:S(2)}, u32[]{:S(2)}) collective-permute-start(bf16[4,96,768]{2,1,0:T(8,128)(2,1)} %get-tuple-element.809), channel_id=1, source_target_pairs={{0,20},{1,21},{2,22},{3,23},{4,16},{5,17},{6,18},{7,19},{8,28},{9,... | collective-permute-start | bytes 1769480 | tf_op jit(solution)/shard_map/ppermute | solution.py:1152
  215.0 27.4 %collective-permute-start.46 = (bf16[768,768]{1,0:T(8,128)(2,1)}, bf16[768,768]{1,0:T(8,128)(2,1)S(1)}, u32[]{:S(2)}, u32[]{:S(2)}) collective-permute-start(bf16[768,768]{1,0:T(8,128)(2,1)} %get-tuple-element.821), channel_id=1, source_target_pairs={{0,4},{1,5},{2,6},{3,7},{4,0},{5,1},{6,2},{7,3},{8,12},{9,13},{10,... | collective-permute-start | bytes 3538952 | tf_op jit(solution)/shard_map/ppermute | solution.py:1152
  216.7 27.3 %collective-permute-start.47 = (bf16[768,768]{1,0:T(8,128)(2,1)}, bf16[768,768]{1,0:T(8,128)(2,1)}, u32[]{:S(2)}, u32[]{:S(2)}) collective-permute-start(bf16[768,768]{1,0:T(8,128)(2,1)} %get-tuple-element.822), channel_id=1, source_target_pairs={{0,16},{1,17},{2,18},{3,19},{4,20},{5,21},{6,22},{7,23},{8,24},{9,... | collective-permute-start | bytes 3538952 | tf_op jit(solution)/shard_map/ppermute | solution.py:1152
  250.7 54.0 %collective-permute-start.49 = (bf16[2,768,768]{2,1,0:T(8,128)(2,1)}, bf16[2,768,768]{2,1,0:T(8,128)(2,1)}, u32[]{:S(2)}, u32[]{:S(2)}) collective-permute-start(bf16[2,768,768]{2,1,0:T(8,128)(2,1)} %fusion.3), channel_id=1, source_target_pairs={{0,4},{1,5},{2,6},{3,7},{4,0},{5,1},{6,2},{7,3},{8,12},{9,13},{10,... | collective-permute-start | bytes 7077896 | tf_op jit(solution)/shard_map/ppermute | solution.py:1152
  250.9 53.7 %collective-permute-start.50 = (bf16[2,768,768]{2,1,0:T(8,128)(2,1)}, bf16[2,768,768]{2,1,0:T(8,128)(2,1)}, u32[]{:S(2)}, u32[]{:S(2)}) collective-permute-start(bf16[2,768,768]{2,1,0:T(8,128)(2,1)} %fusion.5), channel_id=1, source_target_pairs={{0,16},{1,17},{2,18},{3,19},{4,20},{5,21},{6,22},{7,23},{8,24},{9,... | collective-permute-start | bytes 7077896 | tf_op jit(solution)/shard_map/ppermute | solution.py:1152
  254.6 24.6 %collective-permute-start.53 = (bf16[416,768]{1,0:T(8,128)(2,1)}, bf16[416,768]{1,0:T(8,128)(2,1)}, u32[]{:S(2)}, u32[]{:S(2)}) collective-permute-start(bf16[416,768]{1,0:T(8,128)(2,1)} %get-tuple-element.1187), channel_id=1, source_target_pairs={{0,1},{1,2},{2,3},{3,0},{4,5},{5,6},{6,7},{7,4},{8,9},{9,10},{10,1... | collective-permute-start | bytes 1916936 | tf_op jit(solution)/shard_map/ppermute | solution.py:1197
  254.6 45.9 %collective-permute-start.52 = (bf16[416,768]{1,0:T(8,128)(2,1)}, bf16[416,768]{1,0:T(8,128)(2,1)}, u32[]{:S(2)}, u32[]{:S(2)}) collective-permute-start(bf16[416,768]{1,0:T(8,128)(2,1)} %get-tuple-element.1188), channel_id=1, source_target_pairs={{0,2},{1,3},{2,0},{3,1},{4,6},{5,7},{6,4},{7,5},{8,10},{9,11},{10,... | collective-permute-start | bytes 1916936 | tf_op jit(solution)/shard_map/ppermute | solution.py:1197
  256.5 43.9 %collective-permute-start.51 = (bf16[416,768]{1,0:T(8,128)(2,1)S(1)}, bf16[416,768]{1,0:T(8,128)(2,1)}, u32[]{:S(2)}, u32[]{:S(2)}) collective-permute-start(bf16[416,768]{1,0:T(8,128)(2,1)S(1)} %get-tuple-element.1189), channel_id=1, source_target_pairs={{0,3},{1,0},{2,1},{3,2},{4,7},{5,4},{6,5},{7,6},{8,11},{9,8},{10,9... | collective-permute-start | bytes 1916936 | tf_op jit(solution)/shard_map/ppermute | solution.py:1197
  313.7 42.9 %collective-permute-start.56 = (bf16[768,768]{1,0:T(8,128)(2,1)}, bf16[768,768]{1,0:T(8,128)(2,1)}, u32[]{:S(2)}, u32[]{:S(2)}) collective-permute-start(bf16[768,768]{1,0:T(8,128)(2,1)} %get-tuple-element.1064.refs_5_), channel_id=1, source_target_pairs={{3,0},{0,1},{7,4},{4,5},{9,10},{10,11},{13,14},{14,15},{19,16},{16... | collective-permute-start | bytes 3538952 | tf_op jit(solution)/shard_map/ppermute | solution.py:1178
  324.8 31.9 %collective-permute-start.55 = (bf16[768,768]{1,0:T(8,128)(2,1)}, bf16[768,768]{1,0:T(8,128)(2,1)}, u32[]{:S(2)}, u32[]{:S(2)}) collective-permute-start(bf16[768,768]{1,0:T(8,128)(2,1)} %get-tuple-element.1064.refs_5_), channel_id=1, source_target_pairs={{1,0},{2,1},{5,4},{6,5},{11,10},{8,11},{15,14},{12,15},{17,16},{18... | collective-permute-start | bytes 3538952 | tf_op jit(solution)/shard_map/ppermute | solution.py:1178
  326.1 30.6 %collective-permute-start.57 = (bf16[2,2,96,768]{3,2,1,0:T(8,128)(2,1)}, bf16[2,2,96,768]{3,2,1,0:T(8,128)(2,1)S(1)}, u32[]{:S(2)}, u32[]{:S(2)}) collective-permute-start(bf16[2,2,96,768]{3,2,1,0:T(8,128)(2,1)} %get-tuple-element.930), channel_id=1, source_target_pairs={{0,4},{1,5},{2,6},{3,7},{4,0},{5,1},{6,2},{7,3},{8,12},{9,13},{10,... | collective-permute-start | bytes 1769480 | tf_op jit(solution)/shard_map/ppermute | solution.py:1152
  326.5 30.1 %collective-permute-start.58 = (bf16[2,2,96,768]{3,2,1,0:T(8,128)(2,1)}, bf16[2,2,96,768]{3,2,1,0:T(8,128)(2,1)}, u32[]{:S(2)}, u32[]{:S(2)}) collective-permute-start(bf16[2,2,96,768]{3,2,1,0:T(8,128)(2,1)} %get-tuple-element.931), channel_id=1, source_target_pairs={{0,16},{1,17},{2,18},{3,19},{4,20},{5,21},{6,22},{7,23},{8,24},{9,... | collective-permute-start | bytes 1769480 | tf_op jit(solution)/shard_map/ppermute | solution.py:1152
  328.2 28.4 %collective-permute-start.59 = (bf16[2,2,96,768]{3,2,1,0:T(8,128)(2,1)}, bf16[2,2,96,768]{3,2,1,0:T(8,128)(2,1)}, u32[]{:S(2)}, u32[]{:S(2)}) collective-permute-start(bf16[2,2,96,768]{3,2,1,0:T(8,128)(2,1)} %get-tuple-element.932), channel_id=1, source_target_pairs={{0,20},{1,21},{2,22},{3,23},{4,16},{5,17},{6,18},{7,19},{8,28},{9,... | collective-permute-start | bytes 1769480 | tf_op jit(solution)/shard_map/ppermute | solution.py:1152
  356.7 26.6 %collective-permute-start.62 = (bf16[4,4,2,48,768]{4,3,2,1,0:T(8,128)(2,1)}, bf16[4,4,2,48,768]{4,3,2,1,0:T(8,128)(2,1)S(1)}, u32[]{:S(2)}, u32[]{:S(2)}) collective-permute-start(bf16[4,4,2,48,768]{4,3,2,1,0:T(8,128)(2,1)} %get-tuple-element.939), channel_id=1, source_target_pairs={{0,8},{1,9},{2,10},{3,11},{4,12},{5,13},{6,14},{7,15},{8,0},{9,1},... | collective-permute-start | bytes 7077896 | tf_op jit(solution)/shard_map/ppermute | solution.py:1148
  359.0 24.3 %collective-permute-start.63 = (bf16[4,2,96,768]{3,2,1,0:T(8,128)(2,1)S(1)}, bf16[4,2,96,768]{3,2,1,0:T(8,128)(2,1)S(1)}, u32[]{:S(2)}, u32[]{:S(2)}) collective-permute-start(bf16[4,2,96,768]{3,2,1,0:T(8,128)(2,1)S(1)} %get-tuple-element.1197), channel_id=1, source_target_pairs={{0,8},{1,9},{2,10},{3,11},{4,12},{5,13},{6,14},{7,15},{8,0},{9,1},... | collective-permute-start | bytes 3538952 | tf_op jit(solution)/shard_map/ppermute | solution.py:1148
  360.0 19.0 %collective-permute-start.60 = (bf16[256,768]{1,0:T(8,128)(2,1)S(1)}, bf16[256,768]{1,0:T(8,128)(2,1)S(1)}, u32[]{:S(2)}, u32[]{:S(2)}) collective-permute-start(bf16[256,768]{1,0:T(8,128)(2,1)S(1)} %copy-done.78), channel_id=1, source_target_pairs={{2,0},{3,1},{6,4},{7,5},{8,10},{9,11},{12,14},{13,15},{18,16},{19,... | collective-permute-start | bytes 1179656 | tf_op jit(solution)/shard_map/ppermute | solution.py:1178
  361.3 21.9 %collective-permute-start.61 = (bf16[256,768]{1,0:T(8,128)(2,1)S(1)}, bf16[256,768]{1,0:T(8,128)(2,1)S(1)}, u32[]{:S(2)}, u32[]{:S(2)}) collective-permute-start(bf16[256,768]{1,0:T(8,128)(2,1)S(1)} %copy-done.77), channel_id=1, source_target_pairs={{2,0},{3,1},{6,4},{7,5},{8,10},{9,11},{12,14},{13,15},{18,16},{19,... | collective-permute-start | bytes 1179656 | tf_op jit(solution)/shard_map/ppermute | solution.py:1178
  383.3 19.6 %collective-permute-start.67 = (bf16[416,768]{1,0:T(8,128)(2,1)}, bf16[416,768]{1,0:T(8,128)(2,1)}, u32[]{:S(2)}, u32[]{:S(2)}) collective-permute-start(bf16[416,768]{1,0:T(8,128)(2,1)} %get-tuple-element.967), channel_id=1, source_target_pairs={{0,3},{1,0},{2,1},{3,2},{4,7},{5,4},{6,5},{7,6},{8,11},{9,8},{10,9... | collective-permute-start | bytes 1916936 | tf_op jit(solution)/shard_map/ppermute | solution.py:1197
  386.5 16.4 %collective-permute-start.66 = (bf16[4,2,48,768]{3,2,1,0:T(8,128)(2,1)}, bf16[4,2,48,768]{3,2,1,0:T(8,128)(2,1)}, u32[]{:S(2)}, u32[]{:S(2)}) collective-permute-start(bf16[4,2,48,768]{3,2,1,0:T(8,128)(2,1)} %get-tuple-element.1180), channel_id=1, source_target_pairs={{0,16},{1,17},{2,18},{3,19},{4,20},{5,21},{6,22},{7,23},{8,24},{9,... | collective-permute-start | bytes 1769480 | tf_op jit(solution)/shard_map/ppermute | solution.py:1152
  418.6 20.9 %collective-permute-start.75 = (bf16[4,32,768]{2,1,0:T(8,128)(2,1)}, bf16[4,32,768]{2,1,0:T(8,128)(2,1)S(1)}, u32[]{:S(2)}, u32[]{:S(2)}) collective-permute-start(bf16[4,32,768]{2,1,0:T(8,128)(2,1)} %get-tuple-element.1261), channel_id=1, source_target_pairs={{0,1},{1,2},{2,3},{3,0},{4,5},{5,6},{6,7},{7,4},{8,9},{9,10},{10,1... | collective-permute-start | bytes 589832 | tf_op jit(solution)/shard_map/ppermute | solution.py:1197
  418.7 20.9 %collective-permute-start.73 = (bf16[4,32,768]{2,1,0:T(8,128)(2,1)}, bf16[4,32,768]{2,1,0:T(8,128)(2,1)S(1)}, u32[]{:S(2)}, u32[]{:S(2)}) collective-permute-start(bf16[4,32,768]{2,1,0:T(8,128)(2,1)} %get-tuple-element.1262), channel_id=1, source_target_pairs={{0,3},{1,0},{2,1},{3,2},{4,7},{5,4},{6,5},{7,6},{8,11},{9,8},{10,9... | collective-permute-start | bytes 589832 | tf_op jit(solution)/shard_map/ppermute | solution.py:1197
  422.5 17.1 %collective-permute-start.74 = (bf16[4,32,768]{2,1,0:T(8,128)(2,1)}, bf16[4,32,768]{2,1,0:T(8,128)(2,1)}, u32[]{:S(2)}, u32[]{:S(2)}) collective-permute-start(bf16[4,32,768]{2,1,0:T(8,128)(2,1)} %get-tuple-element.1263), channel_id=1, source_target_pairs={{0,2},{1,3},{2,0},{3,1},{4,6},{5,7},{6,4},{7,5},{8,10},{9,11},{10,... | collective-permute-start | bytes 589832 | tf_op jit(solution)/shard_map/ppermute | solution.py:1197
  444.0 18.2 %collective-permute-start.78 = (bf16[4,24,768]{2,1,0:T(8,128)(2,1)S(1)}, bf16[4,24,768]{2,1,0:T(8,128)(2,1)}, u32[]{:S(2)}, u32[]{:S(2)}) collective-permute-start(bf16[4,24,768]{2,1,0:T(8,128)(2,1)S(1)} %pad_maximum_fusion.24), channel_id=1, source_target_pairs={{0,3},{1,0},{2,1},{3,2},{4,7},{5,4},{6,5},{7,6},{8,11},{9,8},{10,9... | collective-permute-start | bytes 442376 | tf_op jit(solution)/shard_map/ppermute | solution.py:1197
  445.0 17.3 %collective-permute-start.77 = (bf16[4,24,768]{2,1,0:T(8,128)(2,1)S(1)}, bf16[4,24,768]{2,1,0:T(8,128)(2,1)}, u32[]{:S(2)}, u32[]{:S(2)}) collective-permute-start(bf16[4,24,768]{2,1,0:T(8,128)(2,1)S(1)} %pad_maximum_fusion.24), channel_id=1, source_target_pairs={{0,2},{1,3},{2,0},{3,1},{4,6},{5,7},{6,4},{7,5},{8,10},{9,11},{10,... | collective-permute-start | bytes 442376 | tf_op jit(solution)/shard_map/ppermute | solution.py:1197
  462.3 22.5 %collective-permute-start.80 = (bf16[6,256,256]{2,1,0:T(8,128)(2,1)}, bf16[6,256,256]{2,1,0:T(8,128)(2,1)S(1)}, u32[]{:S(2)}, u32[]{:S(2)}) collective-permute-start(bf16[6,256,256]{2,1,0:T(8,128)(2,1)} %wide_last.1.refs_0_), channel_id=1, source_target_pairs={{0,3},{1,0},{4,7},{5,4},{10,9},{11,10},{14,13},{15,14},{16,19},{17... | collective-permute-start | bytes 2359304 | tf_op jit(solution)/shard_map/ppermute | solution.py:1183
  466.1 19.4 %collective-permute-start.79 = (bf16[6,256,256]{2,1,0:T(8,128)(2,1)}, bf16[6,256,256]{2,1,0:T(8,128)(2,1)S(1)}, u32[]{:S(2)}, u32[]{:S(2)}) collective-permute-start(bf16[6,256,256]{2,1,0:T(8,128)(2,1)} %wide_last.1.refs_0_), channel_id=1, source_target_pairs={{0,1},{1,2},{4,5},{5,6},{10,11},{11,8},{14,15},{15,12},{16,17},{17... | collective-permute-start | bytes 2359304 | tf_op jit(solution)/shard_map/ppermute | solution.py:1183
  496.9 35.2 %collective-permute-start.86 = (bf16[2,2,96,768]{3,2,1,0:T(8,128)(2,1)}, bf16[2,2,96,768]{3,2,1,0:T(8,128)(2,1)}, u32[]{:S(2)}, u32[]{:S(2)}) collective-permute-start(bf16[2,2,96,768]{3,2,1,0:T(8,128)(2,1)} %get-tuple-element.1082), channel_id=1, source_target_pairs={{0,4},{1,5},{2,6},{3,7},{4,0},{5,1},{6,2},{7,3},{8,12},{9,13},{10,... | collective-permute-start | bytes 1769480 | tf_op jit(solution)/shard_map/ppermute | solution.py:1152
  498.0 34.1 %collective-permute-start.87 = (bf16[2,2,96,768]{3,2,1,0:T(8,128)(2,1)}, bf16[2,2,96,768]{3,2,1,0:T(8,128)(2,1)}, u32[]{:S(2)}, u32[]{:S(2)}) collective-permute-start(bf16[2,2,96,768]{3,2,1,0:T(8,128)(2,1)} %get-tuple-element.1083), channel_id=1, source_target_pairs={{0,16},{1,17},{2,18},{3,19},{4,20},{5,21},{6,22},{7,23},{8,24},{9,... | collective-permute-start | bytes 1769480 | tf_op jit(solution)/shard_map/ppermute | solution.py:1152
  499.1 33.0 %collective-permute-start.88 = (bf16[2,2,96,768]{3,2,1,0:T(8,128)(2,1)}, bf16[2,2,96,768]{3,2,1,0:T(8,128)(2,1)}, u32[]{:S(2)}, u32[]{:S(2)}) collective-permute-start(bf16[2,2,96,768]{3,2,1,0:T(8,128)(2,1)} %get-tuple-element.1084), channel_id=1, source_target_pairs={{0,20},{1,21},{2,22},{3,23},{4,16},{5,17},{6,18},{7,19},{8,28},{9,... | collective-permute-start | bytes 1769480 | tf_op jit(solution)/shard_map/ppermute | solution.py:1152
  501.6 35.3 %collective-permute-start.89 = (bf16[416,768]{1,0:T(8,128)(2,1)S(1)}, bf16[416,768]{1,0:T(8,128)(2,1)S(1)}, u32[]{:S(2)}, u32[]{:S(2)}) collective-permute-start(bf16[416,768]{1,0:T(8,128)(2,1)S(1)} %add_convert_fusion.2), channel_id=1, source_target_pairs={{0,3},{1,0},{2,1},{3,2},{4,7},{5,4},{6,5},{7,6},{8,11},{9,8},{10,9... | collective-permute-start | bytes 1916936 | tf_op jit(solution)/shard_map/ppermute | solution.py:1197
  514.1 22.9 %collective-permute-start.90 = (bf16[416,768]{1,0:T(8,128)(2,1)S(1)}, bf16[416,768]{1,0:T(8,128)(2,1)S(1)}, u32[]{:S(2)}, u32[]{:S(2)}) collective-permute-start(bf16[416,768]{1,0:T(8,128)(2,1)S(1)} %copy-done.23), channel_id=1, source_target_pairs={{0,1},{1,2},{2,3},{3,0},{4,5},{5,6},{6,7},{7,4},{8,9},{9,10},{10,1... | collective-permute-start | bytes 1916936 | tf_op jit(solution)/shard_map/ppermute | solution.py:1162
  (127 other events, 1175.1 us)

commit v5 on v4

--- a/solution.py
+++ b/solution.py
@@ -434,7 +434,12 @@
     for place, band in enumerate(bands):
         gram[band, :] = gram[band, :] * (factor * factor)
         whole[band, :] = jnp.where(rows + place * TILE == cols, factor, 0.0)
-    wide_steps(2, gram, whole, low, whole_low, mixer)
+    wide_mix(gram, whole, low, whole_low, mixer)
+    for band in bands:
+        half = first_coef * gram[band, :] + dot_nn(mixer[band, :], low[...])
+        gram[band, :] = first_coef * half + dot_nn(half.astype(jnp.bfloat16), mixer[...])
+        whole[band, :] = first_coef * whole[band, :] + factor * mixer[band, :].astype(jnp.float32)
+    wide_steps(1, gram, whole, low, whole_low, mixer)
 
 
 def wide_last_kernel(gram_in, whole_in, out, gram, whole, low, mixer, whole_low):

time: 568 us -> 568 us (level)
  transfers between devices with their start and end apart: 95 -> 95, of which waited for: 35 -> 34; matrix products, arithmetic and copies ran while one was open for 9% -> 9% of each run, Pallas kernels for 33% -> 33%
where the time goes in v5:
time: 568 us; the launch traced here: 560 us
  Pallas kernels  191 us (34%)
  waiting for transfers between devices  174 us (31%)
  starting transfers between devices  110 us (19%)
  other arithmetic  51.4 us (9%)
  local copies, waits for them, and re-layouts  29.3 us (5%)
    ppermute x43, waiting for transfers between devices, swap_chip(): lax.ppermute(value, axes, route_to(lambda s, c, t: (s ^ turn & 2, c ^ tur...  98.6 us
    ppermute x43, starting transfers between devices, swap_chip(): lax.ppermute(value, axes, route_to(lambda s, c, t: (s ^ turn & 2, c ^ tur...  49.4 us
    pallas_call x1, Pallas kernels, experts_pass(): pl.pallas_call(experts_kernel, grid_spec=pltpu.PrefetchScalarGridSpec(num...  48.1 us
    pallas_call x2, Pallas kernels, tokens_pass(): pl.pallas_call(functools.partial(tokens_kernel, gated), grid_spec=pltpu.P...  40.7 us
    ppermute x17, starting transfers between devices, pass_by(): lax.ppermute(value, axes, route_to(lambda s, c, t: (s, c, t + steps)))  34 us
    ppermute x17, waiting for transfers between devices, pass_by(): lax.ppermute(value, axes, route_to(lambda s, c, t: (s, c, t + steps)))  33.9 us
    pallas_call x2, Pallas kernels, wide_call(): pl.pallas_call(kernel, out_shape=out_shape, in_specs=[vmem] * len(inputs)...  29.3 us
    pallas_call x1, Pallas kernels, attention_backward(): pl.pallas_call(backward_kernel, in_specs=[pl.BlockSpec(memory_space=pltpu...  27 us
  transfers between devices with their start and end apart: 95, of which 34 were waited for; matrix products, arithmetic and copies ran while one was open for 9% of the time, Pallas kernels for 33%

profile of v5, /device:TPU:0, one launch (start us, length us, event | category | flops | bytes accessed | tf_op | source)
XLA Modules:
  0.0 559.6 jit_solution(9280148211229037491)
XLA Ops:
  3.3 3.0 collective-permute-start.3
  8.9 3.7 collective-permute-start.6
  14.2 3.8 collective-permute-start.2
  22.7 7.6 %collective-permute-done.1 = bf16[4,24,768]{2,1,0:T(8,128)(2,1)} collective-permute-done((bf16[4,24,768]{2,1,0:T(8,128)(2,1)}, bf16[4,24,768]{2,1,0:T(8,128)(2,1)}, u32[]{:S(2)}, u32[]{:S(2)}) %collective-permute-start.1) | collective-permute-done | bytes 147488 | tf_op jit(solution)/shard_map/ppermute | solution.py:1202
  34.5 13.2 %collective-permute-done.12.w2 = bf16[4,96,768]{2,1,0:T(8,128)(2,1)S(1)} collective-permute-done((bf16[4,96,768]{2,1,0:T(8,128)(2,1)S(1)}, bf16[4,96,768]{2,1,0:T(8,128)(2,1)S(1)}, u32[]{:S(2)}, u32[]{:S(2)}) %collective-permute-start.12) | collective-permute-done | bytes 589856 | tf_op jit(solution)/shard_map/ppermute | solution.py:1157
  56.6 3.4 collective-permute-done.13
  65.9 11.7 %collective-permute-done.19 = f32[2,2,4,4,24]{4,3,2,1,0:T(4,128)S(1)} collective-permute-done((f32[2,2,4,4,24]{4,3,2,1,0:T(4,128)S(1)}, f32[2,2,4,4,24]{4,3,2,1,0:T(4,128)S(1)}, u32[]{:S(2)}, u32[]{:S(2)}) %collective-permute-start.19) | collective-permute-done | bytes 6176 | tf_op jit(solution)/shard_map/ppermute | solution.py:1157
  86.3 11.9 %attention_forward.1 = (bf16[416,768]{1,0:T(8,128)(2,1)}, bf16[3,416,768]{2,1,0:T(8,128)(2,1)}, bf16[416,768]{1,0:T(8,128)(2,1)}, f32[416,768]{1,0:T(8,128)}, bf...) custom-call(s32[3]{0:T(128)} %pad_add_fusion.place, bf16[416,768]{1,0:T(8,128)(2,1)} %bitcast.275, ...), custom_call_target="tpu_custom_call" | custom-call | flops 2453667840 | bytes 16777216 | tf_op jit(solution)/shard_map/attention_forward/pallas_call | solution.py:1001
  104.2 9.1 %collective-permute-done.29.refs_15_.refs_7_ = bf16[4,96,768]{2,1,0:T(8,128)(2,1)S(1)} collective-permute-done((bf16[4,96,768]{2,1,0:T(8,128)(2,1)}, bf16[4,96,768]{2,1,0:T(8,128)(2,1)S(1)}, u32[]{:S(2)}, u32[]{:S(2)}) %collective-permute-start.29) | collective-permute-done | bytes 589856 | tf_op jit(solution)/shard_map/ppermute | solution.py:1157
  113.2 3.1 collective-permute-done.31.refs_7_
  116.4 5.8 %collective-permute-done.30.refs_17_ = bf16[416,768]{1,0:T(8,128)(2,1)S(1)} collective-permute-done((bf16[416,768]{1,0:T(8,128)(2,1)S(1)}, bf16[416,768]{1,0:T(8,128)(2,1)S(1)}, u32[]{:S(2)}, u32[]{:S(2)}) %collective-permute-start.30) | collective-permute-done | bytes 639008 | tf_op jit(solution)/shard_map/ppermute | solution.py:1167
  123.7 14.4 %collective-permute-done.32.refs_10_.refs_2_ = bf16[4,96,768]{2,1,0:T(8,128)(2,1)S(1)} collective-permute-done((bf16[4,96,768]{2,1,0:T(8,128)(2,1)}, bf16[4,96,768]{2,1,0:T(8,128)(2,1)S(1)}, u32[]{:S(2)}, u32[]{:S(2)}) %collective-permute-start.32) | collective-permute-done | bytes 589856 | tf_op jit(solution)/shard_map/ppermute | solution.py:1157
  138.4 2.4 collective-permute-done.34.refs_18_
  144.3 12.5 %collective-permute-done.37.refs_11_.refs_3_ = bf16[4,96,768]{2,1,0:T(8,128)(2,1)S(1)} collective-permute-done((bf16[4,96,768]{2,1,0:T(8,128)(2,1)S(1)}, bf16[4,96,768]{2,1,0:T(8,128)(2,1)S(1)}, u32[]{:S(2)}, u32[]{:S(2)}) %collective-permute-start.37) | collective-permute-done | bytes 589856 | tf_op jit(solution)/shard_map/ppermute | solution.py:1157
  157.1 2.5 collective-permute-done.38.refs_19_
  159.5 2.1 collective-permute-done.42.refs_23_
  163.0 2.2 collective-permute-start.45
  165.2 48.1 %experts_pass.1 = (bf16[4,1792,768]{2,1,0:T(8,128)(2,1)}, bf16[4,1792,768]{2,1,0:T(8,128)(2,1)}, bf16[2,768,768]{2,1,0:T(8,128)(2,1)}, bf16[2,768,768]{2,1,0:T(8...) custom-call(s32[38]{0:T(128)} %pad_add_fusion.1.starts, ...), custom_call_target="tpu_custom_call" | custom-call | flops 15703474176 | bytes 62914560 | tf_op jit(solution)/shard_map/experts_pass/pallas_call | solution.py:852
  214.9 2.5 collective-permute-start.47
  217.3 20.0 %tokens_plain.1 = (bf16[4,416,768]{2,1,0:T(8,128)(2,1)}, bf16[4,416,768]{2,1,0:T(8,128)(2,1)}) custom-call(s32[38]{0:T(128)} %pad_add_fusion.1.starts, s32[4,8,416]{2,1,0:T(8,128)} %fusion.6.rank, f32[4,8,416]{2,1,0:T(8,128)} %fusion.17.gate, bf16[4,1792,768]{2,1,0:T(8,128)(2,1)} %get-tuple-element.834.acts, bf16[4,96,768]{2,1,0:T(8,128)(2,1)} %pad_maximum_fusion.11.refs_0_, ...), custom_call_target="tpu_custom_call" | custom-call | flops 7851737088 | bytes 31457280 | tf_op jit(solution)/shard_map/tokens_plain/pallas_call | solution.py:895
  237.3 5.2 collective-permute-done.46
  246.8 2.6 fusion.3
  258.6 20.7 %tokens_gated.1 = (bf16[4,416,768]{2,1,0:T(8,128)(2,1)}, bf16[4,416,768]{2,1,0:T(8,128)(2,1)}) custom-call(s32[38]{0:T(128)} %pad_add_fusion.1.starts, s32[4,8,416]{2,1,0:T(8,128)} %fusion.6.rank, f32[4,8,416]{2,1,0:T(8,128)} %fusion.17.gate, bf16[4,1792,768]{2,1,0:T(8,128)(2,1)} %get-tuple-element.880.acts, ...), custom_call_target="tpu_custom_call" | custom-call | flops 7851737088 | bytes 31457280 | tf_op jit(solution)/shard_map/tokens_gated/pallas_call | solution.py:895
  279.3 21.3 %collective-permute-done.52.second2 = bf16[416,768]{1,0:T(8,128)(2,1)} collective-permute-done((bf16[416,768]{1,0:T(8,128)(2,1)}, bf16[416,768]{1,0:T(8,128)(2,1)}, u32[]{:S(2)}, u32[]{:S(2)}) %collective-permute-start.52) | collective-permute-done | bytes 639008 | tf_op jit(solution)/shard_map/ppermute | solution.py:1202
  300.6 4.1 collective-permute-done.49.refs_0_
  304.7 9.1 %push_rows.1 = (bf16[768,768]{1,0:T(8,128)(2,1)}, bf16[768,768]{1,0:T(8,128)(2,1)}, bf16[256,768]{1,0:T(8,128)(2,1)}, bf16[256,768]{1,0:T(8,128)(2,1)}, bf16[256...) custom-call(s32[3]{0:T(128)} %pad_add_fusion.place, ...), custom_call_target="tpu_custom_call" | custom-call | flops 11796480 | bytes 14155776 | tf_op jit(solution)/shard_map/push_rows/pallas_call | solution.py:583
  313.8 11.1 %collective-permute-start.56 = (bf16[768,768]{1,0:T(8,128)(2,1)}, bf16[768,768]{1,0:T(8,128)(2,1)}, u32[]{:S(2)}, u32[]{:S(2)}) collective-permute-start(bf16[768,768]{1,0:T(8,128)(2,1)} %get-tuple-element.1064.refs_5_), channel_id=1, source_target_pairs={{3,0},{0,1},{7,4},{4,5},{9,10},{10,11},{13,14},{14,15},{19,16},{16... | collective-permute-start | bytes 3538952 | tf_op jit(solution)/shard_map/ppermute | solution.py:1183
  329.8 27.0 %attention_backward.1 = (f32[416,768]{1,0:T(8,128)}, bf16[4,4,2,48,768]{4,3,2,1,0:T(8,128)(2,1)}, bf16[4,4,2,48,768]{4,3,2,1,0:T(8,128)(2,1)}, f32[8,768]{1,0:T(8,128)}) custom-call(s32[3]{0:T(128)} %pad_add_fusion.place, bf16[416,768]{1,0:T(8,128)(2,1)} %bitcast.276, bf16[416,768]{1,0:T(8,128)(2,1)} %bitcast.5.refs_24_.cots, ...), custom_call_target="tpu_custom_call" | custom-call | flops 9814671360 | bytes 25165824 | tf_op jit(solution)/shard_map/attention_backward/pallas_call | solution.py:1110
  362.8 2.4 fusion.28
  367.7 11.5 %collective-permute-done.60.part0 = bf16[256,768]{1,0:T(8,128)(2,1)S(1)} collective-permute-done((bf16[256,768]{1,0:T(8,128)(2,1)S(1)}, bf16[256,768]{1,0:T(8,128)(2,1)S(1)}, u32[]{:S(2)}, u32[]{:S(2)}) %collective-permute-start.60) | collective-permute-done | bytes 393248 | tf_op jit(solution)/shard_map/ppermute | solution.py:1183
  379.2 4.2 collective-permute-done.61.part1
  389.0 14.1 %collective-permute-done.68 = f32[4,768]{1,0:T(4,128)} collective-permute-done((f32[4,768]{1,0:T(4,128)S(1)}, f32[4,768]{1,0:T(4,128)}, u32[]{:S(2)}, u32[]{:S(2)}) %collective-permute-start.68) | collective-permute-done | bytes 12320 | tf_op jit(solution)/shard_map/ppermute | solution.py:1157
  412.0 2.9 collective-permute-done.72
  414.9 2.3 collective-permute-done.71
  418.9 3.8 collective-permute-start.73
  423.1 15.9 %wide_first.1 = (f32[768,768]{1,0:T(8,128)}, f32[768,768]{1,0:T(8,128)}) custom-call(bf16[768,768]{1,0:T(8,128)(2,1)} %get-tuple-element.1063.block0.refs_4_, bf16[768,768]{1,0:T(8,128)(2,1)} %collective-permute-done.55.block1, bf16[768,768]{1,0:T(8,128)(2,1)} %collective-permute-done.56.block3, bf16[256,768]{1,0:T(8,128)(2,1)} %copy-done.75, ...), custom_call_target="tpu_custom_call" | custom-call | flops 9059696640 | bytes 4718592 | tf_op jit(solution)/shard_map/wide_first/pallas_call | solution.py:461
  446.2 2.1 collective-permute-start.76
  448.3 13.4 %wide_last.1.refs_0_ = bf16[6,256,256]{2,1,0:T(8,128)(2,1)} custom-call(f32[768,768]{1,0:T(8,128)} %get-tuple-element.1017.gram_in, f32[768,768]{1,0:T(8,128)} %get-tuple-element.1018.whole_in), custom_call_target="tpu_custom_call" | custom-call | flops 9059696640 | bytes 4718592 | tf_op jit(solution)/shard_map/wide_last/pallas_call | solution.py:461
  461.8 3.8 collective-permute-start.80
  465.6 2.1 collective-permute-start.79
  478.9 5.5 collective-permute-done.80.refs_3_
  486.1 2.0 collective-permute-done.85
  489.4 7.1 %apply_mixers.1 = (bf16[2,2,96,768]{3,2,1,0:T(8,128)(2,1)}, bf16[2,2,96,768]{3,2,1,0:T(8,128)(2,1)}, bf16[2,2,96,768]{3,2,1,0:T(8,128)(2,1)}, bf16[2,2,96,768]{3,2,1,0:T(8,128)(2,1)}) custom-call(s32[3]{0:T(128)} %pad_add_fusion.place, bf16[6,256,256]{2,1,0:T(8,128)(2,1)} %wide_last.1.refs_0_, bf16[6,256,256]{2,1,0:T(8,128)(2,1)} %copy-done.56, ...), custom_call_target="tpu_custom_call" | custom-call | flops 1811939328 | bytes 5898240 | tf_op jit(solution)/shard_map/apply_mixers/pallas_call | solution.py:529
  501.2 12.4 %collective-permute-start.89 = (bf16[416,768]{1,0:T(8,128)(2,1)S(1)}, bf16[416,768]{1,0:T(8,128)(2,1)S(1)}, u32[]{:S(2)}, u32[]{:S(2)}) collective-permute-start(bf16[416,768]{1,0:T(8,128)(2,1)S(1)} %add_convert_fusion.2), channel_id=1, source_target_pairs={{0,3},{1,0},{2,1},{3,2},{4,7},{5,4},{6,5},{7,6},{8,11},{9,8},{10,9... | collective-permute-start | bytes 1916936 | tf_op jit(solution)/shard_map/ppermute | solution.py:1202
  513.6 18.0 %square_orthogonal.1 = bf16[768,768]{1,0:T(8,128)(2,1)} custom-call(bf16[768,768]{1,0:T(8,128)(2,1)} %bitcast.274), custom_call_target="tpu_custom_call" | custom-call | flops 13589544960 | bytes 2359296 | tf_op jit(solution)/shard_map/square_orthogonal/pallas_call | solution.py:631
  531.6 4.9 collective-permute-done.89
  545.2 2.3 broadcast_in_dim_reshape.8
  551.8 2.1 convert_bitcast_fusion
  (450 shorter events, 140.2 us)
Async XLA Ops:
  3.3 27.0 %collective-permute-start.3 = (bf16[4,96,768]{2,1,0:T(8,128)(2,1)}, bf16[4,96,768]{2,1,0:T(8,128)(2,1)}, u32[]{:S(2)}, u32[]{:S(2)}) collective-permute-start(bf16[4,96,768]{2,1,0:T(8,128)(2,1)} %pad_maximum_fusion.10.refs_8_.refs_0_), channel_id=1, source_target_pairs={{0,16},{1,17},{2,18},{3,19},{4,20},{5,21},{6,22},{7,23},{8,24},{9,... | collective-permute-start | bytes 1769480 | tf_op jit(solution)/shard_map/ppermute | solution.py:1157
  7.1 23.2 %collective-permute-start.7 = (bf16[4,96,768]{2,1,0:T(8,128)(2,1)}, bf16[4,96,768]{2,1,0:T(8,128)(2,1)}, u32[]{:S(2)}, u32[]{:S(2)}) collective-permute-start(bf16[4,96,768]{2,1,0:T(8,128)(2,1)} %pad_maximum_fusion.11.refs_0_), channel_id=1, source_target_pairs={{0,4},{1,5},{2,6},{3,7},{4,0},{5,1},{6,2},{7,3},{8,12},{9,13},{10,... | collective-permute-start | bytes 1769480 | tf_op jit(solution)/shard_map/ppermute | solution.py:1157
  30.3 19.0 %collective-permute-start.9 = (bf16[2,4,96,768]{3,2,1,0:T(8,128)(2,1)}, bf16[2,4,96,768]{3,2,1,0:T(8,128)(2,1)S(1)}, u32[]{:S(2)}, u32[]{:S(2)}) collective-permute-start(bf16[2,4,96,768]{3,2,1,0:T(8,128)(2,1)} %pad_maximum_fusion.5), channel_id=1, source_target_pairs={{0,8},{1,9},{2,10},{3,11},{4,12},{5,13},{6,14},{7,15},{8,0},{9,1},... | collective-permute-start | bytes 3538952 | tf_op jit(solution)/shard_map/ppermute | solution.py:1153
  30.5 18.8 %collective-permute-start.8 = (bf16[416,768]{1,0:T(8,128)(2,1)}, bf16[416,768]{1,0:T(8,128)(2,1)}, u32[]{:S(2)}, u32[]{:S(2)}) collective-permute-start(bf16[416,768]{1,0:T(8,128)(2,1)} %bitcast.5.refs_24_.cots), channel_id=1, source_target_pairs={{0,1},{1,2},{2,3},{3,0},{4,5},{5,6},{6,7},{7,4},{8,9},{9,10},{10,1... | collective-permute-start | bytes 1916936 | tf_op jit(solution)/shard_map/ppermute | solution.py:1167
  60.5 19.0 %collective-permute-start.20 = (bf16[2,4,96,768]{3,2,1,0:T(8,128)(2,1)S(1)}, bf16[2,4,96,768]{3,2,1,0:T(8,128)(2,1)}, u32[]{:S(2)}, u32[]{:S(2)}) collective-permute-start(bf16[2,4,96,768]{3,2,1,0:T(8,128)(2,1)S(1)} %pad_maximum_fusion.7), channel_id=1, source_target_pairs={{0,8},{1,9},{2,10},{3,11},{4,12},{5,13},{6,14},{7,15},{8,0},{9,1},... | collective-permute-start | bytes 3538952 | tf_op jit(solution)/shard_map/ppermute | solution.py:1153
  60.6 18.9 %collective-permute-start.17 = (bf16[416,768]{1,0:T(8,128)(2,1)}, bf16[416,768]{1,0:T(8,128)(2,1)}, u32[]{:S(2)}, u32[]{:S(2)}) collective-permute-start(bf16[416,768]{1,0:T(8,128)(2,1)} %collective-permute-done.8.refs_25_), channel_id=1, source_target_pairs={{0,1},{1,2},{2,3},{3,0},{4,5},{5,6},{6,7},{7,4},{8,9},{9,10},{10,1... | collective-permute-start | bytes 1916936 | tf_op jit(solution)/shard_map/ppermute | solution.py:1167
  79.5 18.8 %collective-permute-start.23 = (bf16[416,768]{1,0:T(8,128)(2,1)}, bf16[416,768]{1,0:T(8,128)(2,1)}, u32[]{:S(2)}, u32[]{:S(2)}) collective-permute-start(bf16[416,768]{1,0:T(8,128)(2,1)} %bitcast.5.refs_24_.cots), channel_id=1, source_target_pairs={{0,8},{1,9},{2,10},{3,11},{4,12},{5,13},{6,14},{7,15},{8,0},{9,1},... | collective-permute-start | bytes 1916936 | tf_op jit(solution)/shard_map/ppermute | solution.py:1153
  79.5 18.8 %collective-permute-start.24 = (bf16[416,768]{1,0:T(8,128)(2,1)}, bf16[416,768]{1,0:T(8,128)(2,1)}, u32[]{:S(2)}, u32[]{:S(2)}) collective-permute-start(bf16[416,768]{1,0:T(8,128)(2,1)} %collective-permute-done.8.refs_25_), channel_id=1, source_target_pairs={{0,8},{1,9},{2,10},{3,11},{4,12},{5,13},{6,14},{7,15},{8,0},{9,1},... | collective-permute-start | bytes 1916936 | tf_op jit(solution)/shard_map/ppermute | solution.py:1153
  80.0 18.4 %collective-permute-start.22 = (bf16[416,768]{1,0:T(8,128)(2,1)}, bf16[416,768]{1,0:T(8,128)(2,1)}, u32[]{:S(2)}, u32[]{:S(2)}) collective-permute-start(bf16[416,768]{1,0:T(8,128)(2,1)} %collective-permute-done.17.refs_26_), channel_id=1, source_target_pairs={{0,1},{1,2},{2,3},{3,0},{4,5},{5,6},{6,7},{7,4},{8,9},{9,10},{10,1... | collective-permute-start | bytes 1916936 | tf_op jit(solution)/shard_map/ppermute | solution.py:1167
  80.0 18.2 %collective-permute-start.25 = (bf16[4,96,768]{2,1,0:T(8,128)(2,1)}, bf16[4,96,768]{2,1,0:T(8,128)(2,1)S(1)}, u32[]{:S(2)}, u32[]{:S(2)}) collective-permute-start(bf16[4,96,768]{2,1,0:T(8,128)(2,1)} %collective-permute-done.3.refs_12_.refs_4_), channel_id=1, source_target_pairs={{0,4},{1,5},{2,6},{3,7},{4,0},{5,1},{6,2},{7,3},{8,12},{9,13},{10,... | collective-permute-start | bytes 1769480 | tf_op jit(solution)/shard_map/ppermute | solution.py:1157
  81.4 16.9 %collective-permute-start.26 = (bf16[4,96,768]{2,1,0:T(8,128)(2,1)}, bf16[4,96,768]{2,1,0:T(8,128)(2,1)}, u32[]{:S(2)}, u32[]{:S(2)}) collective-permute-start(bf16[4,96,768]{2,1,0:T(8,128)(2,1)} %collective-permute-done.7.refs_2_), channel_id=1, source_target_pairs={{0,16},{1,17},{2,18},{3,19},{4,20},{5,21},{6,22},{7,23},{8,24},{9,... | collective-permute-start | bytes 1769480 | tf_op jit(solution)/shard_map/ppermute | solution.py:1157
  104.1 18.1 %collective-permute-start.30 = (bf16[416,768]{1,0:T(8,128)(2,1)S(1)}, bf16[416,768]{1,0:T(8,128)(2,1)S(1)}, u32[]{:S(2)}, u32[]{:S(2)}) collective-permute-start(bf16[416,768]{1,0:T(8,128)(2,1)S(1)} %copy-done.58), channel_id=1, source_target_pairs={{0,1},{1,2},{2,3},{3,0},{4,5},{5,6},{6,7},{7,4},{8,9},{9,10},{10,1... | collective-permute-start | bytes 1916936 | tf_op jit(solution)/shard_map/ppermute | solution.py:1167
  122.2 18.6 %collective-permute-start.34 = (bf16[416,768]{1,0:T(8,128)(2,1)S(1)}, bf16[416,768]{1,0:T(8,128)(2,1)S(1)}, u32[]{:S(2)}, u32[]{:S(2)}) collective-permute-start(bf16[416,768]{1,0:T(8,128)(2,1)S(1)} %collective-permute-done.30.refs_17_), channel_id=1, source_target_pairs={{0,1},{1,2},{2,3},{3,0},{4,5},{5,6},{6,7},{7,4},{8,9},{9,10},{10,1... | collective-permute-start | bytes 1916936 | tf_op jit(solution)/shard_map/ppermute | solution.py:1167
  140.8 16.3 %collective-permute-start.40 = (bf16[416,768]{1,0:T(8,128)(2,1)S(1)}, bf16[416,768]{1,0:T(8,128)(2,1)S(1)}, u32[]{:S(2)}, u32[]{:S(2)}) collective-permute-start(bf16[416,768]{1,0:T(8,128)(2,1)S(1)} %collective-permute-done.34.refs_18_), channel_id=1, source_target_pairs={{0,8},{1,9},{2,10},{3,11},{4,12},{5,13},{6,14},{7,15},{8,0},{9,1},... | collective-permute-start | bytes 1916936 | tf_op jit(solution)/shard_map/ppermute | solution.py:1153
  140.8 18.8 %collective-permute-start.38 = (bf16[416,768]{1,0:T(8,128)(2,1)S(1)}, bf16[416,768]{1,0:T(8,128)(2,1)S(1)}, u32[]{:S(2)}, u32[]{:S(2)}) collective-permute-start(bf16[416,768]{1,0:T(8,128)(2,1)S(1)} %collective-permute-done.34.refs_18_), channel_id=1, source_target_pairs={{0,1},{1,2},{2,3},{3,0},{4,5},{5,6},{6,7},{7,4},{8,9},{9,10},{10,1... | collective-permute-start | bytes 1916936 | tf_op jit(solution)/shard_map/ppermute | solution.py:1167
  161.6 51.7 %collective-permute-start.43 = (bf16[4,96,768]{2,1,0:T(8,128)(2,1)}, bf16[4,96,768]{2,1,0:T(8,128)(2,1)S(1)}, u32[]{:S(2)}, u32[]{:S(2)}) collective-permute-start(bf16[4,96,768]{2,1,0:T(8,128)(2,1)} %get-tuple-element.807), channel_id=1, source_target_pairs={{0,4},{1,5},{2,6},{3,7},{4,0},{5,1},{6,2},{7,3},{8,12},{9,13},{10,... | collective-permute-start | bytes 1769480 | tf_op jit(solution)/shard_map/ppermute | solution.py:1157
  162.2 51.1 %collective-permute-start.44 = (bf16[4,96,768]{2,1,0:T(8,128)(2,1)}, bf16[4,96,768]{2,1,0:T(8,128)(2,1)S(1)}, u32[]{:S(2)}, u32[]{:S(2)}) collective-permute-start(bf16[4,96,768]{2,1,0:T(8,128)(2,1)} %get-tuple-element.808), channel_id=1, source_target_pairs={{0,16},{1,17},{2,18},{3,19},{4,20},{5,21},{6,22},{7,23},{8,24},{9,... | collective-permute-start | bytes 1769480 | tf_op jit(solution)/shard_map/ppermute | solution.py:1157
  163.0 50.3 %collective-permute-start.45 = (bf16[4,96,768]{2,1,0:T(8,128)(2,1)}, bf16[4,96,768]{2,1,0:T(8,128)(2,1)}, u32[]{:S(2)}, u32[]{:S(2)}) collective-permute-start(bf16[4,96,768]{2,1,0:T(8,128)(2,1)} %get-tuple-element.809), channel_id=1, source_target_pairs={{0,20},{1,21},{2,22},{3,23},{4,16},{5,17},{6,18},{7,19},{8,28},{9,... | collective-permute-start | bytes 1769480 | tf_op jit(solution)/shard_map/ppermute | solution.py:1157
  214.3 28.2 %collective-permute-start.46 = (bf16[768,768]{1,0:T(8,128)(2,1)}, bf16[768,768]{1,0:T(8,128)(2,1)S(1)}, u32[]{:S(2)}, u32[]{:S(2)}) collective-permute-start(bf16[768,768]{1,0:T(8,128)(2,1)} %get-tuple-element.821), channel_id=1, source_target_pairs={{0,4},{1,5},{2,6},{3,7},{4,0},{5,1},{6,2},{7,3},{8,12},{9,13},{10,... | collective-permute-start | bytes 3538952 | tf_op jit(solution)/shard_map/ppermute | solution.py:1157
  214.9 29.2 %collective-permute-start.47 = (bf16[768,768]{1,0:T(8,128)(2,1)}, bf16[768,768]{1,0:T(8,128)(2,1)}, u32[]{:S(2)}, u32[]{:S(2)}) collective-permute-start(bf16[768,768]{1,0:T(8,128)(2,1)} %get-tuple-element.822), channel_id=1, source_target_pairs={{0,16},{1,17},{2,18},{3,19},{4,20},{5,21},{6,22},{7,23},{8,24},{9,... | collective-permute-start | bytes 3538952 | tf_op jit(solution)/shard_map/ppermute | solution.py:1157
  250.7 54.0 %collective-permute-start.49 = (bf16[2,768,768]{2,1,0:T(8,128)(2,1)}, bf16[2,768,768]{2,1,0:T(8,128)(2,1)}, u32[]{:S(2)}, u32[]{:S(2)}) collective-permute-start(bf16[2,768,768]{2,1,0:T(8,128)(2,1)} %fusion.3), channel_id=1, source_target_pairs={{0,4},{1,5},{2,6},{3,7},{4,0},{5,1},{6,2},{7,3},{8,12},{9,13},{10,... | collective-permute-start | bytes 7077896 | tf_op jit(solution)/shard_map/ppermute | solution.py:1157
  251.0 53.7 %collective-permute-start.50 = (bf16[2,768,768]{2,1,0:T(8,128)(2,1)}, bf16[2,768,768]{2,1,0:T(8,128)(2,1)}, u32[]{:S(2)}, u32[]{:S(2)}) collective-permute-start(bf16[2,768,768]{2,1,0:T(8,128)(2,1)} %fusion.5), channel_id=1, source_target_pairs={{0,16},{1,17},{2,18},{3,19},{4,20},{5,21},{6,22},{7,23},{8,24},{9,... | collective-permute-start | bytes 7077896 | tf_op jit(solution)/shard_map/ppermute | solution.py:1157
  254.8 24.5 %collective-permute-start.53 = (bf16[416,768]{1,0:T(8,128)(2,1)}, bf16[416,768]{1,0:T(8,128)(2,1)}, u32[]{:S(2)}, u32[]{:S(2)}) collective-permute-start(bf16[416,768]{1,0:T(8,128)(2,1)} %get-tuple-element.1187), channel_id=1, source_target_pairs={{0,1},{1,2},{2,3},{3,0},{4,5},{5,6},{6,7},{7,4},{8,9},{9,10},{10,1... | collective-permute-start | bytes 1916936 | tf_op jit(solution)/shard_map/ppermute | solution.py:1202
  254.8 45.9 %collective-permute-start.52 = (bf16[416,768]{1,0:T(8,128)(2,1)}, bf16[416,768]{1,0:T(8,128)(2,1)}, u32[]{:S(2)}, u32[]{:S(2)}) collective-permute-start(bf16[416,768]{1,0:T(8,128)(2,1)} %get-tuple-element.1188), channel_id=1, source_target_pairs={{0,2},{1,3},{2,0},{3,1},{4,6},{5,7},{6,4},{7,5},{8,10},{9,11},{10,... | collective-permute-start | bytes 1916936 | tf_op jit(solution)/shard_map/ppermute | solution.py:1202
  256.7 43.9 %collective-permute-start.51 = (bf16[416,768]{1,0:T(8,128)(2,1)S(1)}, bf16[416,768]{1,0:T(8,128)(2,1)}, u32[]{:S(2)}, u32[]{:S(2)}) collective-permute-start(bf16[416,768]{1,0:T(8,128)(2,1)S(1)} %get-tuple-element.1189), channel_id=1, source_target_pairs={{0,3},{1,0},{2,1},{3,2},{4,7},{5,4},{6,5},{7,6},{8,11},{9,8},{10,9... | collective-permute-start | bytes 1916936 | tf_op jit(solution)/shard_map/ppermute | solution.py:1202
  313.8 43.0 %collective-permute-start.56 = (bf16[768,768]{1,0:T(8,128)(2,1)}, bf16[768,768]{1,0:T(8,128)(2,1)}, u32[]{:S(2)}, u32[]{:S(2)}) collective-permute-start(bf16[768,768]{1,0:T(8,128)(2,1)} %get-tuple-element.1064.refs_5_), channel_id=1, source_target_pairs={{3,0},{0,1},{7,4},{4,5},{9,10},{10,11},{13,14},{14,15},{19,16},{16... | collective-permute-start | bytes 3538952 | tf_op jit(solution)/shard_map/ppermute | solution.py:1183
  324.9 31.9 %collective-permute-start.55 = (bf16[768,768]{1,0:T(8,128)(2,1)}, bf16[768,768]{1,0:T(8,128)(2,1)}, u32[]{:S(2)}, u32[]{:S(2)}) collective-permute-start(bf16[768,768]{1,0:T(8,128)(2,1)} %get-tuple-element.1064.refs_5_), channel_id=1, source_target_pairs={{1,0},{2,1},{5,4},{6,5},{11,10},{8,11},{15,14},{12,15},{17,16},{18... | collective-permute-start | bytes 3538952 | tf_op jit(solution)/shard_map/ppermute | solution.py:1183
  326.2 30.6 %collective-permute-start.57 = (bf16[2,2,96,768]{3,2,1,0:T(8,128)(2,1)}, bf16[2,2,96,768]{3,2,1,0:T(8,128)(2,1)S(1)}, u32[]{:S(2)}, u32[]{:S(2)}) collective-permute-start(bf16[2,2,96,768]{3,2,1,0:T(8,128)(2,1)} %get-tuple-element.930), channel_id=1, source_target_pairs={{0,4},{1,5},{2,6},{3,7},{4,0},{5,1},{6,2},{7,3},{8,12},{9,13},{10,... | collective-permute-start | bytes 1769480 | tf_op jit(solution)/shard_map/ppermute | solution.py:1157
  326.6 30.2 %collective-permute-start.58 = (bf16[2,2,96,768]{3,2,1,0:T(8,128)(2,1)}, bf16[2,2,96,768]{3,2,1,0:T(8,128)(2,1)}, u32[]{:S(2)}, u32[]{:S(2)}) collective-permute-start(bf16[2,2,96,768]{3,2,1,0:T(8,128)(2,1)} %get-tuple-element.931), channel_id=1, source_target_pairs={{0,16},{1,17},{2,18},{3,19},{4,20},{5,21},{6,22},{7,23},{8,24},{9,... | collective-permute-start | bytes 1769480 | tf_op jit(solution)/shard_map/ppermute | solution.py:1157
  328.3 28.5 %collective-permute-start.59 = (bf16[2,2,96,768]{3,2,1,0:T(8,128)(2,1)}, bf16[2,2,96,768]{3,2,1,0:T(8,128)(2,1)}, u32[]{:S(2)}, u32[]{:S(2)}) collective-permute-start(bf16[2,2,96,768]{3,2,1,0:T(8,128)(2,1)} %get-tuple-element.932), channel_id=1, source_target_pairs={{0,20},{1,21},{2,22},{3,23},{4,16},{5,17},{6,18},{7,19},{8,28},{9,... | collective-permute-start | bytes 1769480 | tf_op jit(solution)/shard_map/ppermute | solution.py:1157
  356.8 26.6 %collective-permute-start.62 = (bf16[4,4,2,48,768]{4,3,2,1,0:T(8,128)(2,1)}, bf16[4,4,2,48,768]{4,3,2,1,0:T(8,128)(2,1)S(1)}, u32[]{:S(2)}, u32[]{:S(2)}) collective-permute-start(bf16[4,4,2,48,768]{4,3,2,1,0:T(8,128)(2,1)} %get-tuple-element.939), channel_id=1, source_target_pairs={{0,8},{1,9},{2,10},{3,11},{4,12},{5,13},{6,14},{7,15},{8,0},{9,1},... | collective-permute-start | bytes 7077896 | tf_op jit(solution)/shard_map/ppermute | solution.py:1153
  359.2 24.3 %collective-permute-start.63 = (bf16[4,2,96,768]{3,2,1,0:T(8,128)(2,1)S(1)}, bf16[4,2,96,768]{3,2,1,0:T(8,128)(2,1)S(1)}, u32[]{:S(2)}, u32[]{:S(2)}) collective-permute-start(bf16[4,2,96,768]{3,2,1,0:T(8,128)(2,1)S(1)} %get-tuple-element.1197), channel_id=1, source_target_pairs={{0,8},{1,9},{2,10},{3,11},{4,12},{5,13},{6,14},{7,15},{8,0},{9,1},... | collective-permute-start | bytes 3538952 | tf_op jit(solution)/shard_map/ppermute | solution.py:1153
  360.2 19.0 %collective-permute-start.60 = (bf16[256,768]{1,0:T(8,128)(2,1)S(1)}, bf16[256,768]{1,0:T(8,128)(2,1)S(1)}, u32[]{:S(2)}, u32[]{:S(2)}) collective-permute-start(bf16[256,768]{1,0:T(8,128)(2,1)S(1)} %copy-done.78), channel_id=1, source_target_pairs={{2,0},{3,1},{6,4},{7,5},{8,10},{9,11},{12,14},{13,15},{18,16},{19,... | collective-permute-start | bytes 1179656 | tf_op jit(solution)/shard_map/ppermute | solution.py:1183
  361.5 21.9 %collective-permute-start.61 = (bf16[256,768]{1,0:T(8,128)(2,1)S(1)}, bf16[256,768]{1,0:T(8,128)(2,1)S(1)}, u32[]{:S(2)}, u32[]{:S(2)}) collective-permute-start(bf16[256,768]{1,0:T(8,128)(2,1)S(1)} %copy-done.77), channel_id=1, source_target_pairs={{2,0},{3,1},{6,4},{7,5},{8,10},{9,11},{12,14},{13,15},{18,16},{19,... | collective-permute-start | bytes 1179656 | tf_op jit(solution)/shard_map/ppermute | solution.py:1183
  383.4 19.6 %collective-permute-start.67 = (bf16[416,768]{1,0:T(8,128)(2,1)}, bf16[416,768]{1,0:T(8,128)(2,1)}, u32[]{:S(2)}, u32[]{:S(2)}) collective-permute-start(bf16[416,768]{1,0:T(8,128)(2,1)} %get-tuple-element.967), channel_id=1, source_target_pairs={{0,3},{1,0},{2,1},{3,2},{4,7},{5,4},{6,5},{7,6},{8,11},{9,8},{10,9... | collective-permute-start | bytes 1916936 | tf_op jit(solution)/shard_map/ppermute | solution.py:1202
  386.6 16.4 %collective-permute-start.66 = (bf16[4,2,48,768]{3,2,1,0:T(8,128)(2,1)}, bf16[4,2,48,768]{3,2,1,0:T(8,128)(2,1)}, u32[]{:S(2)}, u32[]{:S(2)}) collective-permute-start(bf16[4,2,48,768]{3,2,1,0:T(8,128)(2,1)} %get-tuple-element.1180), channel_id=1, source_target_pairs={{0,16},{1,17},{2,18},{3,19},{4,20},{5,21},{6,22},{7,23},{8,24},{9,... | collective-permute-start | bytes 1769480 | tf_op jit(solution)/shard_map/ppermute | solution.py:1157
  418.9 20.2 %collective-permute-start.75 = (bf16[4,32,768]{2,1,0:T(8,128)(2,1)}, bf16[4,32,768]{2,1,0:T(8,128)(2,1)S(1)}, u32[]{:S(2)}, u32[]{:S(2)}) collective-permute-start(bf16[4,32,768]{2,1,0:T(8,128)(2,1)} %get-tuple-element.1261), channel_id=1, source_target_pairs={{0,1},{1,2},{2,3},{3,0},{4,5},{5,6},{6,7},{7,4},{8,9},{9,10},{10,1... | collective-permute-start | bytes 589832 | tf_op jit(solution)/shard_map/ppermute | solution.py:1202
  418.9 20.2 %collective-permute-start.73 = (bf16[4,32,768]{2,1,0:T(8,128)(2,1)}, bf16[4,32,768]{2,1,0:T(8,128)(2,1)S(1)}, u32[]{:S(2)}, u32[]{:S(2)}) collective-permute-start(bf16[4,32,768]{2,1,0:T(8,128)(2,1)} %get-tuple-element.1262), channel_id=1, source_target_pairs={{0,3},{1,0},{2,1},{3,2},{4,7},{5,4},{6,5},{7,6},{8,11},{9,8},{10,9... | collective-permute-start | bytes 589832 | tf_op jit(solution)/shard_map/ppermute | solution.py:1202
  422.7 16.4 %collective-permute-start.74 = (bf16[4,32,768]{2,1,0:T(8,128)(2,1)}, bf16[4,32,768]{2,1,0:T(8,128)(2,1)}, u32[]{:S(2)}, u32[]{:S(2)}) collective-permute-start(bf16[4,32,768]{2,1,0:T(8,128)(2,1)} %get-tuple-element.1263), channel_id=1, source_target_pairs={{0,2},{1,3},{2,0},{3,1},{4,6},{5,7},{6,4},{7,5},{8,10},{9,11},{10,... | collective-permute-start | bytes 589832 | tf_op jit(solution)/shard_map/ppermute | solution.py:1202
  443.6 18.3 %collective-permute-start.78 = (bf16[4,24,768]{2,1,0:T(8,128)(2,1)S(1)}, bf16[4,24,768]{2,1,0:T(8,128)(2,1)}, u32[]{:S(2)}, u32[]{:S(2)}) collective-permute-start(bf16[4,24,768]{2,1,0:T(8,128)(2,1)S(1)} %pad_maximum_fusion.24), channel_id=1, source_target_pairs={{0,3},{1,0},{2,1},{3,2},{4,7},{5,4},{6,5},{7,6},{8,11},{9,8},{10,9... | collective-permute-start | bytes 442376 | tf_op jit(solution)/shard_map/ppermute | solution.py:1202
  444.5 17.3 %collective-permute-start.77 = (bf16[4,24,768]{2,1,0:T(8,128)(2,1)S(1)}, bf16[4,24,768]{2,1,0:T(8,128)(2,1)}, u32[]{:S(2)}, u32[]{:S(2)}) collective-permute-start(bf16[4,24,768]{2,1,0:T(8,128)(2,1)S(1)} %pad_maximum_fusion.24), channel_id=1, source_target_pairs={{0,2},{1,3},{2,0},{3,1},{4,6},{5,7},{6,4},{7,5},{8,10},{9,11},{10,... | collective-permute-start | bytes 442376 | tf_op jit(solution)/shard_map/ppermute | solution.py:1202
  461.8 22.5 %collective-permute-start.80 = (bf16[6,256,256]{2,1,0:T(8,128)(2,1)}, bf16[6,256,256]{2,1,0:T(8,128)(2,1)S(1)}, u32[]{:S(2)}, u32[]{:S(2)}) collective-permute-start(bf16[6,256,256]{2,1,0:T(8,128)(2,1)} %wide_last.1.refs_0_), channel_id=1, source_target_pairs={{0,3},{1,0},{4,7},{5,4},{10,9},{11,10},{14,13},{15,14},{16,19},{17... | collective-permute-start | bytes 2359304 | tf_op jit(solution)/shard_map/ppermute | solution.py:1188
  465.6 19.4 %collective-permute-start.79 = (bf16[6,256,256]{2,1,0:T(8,128)(2,1)}, bf16[6,256,256]{2,1,0:T(8,128)(2,1)S(1)}, u32[]{:S(2)}, u32[]{:S(2)}) collective-permute-start(bf16[6,256,256]{2,1,0:T(8,128)(2,1)} %wide_last.1.refs_0_), channel_id=1, source_target_pairs={{0,1},{1,2},{4,5},{5,6},{10,11},{11,8},{14,15},{15,12},{16,17},{17... | collective-permute-start | bytes 2359304 | tf_op jit(solution)/shard_map/ppermute | solution.py:1188
  496.5 35.2 %collective-permute-start.86 = (bf16[2,2,96,768]{3,2,1,0:T(8,128)(2,1)}, bf16[2,2,96,768]{3,2,1,0:T(8,128)(2,1)}, u32[]{:S(2)}, u32[]{:S(2)}) collective-permute-start(bf16[2,2,96,768]{3,2,1,0:T(8,128)(2,1)} %get-tuple-element.1082), channel_id=1, source_target_pairs={{0,4},{1,5},{2,6},{3,7},{4,0},{5,1},{6,2},{7,3},{8,12},{9,13},{10,... | collective-permute-start | bytes 1769480 | tf_op jit(solution)/shard_map/ppermute | solution.py:1157
  497.4 34.2 %collective-permute-start.87 = (bf16[2,2,96,768]{3,2,1,0:T(8,128)(2,1)}, bf16[2,2,96,768]{3,2,1,0:T(8,128)(2,1)}, u32[]{:S(2)}, u32[]{:S(2)}) collective-permute-start(bf16[2,2,96,768]{3,2,1,0:T(8,128)(2,1)} %get-tuple-element.1083), channel_id=1, source_target_pairs={{0,16},{1,17},{2,18},{3,19},{4,20},{5,21},{6,22},{7,23},{8,24},{9,... | collective-permute-start | bytes 1769480 | tf_op jit(solution)/shard_map/ppermute | solution.py:1157
  498.4 33.2 %collective-permute-start.88 = (bf16[2,2,96,768]{3,2,1,0:T(8,128)(2,1)}, bf16[2,2,96,768]{3,2,1,0:T(8,128)(2,1)}, u32[]{:S(2)}, u32[]{:S(2)}) collective-permute-start(bf16[2,2,96,768]{3,2,1,0:T(8,128)(2,1)} %get-tuple-element.1084), channel_id=1, source_target_pairs={{0,20},{1,21},{2,22},{3,23},{4,16},{5,17},{6,18},{7,19},{8,28},{9,... | collective-permute-start | bytes 1769480 | tf_op jit(solution)/shard_map/ppermute | solution.py:1157
  501.2 35.3 %collective-permute-start.89 = (bf16[416,768]{1,0:T(8,128)(2,1)S(1)}, bf16[416,768]{1,0:T(8,128)(2,1)S(1)}, u32[]{:S(2)}, u32[]{:S(2)}) collective-permute-start(bf16[416,768]{1,0:T(8,128)(2,1)S(1)} %add_convert_fusion.2), channel_id=1, source_target_pairs={{0,3},{1,0},{2,1},{3,2},{4,7},{5,4},{6,5},{7,6},{8,11},{9,8},{10,9... | collective-permute-start | bytes 1916936 | tf_op jit(solution)/shard_map/ppermute | solution.py:1202
  513.6 22.9 %collective-permute-start.90 = (bf16[416,768]{1,0:T(8,128)(2,1)S(1)}, bf16[416,768]{1,0:T(8,128)(2,1)S(1)}, u32[]{:S(2)}, u32[]{:S(2)}) collective-permute-start(bf16[416,768]{1,0:T(8,128)(2,1)S(1)} %copy-done.23), channel_id=1, source_target_pairs={{0,1},{1,2},{2,3},{3,0},{4,5},{5,6},{6,7},{7,4},{8,9},{9,10},{10,1... | collective-permute-start | bytes 1916936 | tf_op jit(solution)/shard_map/ppermute | solution.py:1167
  (127 other events, 1172.6 us)
